TPU v7x, 32 devices: a whole 2x2x4 slice. The times are simulated.
32 devices in a mesh: dp: 4 (over x, core), seq: 8 (over z, y).
Axes of the slice: x: 2, y: 2, z: 4, core: 2. Of those that a mesh axis runs over, the one named last changes fastest.
Arguments:
- tokens: bfloat16 [4, 6144, 2560], P('dp', 'seq'), may hold values from -6 to 6
- w_xbc: bfloat16 [2560, 2816], P(('dp', 'seq')), may hold values from -0.125 to 0.125
- conv_weight: float32 [4, 2816], replicated, may hold values from -3 to 3
- conv_bias: float32 [2816], replicated, may hold values from -2 to 2
- a_log: float32 [40], replicated, may hold values from -13 to -3
- dt_in: float32 [4, 40, 6144], P('dp', None, 'seq'), may hold values from -2 to 49152
- d_skip: float32 [40], replicated, may hold values from 0.5 to 1.5
- norm_gain: float32 [2560], replicated, may hold values from 0.25 to 1.75
Outputs:
- normed: bfloat16 [4, 6144, 2560], P('dp', 'seq')
All inputs are finite; a program needn't handle non-finite values.
Results may differ from a plain program's by a relative error of at most 0.012.
Values may be sent and summed in bfloat16 or wider, within the bound.
No kernel may reach another device: no remote copies, remote signals or barrier semaphores. Data moves between devices by JAX's collectives and lax.ppermute only.
A program may use at most 128 MiB of HBM per device.

v0:
```python
import jax
import jax.numpy as jnp
from jax import lax
from jax.sharding import PartitionSpec as P

GROUP = 256


def passed_along(value, axis, by):
    length = lax.axis_size(axis)
    pairs = [(i, i + by) for i in range(length) if 0 <= i + by < length]
    return lax.ppermute(value, axis, pairs)


def prefix(value, axis, join, neutral):
    count, mine = (lax.axis_size(axis), lax.axis_index(axis))
    pieces = jax.tree.map(lambda part: lax.all_gather(part, axis), value)
    running = jax.tree.map(
        lambda part, zero: jnp.full_like(part, 0) + jnp.asarray(zero, part.dtype), value, neutral
    )

    def hop(position, running):
        longer = join(running, jax.tree.map(lambda part: part[position], pieces))
        return jax.tree.map(lambda new, old: jnp.where(position < mine, new, old), longer, running)

    return lax.fori_loop(0, count - 1, hop, running)


def block_state(x_block, b_block, dt_block, decay_block):
    heads = dt_block.shape[0]
    length = dt_block.shape[1]
    x_heads = x_block.astype(jnp.float32).reshape(length, heads, -1)
    cumul = jnp.cumsum(decay_block, axis=1)
    tail_weight = jnp.exp(cumul[:, -1:] - cumul) * dt_block
    weighted = tail_weight.T[:, :, None] * x_heads
    span_state = jnp.einsum(
        "jhp,jn->hpn", weighted, b_block.astype(jnp.float32), precision=lax.Precision.HIGH
    )
    return (span_state, cumul[:, -1])


def block_inner(x_block, b_block, c_block, dt_block, decay_block):
    heads = dt_block.shape[0]
    length = dt_block.shape[1]
    x_heads = x_block.astype(jnp.float32).reshape(length, heads, -1)
    cumul = jnp.cumsum(decay_block, axis=1)
    spread = cumul[:, :, None] - cumul[:, None, :]
    lower = jnp.arange(length)[:, None] >= jnp.arange(length)[None, :]
    decay_mat = jnp.exp(jnp.where(lower[None], spread, -jnp.inf))
    scores = jnp.dot(c_block, b_block.T, preferred_element_type=jnp.float32)
    mixing = decay_mat * scores[None] * dt_block[:, None, :]
    y_inner = jnp.einsum("hij,jhp->ihp", mixing, x_heads, precision=lax.Precision.HIGH)
    return (y_inner, cumul, x_heads)


def combine_carry(earlier, later):
    return (earlier[0] + later[0], jnp.exp(later[0])[:, None, None] * earlier[1] + later[1])


def local(tokens, w_xbc, conv_weight, conv_bias, a_log, dt_in, d_skip, norm_gain):
    token_rows = tokens[0]
    tok_count = token_rows.shape[0]
    heads = a_log.shape[0]
    width_x = norm_gain.shape[0]
    head_size = width_x // heads
    channels = w_xbc.shape[1]
    state_size = (channels - width_x) // 2
    kernel = conv_weight.shape[0]
    projected = jnp.dot(
        token_rows,
        lax.all_gather(w_xbc, ("dp", "seq"), axis=0, tiled=True),
        preferred_element_type=jnp.float32,
    )
    xbc = projected.astype(jnp.bfloat16)
    rim_rows = passed_along(xbc[tok_count - (kernel - 1) :], "seq", 1)
    padded = jnp.concatenate([rim_rows, xbc], axis=0)
    accum = conv_bias[None, :] + jnp.zeros((tok_count, channels), jnp.float32)
    for tap_index in range(kernel):
        accum = accum + conv_weight[tap_index][None, :] * padded[
            tap_index : tap_index + tok_count
        ].astype(jnp.float32)
    conv_out = jax.nn.silu(accum).astype(jnp.bfloat16)
    step_size = jax.nn.softplus(dt_in[0])
    log_decay = -jnp.exp(a_log)[:, None] * step_size
    blocks = tok_count // GROUP
    gain_heads = norm_gain.reshape(heads, head_size)[None]
    pieces = []
    own_state = jnp.zeros((heads, head_size, state_size), jnp.float32)
    own_decay = jnp.zeros((heads,), jnp.float32)
    for block_index in range(blocks):
        lo_row = block_index * GROUP
        block_rows = conv_out[lo_row : lo_row + GROUP]
        x_block = block_rows[:, :width_x]
        b_block = block_rows[:, width_x : width_x + state_size]
        c_block = block_rows[:, width_x + state_size :]
        dt_block = step_size[:, lo_row : lo_row + GROUP]
        decay_block = log_decay[:, lo_row : lo_row + GROUP]
        span_state, totals = block_state(x_block, b_block, dt_block, decay_block)
        own_state = jnp.exp(totals)[:, None, None] * own_state + span_state
        own_decay = own_decay + totals
        pieces.append((x_block, b_block, c_block, dt_block, decay_block, span_state, totals))
    identity = (jnp.zeros_like(own_decay), jnp.zeros_like(own_state))
    earlier_decay, incoming = prefix((own_decay, own_state), "seq", combine_carry, identity)
    state = incoming
    outputs = []
    for block_index in range(blocks):
        x_block, b_block, c_block, dt_block, decay_block, span_state, totals = pieces[block_index]
        y_inner, cumul, x_heads = block_inner(x_block, b_block, c_block, dt_block, decay_block)
        from_state = jnp.einsum(
            "in,hpn->ihp", c_block.astype(jnp.float32), state, precision=lax.Precision.HIGH
        )
        ssd = y_inner + jnp.exp(cumul).T[:, :, None] * from_state + d_skip[None, :, None] * x_heads
        mean_sq = jnp.mean(ssd * ssd, axis=-1, keepdims=True)
        scaled = ssd * lax.rsqrt(mean_sq + 1e-05) * gain_heads
        outputs.append(scaled.reshape(GROUP, width_x).astype(jnp.bfloat16))
        state = jnp.exp(totals)[:, None, None] * state + span_state
    return jnp.concatenate(outputs, axis=0)[None]


def solution(mesh):
    return jax.shard_map(
        local,
        mesh=mesh,
        in_specs=(
            P("dp", "seq", None),
            P(("dp", "seq"), None),
            P(),
            P(),
            P(),
            P("dp", None, "seq"),
            P(),
            P(),
        ),
        out_specs=P("dp", "seq", None),
        check_vma=False,
    )
```

profile of v0, /device:TPU:24, one launch (start us, length us, event | category | flops | bytes accessed | tf_op | source)
XLA Modules:
  0.0 365.2 jit_solution(17380342720437518462)
XLA Ops:
  6.5 0.7 all-gather.5.cloned.1.call-update
  8.0 1.0 compare_select_fusion
  12.4 0.8 fusion.91
  13.2 100.6 %all-gather.5.cloned.1.call-done = bf16[2560,2816]{1,0:T(8,128)(2,1)} async-done(((bf16[80,2816]{1,0:T(8,128)(2,1)}), bf16[2560,2816]{1,0:T(8,128)(2,1)}) %all-gather.5.cloned.1.call-update) | async-done | bytes 14417936 | tf_op jit(solution)/shard_map/all_gather | solution.py:71
  113.8 16.4 %convolution_convert_fusion = bf16[768,2816]{1,0:T(8,128)(2,1)S(1)} fusion(bf16[2560,2816]{1,0:T(8,128)(2,1)} %all-gather.5.cloned.1.call-done, bf16[1,768,2560]{2,1,0:T(8,128)(2,1)} %param.10), kind=kOutput, calls=%fused_computation.42 | convolution fusion | flops 11075125248 | bytes 22675456 | tf_op jit(solution)/shard_map/dot_general | solution.py:69
  130.2 3.4 collective-permute-start
  133.8 3.0 collective-permute-done
  136.8 6.3 %multiply_convert_fusion = bf16[768,2816]{1,0:T(8,128)(2,1)S(1)} fusion(bf16[768,2816]{1,0:T(8,128)(2,1)S(1)} %convolution_convert_fusion, bf16[3,2816]{1,0:T(4,128)(2,1)S(1)} %collective-permute-done, f32[2816]{0:T(1024)S(1)} %get-tuple-element.120, f32[2816]{0:T(1024)S(1)} %get-tuple-element.121, f32[2816]{0:T(1024)S(1)} %get-tuple-element.119, ...), kind=kLoop, calls=%fused_computation.21 | loop fusion | flops 56229888 | bytes 8723968 | tf_op jit(solution)/shard_map/convert_element_type | solution.py:82
  143.2 2.1 fusion.90
  145.2 0.9 copy-done
  146.2 1.6 copy.33
  147.8 2.9 copy.40
  150.7 1.4 copy.41
  152.1 1.8 fusion.40
  154.0 1.7 fusion.42
  155.7 1.1 copy-done.1
  156.8 2.8 fusion.52
  161.2 17.4 %all-reduce = f32[320]{0:T(512)S(1)} all-reduce(f32[320]{0:T(512)S(1)} %dynamic-update-slice), channel_id=2, replica_groups=mesh['dp'=4,'seq'=8] {'seq'}, use_global_device_ids=true, to_apply=%add | all-reduce | flops 320 | bytes 2560
  180.1 1.1 fusion.73
  181.1 1.1 fusion.76
  182.2 1.1 fusion.83
  183.2 125.4 %all-gather.7.cloned.1.call-done = f32[320,64,128]{2,1,0:T(8,128)} async-done(((f32[40,64,128]{2,1,0:T(8,128)}), f32[320,64,128]{2,1,0:T(8,128)}) %all-gather.7.cloned.1.call-update) | async-done | bytes 10485776 | tf_op jit(solution)/shard_map/all_gather | solution.py:17
  308.6 16.4 %while.14 = (s32[]{:T(128)}, f32[40,64,128]{2,1,0:T(8,128)S(1)}, s32[]{:T(128)}, f32[8,40]{1,0:T(8,128)}, f32[8,40,64,128]{3,2,1,0:T(8,128)}, /*index=5*/s32[]{:T(128)}, s32[]{:T(128)}) while((s32[]{:T(128)}, f32[40,64,128]{2,1,0:T(8,128)S(1)}, s32[]{:T(128)}, f32[8,40]{1,0:T(8,128)}, f32[8,40,64,128]{3,2,1,0:T(8,128)}, ...), condition=%wide.region_7.8_spmd.clone, body=%wide.region_6.7_spmd.clone.sunk | while | flops 1310724 | bytes 3932745 | solution.py:26
  308.6 0.7 exponential_bitcast_fusion.5
  309.3 1.6 fusion.99
  310.9 0.7 exponential_bitcast_fusion.5
  311.6 1.6 fusion.99
  313.3 0.7 exponential_bitcast_fusion.5
  314.0 1.6 fusion.99
  315.6 0.7 exponential_bitcast_fusion.5
  316.3 1.6 fusion.99
  317.9 0.7 exponential_bitcast_fusion.5
  318.6 1.6 fusion.99
  320.2 0.7 exponential_bitcast_fusion.5
  320.9 1.6 fusion.99
  322.6 0.7 exponential_bitcast_fusion.5
  323.2 1.6 fusion.99
  325.1 2.2 fusion.53
  327.3 1.7 fusion.60
  329.1 1.8 fusion.70
  330.9 5.3 %multiply_reduce_fusion = (f32[256,40]{0,1:T(8,128)S(1)}, f32[256,40,64]{0,2,1:T(8,128)S(1)}) fusion(bf16[256,40,64]{0,2,1:T(8,128)(2,1)S(1)} %bitcast.139, f32[40]{0:T(128)S(1)} %copy-done.21, f32[256,40,64]{0,2,1:T(8,128)S(1)} %fusion.53, f32[256,40]{0,1:T(8,128)S(1)} %copy-done.16, f32[40,256]{1,0:T(8,128)S(1)} %copy-done.15, ...), kind=kOutput, calls=%fused_computation.64 | convolution fusion | flops 1021696000 | bytes 7045280 | tf_op jit(solution)/shard_map/hij,jhp->ihp/dot_general | solution.py:52
  336.3 5.5 %multiply_reduce_fusion.1 = (f32[256,40]{0,1:T(8,128)S(1)}, f32[256,40,64]{0,2,1:T(8,128)S(1)}) fusion(bf16[256,40,64]{0,2,1:T(8,128)(2,1)S(1)} %bitcast.137, f32[40]{0:T(128)S(1)} %copy-done.21, f32[256,40,64]{0,2,1:T(8,128)S(1)} %fusion.60, f32[256,40]{0,1:T(8,128)S(1)} %copy-done.14, f32[40,256]{1,0:T(8,128)S(1)} %copy-done.13, ...), kind=kOutput, calls=%fused_computation.66 | convolution fusion | flops 1021696000 | bytes 7045280 | tf_op jit(solution)/shard_map/hij,jhp->ihp/dot_general | solution.py:52
  341.9 5.2 %multiply_reduce_fusion.2 = (f32[256,40]{0,1:T(8,128)S(1)}, f32[256,40,64]{0,2,1:T(8,128)S(1)}) fusion(bf16[256,40,64]{0,2,1:T(8,128)(2,1)S(1)} %bitcast.135, f32[40]{0:T(128)S(1)} %copy-done.21, f32[256,40,64]{0,2,1:T(8,128)S(1)} %fusion.70, f32[256,40]{0,1:T(8,128)S(1)} %copy-done.12, f32[40,256]{1,0:T(8,128)S(1)} %copy-done.11, ...), kind=kOutput, calls=%fused_computation.68 | convolution fusion | flops 1021696000 | bytes 7045280 | tf_op jit(solution)/shard_map/hij,jhp->ihp/dot_general | solution.py:52
  347.1 2.2 multiply_convert_fusion.3
  349.4 2.4 copy.42
  351.8 1.6 copy.43
  353.4 1.6 copy.44
  355.0 3.3 maximum_bitcast_fusion
  (82 shorter events, 6.7 us)
Async XLA Ops:
  6.5 107.3 %all-gather.5.cloned.1.call-start = ((), (), s32[]{:S(2)}) async-start(), calls=%async_computation | async-start | bytes 14868480 | tf_op jit(solution)/shard_map/all_gather | solution.py:71
  7.3 301.4 %all-gather.7.cloned.1.call-start = ((), (), s32[]{:S(2)}) async-start(), calls=%async_computation.1 | async-start | bytes 11796480 | tf_op jit(solution)/shard_map/all_gather | solution.py:17
  13.2 120.5 %copy-start.10 = (f32[4,2816]{1,0:T(4,128)S(1)}, f32[4,2816]{1,0:T(4,128)}, u32[]{:S(2)}) copy-start(f32[4,2816]{1,0:T(4,128)} %param.12) | copy-start | bytes 135172
  13.2 123.7 %copy-start.17 = (f32[2816]{0:T(1024)S(1)}, f32[2816]{0:T(1024)}, u32[]{:S(2)}) copy-start(f32[2816]{0:T(1024)} %param.13) | copy-start | bytes 33796
  130.2 6.6 %collective-permute-start = (bf16[3,2816]{1,0:T(4,128)(2,1)S(1)}, bf16[3,2816]{1,0:T(4,128)(2,1)S(1)}, u32[]{:S(2)}, u32[]{:S(2)}) collective-permute-start(bf16[3,2816]{1,0:T(4,128)(2,1)S(1)} %slice.143), channel_id=1, source_target_pairs={{0,1},{1,2},{2,3},{3,4},{4,5},{5,6},{6,7},{8,9},{9,10},{10,11},{11... | collective-permute-start | bytes 50696 | tf_op jit(solution)/shard_map/ppermute | solution.py:12
  133.8 21.9 %copy-start.20 = (f32[40]{0:T(128)}, f32[40]{0:T(128)S(1)}, u32[]{:S(2)}) copy-start(f32[40]{0:T(128)S(1)} %exp.81) | copy-start | bytes 484
  143.1 3.0 copy-start
  147.7 4.4 %copy-start.2 = (bf16[256,2560]{0,1:T(8,128)(2,1)}, bf16[256,2560]{0,1:T(8,128)(2,1)S(1)}, u32[]{:S(2)}) copy-start(bf16[256,2560]{0,1:T(8,128)(2,1)S(1)} %copy.33) | copy-start | bytes 3932164
  152.1 1.9 copy-start.4
  152.1 4.6 %copy-start.6 = (bf16[256,2560]{0,1:T(8,128)(2,1)S(1)}, bf16[256,2560]{0,1:T(8,128)(2,1)}, u32[]{:S(2)}) copy-start(bf16[256,2560]{0,1:T(8,128)(2,1)} %copy.41) | copy-start | bytes 3932164
  155.7 1.1 copy-start.1
  156.8 2.9 copy-start.22
  156.8 22.6 %copy-start.18 = (f32[2560]{0:T(1024)S(1)}, f32[2560]{0:T(1024)}, u32[]{:S(2)}) copy-start(f32[2560]{0:T(1024)} %param.17) | copy-start | bytes 30724
  325.0 2.2 copy-start.19
  329.0 1.8 copy-start.7
  329.0 1.8 copy-start.9
  329.0 1.8 copy-start.15
  329.0 1.8 copy-start.16
  329.1 1.8 copy-start.21
  330.9 5.3 %copy-start.5 = (bf16[256,2560]{0,1:T(8,128)(2,1)S(1)}, bf16[256,2560]{0,1:T(8,128)(2,1)}, u32[]{:S(2)}) copy-start(bf16[256,2560]{0,1:T(8,128)(2,1)} %copy.40) | copy-start | bytes 3932164
  330.9 5.3 %copy-start.13 = (f32[40,256]{1,0:T(8,128)S(1)}, f32[40,256]{1,0:T(8,128)}, u32[]{:S(2)}) copy-start(f32[40,256]{1,0:T(8,128)} %get-tuple-element.143) | copy-start | bytes 122884
  330.9 5.3 %copy-start.14 = (f32[256,40]{0,1:T(8,128)S(1)}, f32[256,40]{0,1:T(8,128)}, u32[]{:S(2)}) copy-start(f32[256,40]{0,1:T(8,128)} %get-tuple-element.152) | copy-start | bytes 122884
  336.3 5.6 %copy-start.3 = (bf16[256,2560]{0,1:T(8,128)(2,1)S(1)}, bf16[256,2560]{0,1:T(8,128)(2,1)}, u32[]{:S(2)}) copy-start(bf16[256,2560]{0,1:T(8,128)(2,1)} %copy-done.2) | copy-start | bytes 3932164
  336.3 5.6 %copy-start.11 = (f32[40,256]{1,0:T(8,128)S(1)}, f32[40,256]{1,0:T(8,128)}, u32[]{:S(2)}) copy-start(f32[40,256]{1,0:T(8,128)} %get-tuple-element.139) | copy-start | bytes 122884
  336.3 5.6 %copy-start.12 = (f32[256,40]{0,1:T(8,128)S(1)}, f32[256,40]{0,1:T(8,128)}, u32[]{:S(2)}) copy-start(f32[256,40]{0,1:T(8,128)} %get-tuple-element.150) | copy-start | bytes 122884
  353.4 1.6 copy-start.8
Sparse Core Ops, SparseCore 0:
  10.3 103.4 all-gather.4
  159.7 148.8 all-gather.6
where the time goes:
time: 370 us; the launch traced here: 365 us
  waiting for transfers between devices  230 us (62%)
  matrix products  47.7 us (13%)
  other arithmetic  29.2 us (8%)
  local copies, waits for them, and re-layouts  22.8 us (6%)
  blocking collectives  17.4 us (5%)
  between operations  14.6 us (4%)
    all_gather x1, waiting for transfers between devices, prefix(): pieces = jax.tree.map(lambda part: lax.all_gather(part, axis), value)  125 us
    all_gather x1, waiting for transfers between devices, local(): lax.all_gather(w_xbc, ('dp', 'seq'), axis=0, tiled=True)  101 us
    unnamed x1, blocking collectives  17.4 us
    dot_general x1, matrix products, local(): jnp.dot(token_rows, lax.all_gather(w_xbc, ('dp', 'seq'), axis=0, tiled=Tr...  16.4 us
    dot_general x3, matrix products, block_inner(): jnp.einsum('hij,jhp->ihp', mixing, x_heads, precision=lax.Precision.HIGH)  16 us
    select_n x7, other arithmetic, hop(): jnp.where(position < mine, new, old)  11.3 us
    slice x4, local copies, waits for them, and re-layouts, local(): x_block = block_rows[:, :width_x]  8 us
  transfers between devices with their start and end apart: 3, of which 3 were waited for; matrix products, arithmetic and copies ran while one was open for 3% of the time, Pallas kernels for 0%

commit v1 on v0

v1 whole, which is shorter than its diff:
```python
import jax
import jax.numpy as jnp
from jax import lax
from jax.experimental import pallas as pl
from jax.experimental.pallas import tpu as pltpu
from jax.sharding import PartitionSpec as P

SPAN = 128
TILE = 256
RIM = 16
VMEM = 56 * 1024 * 1024


def halves(left, right):
    lane = lax.broadcasted_iota(jnp.int32, left.shape, 1)
    return jnp.where(lane < left.shape[1] // 2, left, right)


def spread(columns, index):
    return jnp.broadcast_to(columns[:, index : index + 1], (columns.shape[0], SPAN))


def convolve(rows_ref, taps_ref, base, left):
    cols = pl.ds(left, SPAN)
    accum = jnp.broadcast_to(taps_ref[4:5, cols], (SPAN, SPAN))
    for tap in range(4):
        accum = accum + taps_ref[tap : tap + 1, cols] * rows_ref[pl.ds(base + RIM - 3 + tap, SPAN), cols]
    return 0.5 * accum * (1.0 + jnp.tanh(0.5 * accum))


def project(tok_ref, w_ref, rows_ref):
    out = jnp.dot(tok_ref[...], w_ref[...], preferred_element_type=jnp.float32)
    rows_ref[...] = out.astype(jnp.bfloat16).astype(jnp.float32)


def bc_kernel(tok_ref, w_ref, taps_ref, c_ref, bt_ref, scores_ref, rows_ref):
    project(tok_ref, w_ref, rows_ref)
    row = lax.broadcasted_iota(jnp.int32, (SPAN, SPAN), 0)
    col = lax.broadcasted_iota(jnp.int32, (SPAN, SPAN), 1)
    for block in range(scores_ref.shape[0]):
        at = block * SPAN
        b_t = convolve(rows_ref, taps_ref, at, 0).T.astype(jnp.bfloat16)
        c_rows = convolve(rows_ref, taps_ref, at, SPAN).astype(jnp.bfloat16)
        bt_ref[:, pl.ds(at, SPAN)] = b_t
        c_ref[pl.ds(at, SPAN), :] = c_rows
        scores = jnp.dot(c_rows, b_t, preferred_element_type=jnp.float32)
        scores_ref[block] = jnp.where(row >= col, scores, 0.0)


def ssd_kernel(tok_ref, w_ref, taps_ref, c_ref, bt_ref, scores_ref, cols_ref, rowsv_ref, lanes_ref, y_ref, state_ref, rows_ref):
    project(tok_ref, w_ref, rows_ref)
    blocks = scores_ref.shape[0]
    for pair in range(TILE // SPAN):
        left = pair * SPAN
        state = None
        for block in range(blocks):
            at = block * SPAN
            here = pl.ds(at, SPAN)
            cols = cols_ref[0, here, :]
            first, second = spread(cols, 2 * pair), spread(cols, 2 * pair + 1)
            dts = halves(spread(cols, 4 + 2 * pair), spread(cols, 5 + 2 * pair))
            x = convolve(rows_ref, taps_ref, at, left).astype(jnp.bfloat16).astype(jnp.float32)
            xdt = x * dts
            scores = scores_ref[block]
            mix = []
            for head, cum in enumerate((first, second)):
                across = rowsv_ref[0, 2 * pair + head : 2 * pair + head + 1, here]
                mix.append((jnp.exp(jnp.minimum(cum - across, 0.0)) * scores).astype(jnp.bfloat16))
            zero = jnp.zeros_like(xdt)
            stacked = jnp.concatenate([halves(xdt, zero), halves(zero, xdt)], axis=0).astype(jnp.bfloat16)
            y = jnp.dot(jnp.concatenate(mix, axis=1), stacked, preferred_element_type=jnp.float32)
            cum = halves(first, second)
            total = lanes_ref[0, block : block + 1, pl.ds(left, SPAN)]
            if state is not None:
                carried = jnp.dot(c_ref[here, :], state.astype(jnp.bfloat16), preferred_element_type=jnp.float32)
                y = y + jnp.exp(cum) * carried
            y_ref[here, pl.ds(left, SPAN)] = y + lanes_ref[0, blocks : blocks + 1, pl.ds(left, SPAN)] * x
            tail = (jnp.exp(jnp.minimum(total - cum, 0.0)) * xdt).astype(jnp.bfloat16)
            span_state = jnp.dot(bt_ref[:, here], tail, preferred_element_type=jnp.float32)
            state = span_state if state is None else jnp.exp(total) * state + span_state
        state_ref[:, pl.ds(left, SPAN)] = state


def norm_kernel(count, *refs):
    y_ref, c_ref, cols_ref, lanes_ref, gather_ref = refs[:5]
    parts = refs[5 : 5 + count]
    out_ref = refs[-1]
    blocks = c_ref.shape[0] // SPAN
    for pair in range(TILE // SPAN):
        left = pl.ds(pair * SPAN, SPAN)
        state = sum(
            lanes_ref[0, k + 1 : k + 2, left] * part[:, left].astype(jnp.float32) for k, part in enumerate(parts)
        ).astype(jnp.bfloat16)
        gain = lanes_ref[0, 0:1, left]
        for block in range(blocks):
            here = pl.ds(block * SPAN, SPAN)
            cols = cols_ref[0, here, :]
            cum = halves(spread(cols, 8 + 2 * pair), spread(cols, 9 + 2 * pair))
            carried = jnp.dot(c_ref[here, :], state, preferred_element_type=jnp.float32)
            ssd = y_ref[here, left] + jnp.exp(cum) * carried
            square = ssd * ssd
            high = square.astype(jnp.bfloat16)
            low = (square - high.astype(jnp.float32)).astype(jnp.bfloat16)
            mean = jnp.dot(high, gather_ref[...], preferred_element_type=jnp.float32)
            mean = mean + jnp.dot(low, gather_ref[...], preferred_element_type=jnp.float32)
            out_ref[here, left] = (ssd * lax.rsqrt(mean + 1e-05) * gain).astype(jnp.bfloat16)


def whole(shape):
    return pl.BlockSpec(shape, lambda *_: (0,) * len(shape))


def params():
    return pltpu.CompilerParams(vmem_limit_bytes=VMEM)


def run_bc(tok_ext, w, taps, tok_count, at):
    rows, depth = tok_ext.shape
    blocks = tok_count // SPAN
    return pl.pallas_call(
        bc_kernel,
        grid=(1,),
        in_specs=[
            whole(tok_ext.shape),
            pl.BlockSpec((depth, TILE), lambda i: (0, at)),
            pl.BlockSpec((8, TILE), lambda i: (0, taps.shape[1] // TILE - 1)),
        ],
        out_specs=[whole((tok_count, SPAN)), whole((SPAN, tok_count)), whole((blocks, SPAN, SPAN))],
        out_shape=[
            jax.ShapeDtypeStruct((tok_count, SPAN), jnp.bfloat16),
            jax.ShapeDtypeStruct((SPAN, tok_count), jnp.bfloat16),
            jax.ShapeDtypeStruct((blocks, SPAN, SPAN), jnp.float32),
        ],
        scratch_shapes=[pltpu.VMEM((rows, TILE), jnp.float32)],
        compiler_params=params(),
        cost_estimate=pl.CostEstimate(flops=2 * rows * depth * TILE, bytes_accessed=2 * depth * (rows + TILE), transcendentals=0),
        name="project_bc",
    )(tok_ext, w, taps)


def run_ssd(tok_ext, w, taps, c_rows, b_t, scores, cols, rowsv, lanes, first, tiles, at):
    rows, depth = tok_ext.shape
    tok_count = c_rows.shape[0]
    blocks = scores.shape[0]
    return pl.pallas_call(
        ssd_kernel,
        grid=(tiles,),
        in_specs=[
            whole(tok_ext.shape),
            pl.BlockSpec((depth, TILE), lambda i: (0, i + at)),
            pl.BlockSpec((8, TILE), lambda i: (0, i + first)),
            whole(c_rows.shape),
            whole(b_t.shape),
            whole(scores.shape),
            pl.BlockSpec((1,) + cols.shape[1:], lambda i: (i + first, 0, 0)),
            pl.BlockSpec((1,) + rowsv.shape[1:], lambda i: (i + first, 0, 0)),
            pl.BlockSpec((1,) + lanes.shape[1:], lambda i: (i + first, 0, 0)),
        ],
        out_specs=[
            pl.BlockSpec((tok_count, TILE), lambda i: (0, i)),
            pl.BlockSpec((SPAN, TILE), lambda i: (0, i)),
        ],
        out_shape=[
            jax.ShapeDtypeStruct((tok_count, tiles * TILE), jnp.float32),
            jax.ShapeDtypeStruct((SPAN, tiles * TILE), jnp.float32),
        ],
        scratch_shapes=[pltpu.VMEM((rows, TILE), jnp.float32)],
        compiler_params=params(),
        cost_estimate=pl.CostEstimate(
            flops=6 * rows * depth * TILE * tiles, bytes_accessed=2 * depth * (rows + TILE * tiles), transcendentals=0
        ),
        name="project_ssd",
    )(tok_ext, w, taps, c_rows, b_t, scores, cols, rowsv, lanes)


def run_norm(out, y, c_rows, cols, lanes, gather, parts, first, width):
    tok_count = c_rows.shape[0]
    tiles = y.shape[1] // TILE
    count = len(parts)
    ins = [y, c_rows, cols, lanes, gather, *parts]
    specs = [
        pl.BlockSpec((tok_count, TILE), lambda i: (0, i)),
        whole(c_rows.shape),
        pl.BlockSpec((1,) + cols.shape[1:], lambda i: (i + first, 0, 0)),
        pl.BlockSpec((1,) + lanes.shape[1:], lambda i: (i + first, 0, 0)),
        whole(gather.shape),
    ] + [pl.BlockSpec((SPAN, TILE), lambda i: (0, i))] * count
    aliases = {}
    if out is not None:
        aliases = {len(ins): 0}
        ins.append(out)
        specs.append(pl.BlockSpec(memory_space=pl.ANY))
    return pl.pallas_call(
        lambda *refs: norm_kernel(count, *refs),
        grid=(tiles,),
        in_specs=specs,
        out_specs=pl.BlockSpec((tok_count, TILE), lambda i: (0, i + first)),
        out_shape=jax.ShapeDtypeStruct((tok_count, width), jnp.bfloat16),
        input_output_aliases=aliases,
        compiler_params=params(),
        cost_estimate=pl.CostEstimate(
            flops=6 * tok_count * SPAN * TILE * tiles, bytes_accessed=8 * tok_count * TILE * tiles, transcendentals=0
        ),
        name="head_norm",
    )(*ins)


def shifted(value, z_by, y_by, z_count, y_count):
    pairs = []
    for z in range(z_count - z_by):
        for y in range(y_count):
            pairs.append((z * y_count + y, (z + z_by) * y_count + (y + y_by) % y_count))
    return lax.ppermute(value, "seq", pairs)


def expand(per_head, head_size):
    return jnp.repeat(per_head, head_size, axis=-1)


def local(tokens, w_xbc, conv_weight, conv_bias, a_log, dt_in, d_skip, norm_gain):
    token_rows = tokens[0]
    tok_count = token_rows.shape[0]
    heads = a_log.shape[0]
    width_x = norm_gain.shape[0]
    head_size = width_x // heads
    channels = w_xbc.shape[1]
    blocks = tok_count // SPAN
    tiles = width_x // TILE
    per_tile = TILE // head_size
    seq_count = lax.axis_size("seq")
    z_count = 4
    y_count = seq_count // z_count
    y_mine = lax.rem(lax.axis_index("seq"), y_count)

    w_full = lax.all_gather(w_xbc, ("dp", "seq"), axis=0, tiled=True)
    rim = lax.ppermute(token_rows[tok_count - RIM :], "seq", [(i, i + 1) for i in range(seq_count - 1)])
    tok_ext = jnp.concatenate([rim, token_rows], axis=0)
    taps = jnp.concatenate([conv_weight, conv_bias[None], jnp.zeros((3, channels), jnp.float32)], axis=0)

    step_size = jax.nn.softplus(dt_in[0])
    log_decay = -jnp.exp(a_log)[:, None] * step_size
    cumul = jnp.cumsum(log_decay.reshape(heads, blocks, SPAN), axis=2)
    totals = cumul[:, :, -1]
    before = jnp.cumsum(totals, axis=1) - totals
    cum_full = (cumul + before[:, :, None]).reshape(heads, tok_count)
    own_decay = jnp.sum(totals, axis=1)
    cumul = cumul.reshape(heads, tok_count)
    by_tile = lambda rows: rows.reshape(tiles, per_tile, tok_count)
    cols = jnp.concatenate([by_tile(cumul), by_tile(step_size), by_tile(cum_full)], axis=1).transpose(0, 2, 1)
    rowsv = by_tile(cumul)
    lane_tiles = lambda rows: rows.reshape(rows.shape[0], tiles, TILE).transpose(1, 0, 2)
    lanes = lane_tiles(jnp.concatenate([expand(totals.T, head_size), expand(d_skip[None], head_size), jnp.zeros((1, width_x), jnp.float32)], axis=0))

    side = jnp.broadcast_to(jnp.pad(own_decay, (0, SPAN - heads))[None], (8, SPAN))
    y_decay = [own_decay] + [shifted(side, 0, k, z_count, y_count)[0, :heads] for k in range(1, y_count)]
    y_place = [lax.rem(y_mine - k + y_count, y_count) for k in range(y_count)]
    z_own = jnp.broadcast_to(jnp.pad(sum(y_decay), (0, SPAN - heads))[None], (8, SPAN))
    z_decay = [shifted(z_own, k, 0, z_count, y_count)[0, :heads] for k in range(1, z_count - 1)]
    zero = jnp.zeros_like(own_decay)
    group_coef, own_coef = [], []
    for k in range(y_count):
        after = sum(jnp.where(y_place[m] > y_place[k], y_decay[m], zero) for m in range(y_count))
        until = sum(jnp.where((y_place[m] > y_place[k]) & (y_place[m] < y_mine), y_decay[m], zero) for m in range(y_count))
        group_coef.append(expand(jnp.exp(after), head_size))
        own_coef.append(expand(jnp.where(y_place[k] < y_mine, jnp.exp(until), zero), head_size))
    inside = sum(jnp.where(y_place[m] < y_mine, y_decay[m], zero) for m in range(y_count))
    z_coef = []
    for k in range(1, z_count):
        z_coef.append(expand(jnp.exp(inside + sum(z_decay[: k - 1], zero)), head_size))
    coef_rows = [norm_gain] + own_coef[1:] + z_coef
    coef_rows += [jnp.zeros_like(norm_gain)] * (-len(coef_rows) % 8)
    coefs = lane_tiles(jnp.stack(coef_rows))
    head_of = jnp.arange(SPAN) // head_size
    gather = jnp.where(head_of[:, None] == head_of[None, :], 1.0 / head_size, 0.0).astype(jnp.bfloat16)

    c_rows, b_t, scores = run_bc(tok_ext, w_full, taps, tok_count, tiles)
    cuts = [0, 4, 8, tiles]
    pending = []
    for first, last in zip(cuts[:-1], cuts[1:]):
        y, own = run_ssd(tok_ext, w_full, taps, c_rows, b_t, scores, cols, rowsv, lanes, first, last - first, first)
        lane = slice(first * TILE, last * TILE)
        sent = own.astype(jnp.bfloat16)
        y_parts = [shifted(sent, 0, k, z_count, y_count) for k in range(1, y_count)]
        group = group_coef[0][lane] * own
        for k, part in enumerate(y_parts):
            group = group + group_coef[k + 1][lane] * part.astype(jnp.float32)
        group = group.astype(jnp.bfloat16)
        z_parts = [shifted(group, k, 0, z_count, y_count) for k in range(1, z_count)]
        pending.append((y, y_parts + z_parts, first))
    out = None
    for y, parts, first in pending:
        out = run_norm(out, y, c_rows, cols, coefs, gather, parts, first, width_x)
    return out[None]


def solution(mesh):
    return jax.shard_map(
        local,
        mesh=mesh,
        in_specs=(
            P("dp", "seq", None),
            P(("dp", "seq"), None),
            P(),
            P(),
            P(),
            P("dp", None, "seq"),
            P(),
            P(),
        ),
        out_specs=P("dp", "seq", None),
        check_vma=False,
    )
```

time: 370 us -> 260 us (0.70)
  waiting for transfers between devices: 230 us -> 119 us
  Pallas kernels: 0 us -> 75.4 us
  matrix products: 47.7 us -> 0 us
  starting transfers between devices: 3.42 us -> 21.3 us
  blocking collectives: 17.4 us -> 0 us
  other arithmetic: 29.2 us -> 13.9 us
  local copies, waits for them, and re-layouts: 22.8 us -> 12.3 us
    all_gather x2 -> x1, waiting for transfers between devices: 226 us -> 79.1 us  [local(): w_full = lax.all_gather(w_xbc, ('dp', 'seq'), axis=0, tiled=True)]
    pallas_call x0 -> x7, Pallas kernels: none -> 75.4 us  [the longest x3 49.2 us: run_ssd(): pl.pallas_call(ssd_kernel, grid=(tiles,), in_specs=[whole(tok_ext.shape),...]
    dot_general x13 -> x0, matrix products: 47.7 us -> none  [the longest x1 16.4 us: local(): jnp.dot(token_rows, lax.all_gather(w_xbc, ('dp', 'seq'), axis=0, tiled=Tr...]
    ppermute x1 -> x16, waiting for transfers between devices: 3.04 us -> 39.5 us  [the longest x15 39.5 us: shifted(): return lax.ppermute(value, 'seq', pairs)]
    ppermute x1 -> x16, starting transfers between devices: 3.38 us -> 21.3 us  [the longest x15 17.9 us: shifted(): return lax.ppermute(value, 'seq', pairs)]
    unnamed x1 -> x0, blocking collectives: 17.4 us -> none
    select_n x7 -> x2, other arithmetic: 11.3 us -> 0.02 us  [the longest x1 0.02 us: local(): jnp.where(y_place[m] < y_mine, y_decay[m], zero)]
    slice x7 -> x6, local copies, waits for them, and re-layouts: 8.29 us -> 1.15 us  [the longest x1 0.9 us: local(): token_rows[tok_count - RIM:]]
  transfers between devices with their start and end apart: 3 -> 17, of which waited for: 3 -> 5; matrix products, arithmetic and copies ran while one was open for 3% -> 10% of each run, Pallas kernels for 0% -> 27%
where the time goes in v1:
time: 260 us; the launch traced here: 256 us
  waiting for transfers between devices  119 us (46%)
  Pallas kernels  75.4 us (29%)
  starting transfers between devices  21.3 us (8%)
  other arithmetic  13.9 us (5%)
  between operations  13.9 us (5%)
  local copies, waits for them, and re-layouts  12.3 us (5%)
    all_gather x1, waiting for transfers between devices, local(): w_full = lax.all_gather(w_xbc, ('dp', 'seq'), axis=0, tiled=True)  79.1 us
    pallas_call x3, Pallas kernels, run_ssd(): pl.pallas_call(ssd_kernel, grid=(tiles,), in_specs=[whole(tok_ext.shape),...  49.2 us
    ppermute x15, waiting for transfers between devices, shifted(): return lax.ppermute(value, 'seq', pairs)  39.5 us
    pallas_call x3, Pallas kernels, run_norm(): pl.pallas_call(lambda *refs: norm_kernel(count, *refs), grid=(tiles,), in...  20.8 us
    ppermute x15, starting transfers between devices, shifted(): return lax.ppermute(value, 'seq', pairs)  17.9 us
    pallas_call x1, Pallas kernels, run_bc(): pl.pallas_call(bc_kernel, grid=(1,), in_specs=[whole(tok_ext.shape), pl.B...  5.29 us
  transfers between devices with their start and end apart: 17, of which 5 were waited for; matrix products, arithmetic and copies ran while one was open for 10% of the time, Pallas kernels for 27%

profile of v1, /device:TPU:24, one launch (start us, length us, event | category | flops | bytes accessed | tf_op | source)
XLA Modules:
  0.0 256.0 jit_solution(289100748078892884)
XLA Ops:
  6.5 0.7 all-gather.2.cloned.1.call-update
  7.3 0.9 slice_bitcast_fusion
  8.2 3.4 %collective-permute-start = (bf16[16,2560]{1,0:T(8,128)(2,1)S(1)}, bf16[16,2560]{1,0:T(8,128)(2,1)S(1)}, u32[]{:S(2)}, u32[]{:S(2)}) collective-permute-start(bf16[16,2560]{1,0:T(8,128)(2,1)S(1)} %slice_bitcast_fusion), channel_id=1, source_target_pairs={{0,1},{1,2},{2,3},{3,4},{4,5},{5,6},{6,7},{8,9},{9,10},{10,11},{11... | collective-permute-start | bytes 245768 | tf_op jit(solution)/shard_map/ppermute | solution.py:236
  11.6 0.9 squeeze.21
  12.5 0.7 exponential_negate_fusion
  13.3 1.8 reduce_window_sum.22
  15.4 0.9 squeeze.22
  16.3 0.7 broadcast_in_dim.92
  17.1 0.7 broadcast_in_dim.89
  18.3 0.3 copy.46
  19.3 0.7 select_convert_fusion.refs_4_
  20.0 0.7 maximum_maximum_fusion.taps_ref
  20.7 0.7 maximum_bitcast_fusion.lanes_ref
  21.4 2.6 %copy.44 = f32[10,12,768]{1,2,0:T(8,128)} copy(f32[10,12,768]{2,1,0:T(8,128)S(1)} %pad_maximum_fusion.1) | data formatting | bytes 737280 | tf_op jit(solution)/shard_map/concatenate | solution.py:249
  24.0 1.3 collective-permute-start.3
  25.3 1.3 collective-permute-start.2
  28.1 2.3 collective-permute-done.3
  30.5 4.3 %pad_maximum_fusion.tok_ref = bf16[784,2560]{1,0:T(8,128)(2,1)} fusion(bf16[768,2560]{1,0:T(8,128)(2,1)} %bitcast.19, bf16[16,2560]{1,0:T(8,128)(2,1)S(1)} %collective-permute-done), kind=kLoop, calls=%fused_computation | loop fusion | flops 8028160 | bytes 8028160 | tf_op jit(solution)/shard_map/concatenate | solution.py:237
  34.7 79.1 %all-gather.2.cloned.1.call-done.w_ref = bf16[2560,2816]{1,0:T(8,128)(2,1)} async-done(((bf16[80,2816]{1,0:T(8,128)(2,1)}), bf16[2560,2816]{1,0:T(8,128)(2,1)}) %all-gather.2.cloned.1.call-update) | async-done | bytes 14417936 | tf_op jit(solution)/shard_map/all_gather | solution.py:235
  113.9 5.3 %project_bc.1 = (bf16[768,128]{1,0:T(8,128)(2,1)}, bf16[128,768]{1,0:T(8,128)(2,1)}, f32[6,128,128]{2,1,0:T(8,128)}) custom-call(bf16[784,2560]{1,0:T(8,128)(2,1)} %pad_maximum_fusion.tok_ref, bf16[2560,2816]{1,0:T(8,128)(2,1)} %all-gather.2.cloned.1.call-done.w_ref, f32[8,2816]{1,0:T(8,128)} %maximum_maximum_fusion.taps_ref), custom_call_target="tpu_custom_call" | custom-call | flops 1027604480 | bytes 5324800 | tf_op jit(solution)/shard_map/project_bc/pallas_call | solution.py:120
  119.1 19.0 %project_ssd.5 = (f32[768,1024]{1,0:T(8,128)}, f32[128,1024]{1,0:T(8,128)}) custom-call(bf16[784,2560]{1,0:T(8,128)(2,1)} %pad_maximum_fusion.tok_ref, bf16[2560,2816]{1,0:T(8,128)(2,1)} %all-gather.2.cloned.1.call-done.w_ref, f32[8,2816]{1,0:T(8,128)} %maximum_maximum_fusion.taps_ref, bf16[768,128]{1,0:T(8,128)(2,1)} %get-tuple-element.14.c_ref.refs_1_, ...), custom_call_target="tpu_custom_call" | custom-call | flops 12331253760 | bytes 9256960 | tf_op jit(solution)/shard_map/project_ssd/pallas_call | solution.py:145
  138.2 1.1 convert_element_type.44
  139.3 18.9 %project_ssd.4 = (f32[768,1024]{1,0:T(8,128)}, f32[128,1024]{1,0:T(8,128)}) custom-call(bf16[784,2560]{1,0:T(8,128)(2,1)} %pad_maximum_fusion.tok_ref, bf16[2560,2816]{1,0:T(8,128)(2,1)} %all-gather.2.cloned.1.call-done.w_ref, f32[8,2816]{1,0:T(8,128)} %maximum_maximum_fusion.taps_ref, bf16[768,128]{1,0:T(8,128)(2,1)} %get-tuple-element.14.c_ref.refs_1_, ...), custom_call_target="tpu_custom_call" | custom-call | flops 12331253760 | bytes 9256960 | tf_op jit(solution)/shard_map/project_ssd/pallas_call | solution.py:145
  158.1 1.1 convert_element_type.41
  159.2 1.5 collective-permute-start.8
  160.8 0.6 collective-permute-start.12
  161.3 11.3 %project_ssd.3 = (f32[768,512]{1,0:T(8,128)}, f32[128,512]{1,0:T(8,128)}) custom-call(bf16[784,2560]{1,0:T(8,128)(2,1)} %pad_maximum_fusion.tok_ref, bf16[2560,2816]{1,0:T(8,128)(2,1)} %all-gather.2.cloned.1.call-done.w_ref, f32[8,2816]{1,0:T(8,128)} %maximum_maximum_fusion.taps_ref, bf16[768,128]{1,0:T(8,128)(2,1)} %get-tuple-element.14.c_ref.refs_1_, ...), custom_call_target="tpu_custom_call" | custom-call | flops 6165626880 | bytes 6635520 | tf_op jit(solution)/shard_map/project_ssd/pallas_call | solution.py:145
  172.7 1.0 convert_element_type.38
  173.6 1.5 collective-permute-start.4
  175.3 1.3 collective-permute-start.15
  176.6 1.3 collective-permute-start.14
  177.9 1.3 collective-permute-start.13
  179.3 1.3 collective-permute-start.11
  180.8 1.0 add_convert_fusion.2
  181.8 1.3 collective-permute-start.7
  183.1 22.1 %collective-permute-done.11.refs_8_ = bf16[128,1024]{1,0:T(8,128)(2,1)S(1)} collective-permute-done((bf16[128,1024]{1,0:T(8,128)(2,1)S(1)}, bf16[128,1024]{1,0:T(8,128)(2,1)S(1)}, u32[]{:S(2)}, u32[]{:S(2)}) %collective-permute-start.11) | collective-permute-done | bytes 262176 | tf_op jit(solution)/shard_map/ppermute | solution.py:213
  205.2 1.3 collective-permute-start.6
  206.6 1.3 collective-permute-start.5
  207.9 1.3 collective-permute-start.10
  209.2 1.3 collective-permute-start.9
  211.0 0.7 stack.11
  211.8 8.0 %head_norm.3.refs_9_ = bf16[768,2560]{1,0:T(8,128)(2,1)} custom-call(f32[768,1024]{1,0:T(8,128)} %get-tuple-element.21.refs_0_, bf16[768,128]{1,0:T(8,128)(2,1)} %get-tuple-element.14.c_ref.refs_1_, f32[10,768,12]{2,1,0:T(8,128)} %bitcast.16, f32[10,8,256]{2,1,0:T(8,128)} %bitcast.20, bf16[128,128]{1,0:T(8,128)(2,1)} %select_convert_fusion.refs_4_, ...), custom_call_target="tpu_custom_call" | custom-call | flops 603979776 | bytes 6291456 | tf_op jit(solution)/shard_map/head_norm/pallas_call | solution.py:193
  219.8 11.9 %collective-permute-done.10.refs_7_ = bf16[128,1024]{1,0:T(8,128)(2,1)S(1)} collective-permute-done((bf16[128,1024]{1,0:T(8,128)(2,1)S(1)}, bf16[128,1024]{1,0:T(8,128)(2,1)S(1)}, u32[]{:S(2)}, u32[]{:S(2)}) %collective-permute-start.10) | collective-permute-done | bytes 262176 | tf_op jit(solution)/shard_map/ppermute | solution.py:213
  231.7 3.2 %collective-permute-done.9.refs_6_ = bf16[128,1024]{1,0:T(8,128)(2,1)S(1)} collective-permute-done((bf16[128,1024]{1,0:T(8,128)(2,1)S(1)}, bf16[128,1024]{1,0:T(8,128)(2,1)S(1)}, u32[]{:S(2)}, u32[]{:S(2)}) %collective-permute-start.9) | collective-permute-done | bytes 262176 | tf_op jit(solution)/shard_map/ppermute | solution.py:213
  234.9 0.7 copy-done.8
  235.6 7.8 %head_norm.4.refs_9_ = bf16[768,2560]{1,0:T(8,128)(2,1)} custom-call(f32[768,1024]{1,0:T(8,128)} %get-tuple-element.19.refs_0_, bf16[768,128]{1,0:T(8,128)(2,1)} %get-tuple-element.14.c_ref.refs_1_, f32[10,768,12]{2,1,0:T(8,128)} %bitcast.17, f32[10,8,256]{2,1,0:T(8,128)} %bitcast.21, ...), custom_call_target="tpu_custom_call", output_to_operand_aliasing={{}: (9, {})} | custom-call | flops 603979776 | bytes 6291456 | tf_op jit(solution)/shard_map/head_norm/pallas_call | solution.py:193
  243.5 0.6 copy-done.12
  244.2 5.0 %head_norm.5 = bf16[768,2560]{1,0:T(8,128)(2,1)} custom-call(f32[768,512]{1,0:T(8,128)} %get-tuple-element.17.refs_0_, bf16[768,128]{1,0:T(8,128)(2,1)} %get-tuple-element.14.c_ref.refs_1_, f32[10,768,12]{2,1,0:T(8,128)} %bitcast.18, f32[10,8,256]{2,1,0:T(8,128)} %bitcast.22, ...), custom_call_target="tpu_custom_call", output_to_operand_aliasing={{}: (9, {})} | custom-call | flops 301989888 | bytes 3145728 | tf_op jit(solution)/shard_map/head_norm/pallas_call | solution.py:193
  (106 shorter events, 4.1 us)
Async XLA Ops:
  6.5 13.4 %copy-start.15 = (f32[4,2816]{1,0:T(4,128)S(1)}, f32[4,2816]{1,0:T(4,128)}, u32[]{:S(2)}) copy-start(f32[4,2816]{1,0:T(4,128)} %param.10) | copy-start | bytes 135172
  6.5 14.8 %copy-start.16 = (f32[2560]{0:T(1024)S(1)}, f32[2560]{0:T(1024)}, u32[]{:S(2)}) copy-start(f32[2560]{0:T(1024)} %param.15) | copy-start | bytes 30724
  6.5 107.3 %all-gather.2.cloned.1.call-start = ((), (), s32[]{:S(2)}) async-start(), calls=%async_computation | async-start | bytes 14868480 | tf_op jit(solution)/shard_map/all_gather | solution.py:235
  8.2 22.3 %collective-permute-start = (bf16[16,2560]{1,0:T(8,128)(2,1)S(1)}, bf16[16,2560]{1,0:T(8,128)(2,1)S(1)}, u32[]{:S(2)}, u32[]{:S(2)}) collective-permute-start(bf16[16,2560]{1,0:T(8,128)(2,1)S(1)} %slice_bitcast_fusion), channel_id=1, source_target_pairs={{0,1},{1,2},{2,3},{3,4},{4,5},{5,6},{6,7},{8,9},{9,10},{10,11},{11... | collective-permute-start | bytes 245768 | tf_op jit(solution)/shard_map/ppermute | solution.py:236
  15.3 8.7 %collective-permute-start.1 = (f32[8,128]{1,0:T(8,128)S(1)}, f32[8,128]{1,0:T(8,128)S(1)}, u32[]{:S(2)}, u32[]{:S(2)}) collective-permute-start(f32[8,128]{1,0:T(8,128)S(1)} %broadcast_in_dim.98), channel_id=1, source_target_pairs={{0,1},{1,0},{2,3},{3,2},{4,5},{5,4},{6,7},{7,6},{8,9},{9,8},{10,11... | collective-permute-start | bytes 12296 | tf_op jit(solution)/shard_map/ppermute | solution.py:213
  18.7 16.0 %copy-start.2 = (f32[10,4,768]{2,1,0:T(4,128)}, f32[10,4,768]{2,1,0:T(4,128)S(1)}, u32[]{:S(2)}) copy-start(f32[10,4,768]{2,1,0:T(4,128)S(1)} %reshape_reshape.2.rowsv_ref) | copy-start | bytes 368644
  24.0 6.4 %collective-permute-start.3 = (f32[8,128]{1,0:T(8,128)S(1)}, f32[8,128]{1,0:T(8,128)S(1)}, u32[]{:S(2)}, u32[]{:S(2)}) collective-permute-start(f32[8,128]{1,0:T(8,128)S(1)} %broadcast_in_dim.102), channel_id=1, source_target_pairs={{0,4},{1,5},{2,6},{3,7},{8,12},{9,13},{10,14},{11,15},{16,20},{17,... | collective-permute-start | bytes 12296 | tf_op jit(solution)/shard_map/ppermute | solution.py:213
  25.3 154.0 %collective-permute-start.2 = (f32[8,128]{1,0:T(8,128)S(1)}, f32[8,128]{1,0:T(8,128)S(1)}, u32[]{:S(2)}, u32[]{:S(2)}) collective-permute-start(f32[8,128]{1,0:T(8,128)S(1)} %broadcast_in_dim.102), channel_id=1, source_target_pairs={{0,2},{1,3},{2,4},{3,5},{4,6},{5,7},{8,10},{9,11},{10,12},{11,13},... | collective-permute-start | bytes 12296 | tf_op jit(solution)/shard_map/ppermute | solution.py:213
  159.2 16.0 %copy-start.1 = (f32[128,1024]{1,0:T(8,128)S(1)}, f32[128,1024]{1,0:T(8,128)}, u32[]{:S(2)}) copy-start(f32[128,1024]{1,0:T(8,128)} %get-tuple-element.22) | copy-start | bytes 1572868
  159.2 20.0 %copy-start = (f32[128,1024]{1,0:T(8,128)S(1)}, f32[128,1024]{1,0:T(8,128)}, u32[]{:S(2)}) copy-start(f32[128,1024]{1,0:T(8,128)} %get-tuple-element.20) | copy-start | bytes 1572868
  159.2 18.6 %collective-permute-start.8 = (bf16[128,1024]{1,0:T(8,128)(2,1)S(1)}, bf16[128,1024]{1,0:T(8,128)(2,1)S(1)}, u32[]{:S(2)}, u32[]{:S(2)}) collective-permute-start(bf16[128,1024]{1,0:T(8,128)(2,1)S(1)} %convert_element_type.41), channel_id=1, source_target_pairs={{0,1},{1,0},{2,3},{3,2},{4,5},{5,4},{6,7},{7,6},{8,9},{9,8},{10,11... | collective-permute-start | bytes 786440 | tf_op jit(solution)/shard_map/ppermute | solution.py:213
  160.8 14.4 %collective-permute-start.12 = (bf16[128,1024]{1,0:T(8,128)(2,1)S(1)}, bf16[128,1024]{1,0:T(8,128)(2,1)S(1)}, u32[]{:S(2)}, u32[]{:S(2)}) collective-permute-start(bf16[128,1024]{1,0:T(8,128)(2,1)S(1)} %convert_element_type.44), channel_id=1, source_target_pairs={{0,1},{1,0},{2,3},{3,2},{4,5},{5,4},{6,7},{7,6},{8,9},{9,8},{10,11... | collective-permute-start | bytes 786440 | tf_op jit(solution)/shard_map/ppermute | solution.py:213
  173.6 7.2 %collective-permute-start.4 = (bf16[128,512]{1,0:T(8,128)(2,1)S(1)}, bf16[128,512]{1,0:T(8,128)(2,1)S(1)}, u32[]{:S(2)}, u32[]{:S(2)}) collective-permute-start(bf16[128,512]{1,0:T(8,128)(2,1)S(1)} %convert_element_type.38), channel_id=1, source_target_pairs={{0,1},{1,0},{2,3},{3,2},{4,5},{5,4},{6,7},{7,6},{8,9},{9,8},{10,11... | collective-permute-start | bytes 393224 | tf_op jit(solution)/shard_map/ppermute | solution.py:213
  175.2 36.6 %copy-start.4 = (bf16[128,1024]{1,0:T(8,128)(2,1)}, bf16[128,1024]{1,0:T(8,128)(2,1)S(1)}, u32[]{:S(2)}) copy-start(bf16[128,1024]{1,0:T(8,128)(2,1)S(1)} %collective-permute-done.12.refs_5_) | copy-start | bytes 786436
  175.3 31.3 %collective-permute-start.15 = (bf16[128,1024]{1,0:T(8,128)(2,1)S(1)}, bf16[128,1024]{1,0:T(8,128)(2,1)S(1)}, u32[]{:S(2)}, u32[]{:S(2)}) collective-permute-start(bf16[128,1024]{1,0:T(8,128)(2,1)S(1)} %add_convert_fusion), channel_id=1, source_target_pairs={{0,6},{1,7},{8,14},{9,15},{16,22},{17,23},{24,30},{25,31}} | collective-permute-start | bytes 786440 | tf_op jit(solution)/shard_map/ppermute | solution.py:213
  176.6 31.3 %collective-permute-start.14 = (bf16[128,1024]{1,0:T(8,128)(2,1)S(1)}, bf16[128,1024]{1,0:T(8,128)(2,1)S(1)}, u32[]{:S(2)}, u32[]{:S(2)}) collective-permute-start(bf16[128,1024]{1,0:T(8,128)(2,1)S(1)} %add_convert_fusion), channel_id=1, source_target_pairs={{0,4},{1,5},{2,6},{3,7},{8,12},{9,13},{10,14},{11,15},{16,20},{17,... | collective-permute-start | bytes 786440 | tf_op jit(solution)/shard_map/ppermute | solution.py:213
  177.9 41.9 %copy-start.3 = (bf16[128,1024]{1,0:T(8,128)(2,1)}, bf16[128,1024]{1,0:T(8,128)(2,1)S(1)}, u32[]{:S(2)}) copy-start(bf16[128,1024]{1,0:T(8,128)(2,1)S(1)} %collective-permute-done.8.refs_5_) | copy-start | bytes 786436
  177.9 31.3 %collective-permute-start.13 = (bf16[128,1024]{1,0:T(8,128)(2,1)S(1)}, bf16[128,1024]{1,0:T(8,128)(2,1)S(1)}, u32[]{:S(2)}, u32[]{:S(2)}) collective-permute-start(bf16[128,1024]{1,0:T(8,128)(2,1)S(1)} %add_convert_fusion), channel_id=1, source_target_pairs={{0,2},{1,3},{2,4},{3,5},{4,6},{5,7},{8,10},{9,11},{10,12},{11,13},... | collective-permute-start | bytes 786440 | tf_op jit(solution)/shard_map/ppermute | solution.py:213
  179.3 25.9 %collective-permute-start.11 = (bf16[128,1024]{1,0:T(8,128)(2,1)S(1)}, bf16[128,1024]{1,0:T(8,128)(2,1)S(1)}, u32[]{:S(2)}, u32[]{:S(2)}) collective-permute-start(bf16[128,1024]{1,0:T(8,128)(2,1)S(1)} %add_convert_fusion.1), channel_id=1, source_target_pairs={{0,6},{1,7},{8,14},{9,15},{16,22},{17,23},{24,30},{25,31}} | collective-permute-start | bytes 786440 | tf_op jit(solution)/shard_map/ppermute | solution.py:213
  180.8 39.0 %copy-start.5 = (bf16[128,512]{1,0:T(8,128)(2,1)}, bf16[128,512]{1,0:T(8,128)(2,1)S(1)}, u32[]{:S(2)}) copy-start(bf16[128,512]{1,0:T(8,128)(2,1)S(1)} %collective-permute-done.4.refs_5_) | copy-start | bytes 393220
  181.8 61.6 %collective-permute-start.7 = (bf16[128,512]{1,0:T(8,128)(2,1)S(1)}, bf16[128,512]{1,0:T(8,128)(2,1)S(1)}, u32[]{:S(2)}, u32[]{:S(2)}) collective-permute-start(bf16[128,512]{1,0:T(8,128)(2,1)S(1)} %add_convert_fusion.2), channel_id=1, source_target_pairs={{0,6},{1,7},{8,14},{9,15},{16,22},{17,23},{24,30},{25,31}} | collective-permute-start | bytes 393224 | tf_op jit(solution)/shard_map/ppermute | solution.py:213
  205.2 14.6 %copy-start.6 = (bf16[128,1024]{1,0:T(8,128)(2,1)}, bf16[128,1024]{1,0:T(8,128)(2,1)S(1)}, u32[]{:S(2)}) copy-start(bf16[128,1024]{1,0:T(8,128)(2,1)S(1)} %collective-permute-done.11.refs_8_) | copy-start | bytes 786436
  205.2 38.2 %collective-permute-start.6 = (bf16[128,512]{1,0:T(8,128)(2,1)S(1)}, bf16[128,512]{1,0:T(8,128)(2,1)S(1)}, u32[]{:S(2)}, u32[]{:S(2)}) collective-permute-start(bf16[128,512]{1,0:T(8,128)(2,1)S(1)} %add_convert_fusion.2), channel_id=1, source_target_pairs={{0,4},{1,5},{2,6},{3,7},{8,12},{9,13},{10,14},{11,15},{16,20},{17,... | collective-permute-start | bytes 393224 | tf_op jit(solution)/shard_map/ppermute | solution.py:213
  206.5 5.2 %copy-start.9 = (bf16[128,1024]{1,0:T(8,128)(2,1)}, bf16[128,1024]{1,0:T(8,128)(2,1)S(1)}, u32[]{:S(2)}) copy-start(bf16[128,1024]{1,0:T(8,128)(2,1)S(1)} %collective-permute-done.15.refs_8_) | copy-start | bytes 786436
  206.6 36.9 %collective-permute-start.5 = (bf16[128,512]{1,0:T(8,128)(2,1)S(1)}, bf16[128,512]{1,0:T(8,128)(2,1)S(1)}, u32[]{:S(2)}, u32[]{:S(2)}) collective-permute-start(bf16[128,512]{1,0:T(8,128)(2,1)S(1)} %add_convert_fusion.2), channel_id=1, source_target_pairs={{0,2},{1,3},{2,4},{3,5},{4,6},{5,7},{8,10},{9,11},{10,12},{11,13},... | collective-permute-start | bytes 393224 | tf_op jit(solution)/shard_map/ppermute | solution.py:213
  207.9 3.9 %copy-start.10 = (bf16[128,1024]{1,0:T(8,128)(2,1)}, bf16[128,1024]{1,0:T(8,128)(2,1)S(1)}, u32[]{:S(2)}) copy-start(bf16[128,1024]{1,0:T(8,128)(2,1)S(1)} %collective-permute-done.14.refs_7_) | copy-start | bytes 786436
  207.9 23.8 %collective-permute-start.10 = (bf16[128,1024]{1,0:T(8,128)(2,1)S(1)}, bf16[128,1024]{1,0:T(8,128)(2,1)S(1)}, u32[]{:S(2)}, u32[]{:S(2)}) collective-permute-start(bf16[128,1024]{1,0:T(8,128)(2,1)S(1)} %add_convert_fusion.1), channel_id=1, source_target_pairs={{0,4},{1,5},{2,6},{3,7},{8,12},{9,13},{10,14},{11,15},{16,20},{17,... | collective-permute-start | bytes 786440 | tf_op jit(solution)/shard_map/ppermute | solution.py:213
  209.2 2.6 %copy-start.11 = (bf16[128,1024]{1,0:T(8,128)(2,1)}, bf16[128,1024]{1,0:T(8,128)(2,1)S(1)}, u32[]{:S(2)}) copy-start(bf16[128,1024]{1,0:T(8,128)(2,1)S(1)} %collective-permute-done.13.refs_6_) | copy-start | bytes 786436
  209.2 25.7 %collective-permute-start.9 = (bf16[128,1024]{1,0:T(8,128)(2,1)S(1)}, bf16[128,1024]{1,0:T(8,128)(2,1)S(1)}, u32[]{:S(2)}, u32[]{:S(2)}) collective-permute-start(bf16[128,1024]{1,0:T(8,128)(2,1)S(1)} %add_convert_fusion.1), channel_id=1, source_target_pairs={{0,2},{1,3},{2,4},{3,5},{4,6},{5,7},{8,10},{9,11},{10,12},{11,13},... | collective-permute-start | bytes 786440 | tf_op jit(solution)/shard_map/ppermute | solution.py:213
  231.7 3.2 %copy-start.7 = (bf16[128,1024]{1,0:T(8,128)(2,1)}, bf16[128,1024]{1,0:T(8,128)(2,1)S(1)}, u32[]{:S(2)}) copy-start(bf16[128,1024]{1,0:T(8,128)(2,1)S(1)} %collective-permute-done.10.refs_7_) | copy-start | bytes 786436
  234.9 0.7 copy-start.8
  243.4 0.6 copy-start.12
  243.4 0.7 copy-start.13
  243.5 0.7 copy-start.14
Sparse Core Ops, SparseCore 0:
  10.3 103.5 all-gather.1

commit v2 on v1

v2 whole, which is shorter than its diff:
```python
import math

import jax
import jax.numpy as jnp
from jax import lax
from jax.experimental import pallas as pl
from jax.experimental.pallas import tpu as pltpu
from jax.sharding import PartitionSpec as P

SPAN = 128
TILE = 256
RIM = 16
VMEM = 56 * 1024 * 1024
LOG2E = math.log2(math.e)
BF16 = jnp.bfloat16
F32 = jnp.float32


def halves(left, right):
    lane = lax.broadcasted_iota(jnp.int32, left.shape, 1)
    return jnp.where(lane < left.shape[1] // 2, left, right)


def spread(columns, index):
    return jnp.broadcast_to(columns[:, index : index + 1], (columns.shape[0], SPAN))


def convolve(rows_ref, taps_ref, base, left):
    cols = pl.ds(left, SPAN)
    accum = jnp.broadcast_to(taps_ref[4:5, cols], (SPAN, SPAN))
    for tap in range(4):
        accum = accum + taps_ref[tap : tap + 1, cols] * rows_ref[pl.ds(base + RIM - 3 + tap, SPAN), cols]
    half = 0.5 * accum
    return half * jnp.tanh(half) + half


def project(tok_ref, w_ref, rows_ref):
    out = jnp.dot(tok_ref[...], w_ref[...], preferred_element_type=F32)
    rows_ref[...] = out.astype(BF16).astype(F32)


def scores_of(taps_ref, c_ref, bt_ref, scores_ref, rows_ref):
    row = lax.broadcasted_iota(jnp.int32, (SPAN, SPAN), 0)
    col = lax.broadcasted_iota(jnp.int32, (SPAN, SPAN), 1)
    for block in range(scores_ref.shape[0]):
        here = pl.ds(block * SPAN, SPAN)
        b_t = convolve(rows_ref, taps_ref, block * SPAN, 0).astype(BF16).astype(F32).T
        c_rows = convolve(rows_ref, taps_ref, block * SPAN, SPAN).astype(BF16)
        bt_ref[:, here] = b_t
        c_ref[here, :] = c_rows
        scores = jnp.dot(c_rows, b_t.astype(BF16), preferred_element_type=F32)
        scores_ref[block] = jnp.where(row >= col, scores, 0.0)


def scan_tile(taps_ref, c_ref, bt_ref, scores_ref, cols_ref, rowsv_ref, lanes_ref, y_ref, state_ref, rows_ref):
    blocks = scores_ref.shape[0]
    pairs = TILE // SPAN
    states = [None] * pairs
    for block in range(blocks):
        here = pl.ds(block * SPAN, SPAN)
        for pair in range(pairs):
            lanes = pl.ds(pair * SPAN, SPAN)
            cols = cols_ref[0, here, :]
            x = convolve(rows_ref, taps_ref, block * SPAN, pair * SPAN).astype(BF16).astype(F32)
            cums = [spread(cols, 2 * pair), spread(cols, 2 * pair + 1)]
            scores, b_t = scores_ref[block], bt_ref[:, here]
            mix, tails = [], []
            for head, cum in enumerate(cums):
                at = 2 * pair + head
                across, step, tail = (rowsv_ref[0, k + at : k + at + 1, here] for k in (0, 4, 8))
                mix.append((jnp.exp2(jnp.minimum(cum - across, 0.0)) * (scores * step)).astype(BF16))
                tails.append((b_t * tail).astype(BF16))
            zero = jnp.zeros_like(x)
            stacked = jnp.concatenate([halves(x, zero), halves(zero, x)], axis=0).astype(BF16)
            weights = jnp.concatenate([jnp.concatenate(mix, axis=1), jnp.concatenate(tails, axis=1)], axis=0)
            out = jnp.dot(weights, stacked, preferred_element_type=F32)
            y, state = out[:SPAN], out[SPAN:]
            if block > 0:
                carried = jnp.dot(c_ref[here, :], states[pair].astype(BF16), preferred_element_type=F32)
                y = y + jnp.exp2(halves(*cums)) * carried
                state = lanes_ref[0, block : block + 1, lanes] * states[pair] + state
            y_ref[here, lanes] = (y + lanes_ref[0, blocks : blocks + 1, lanes] * x).astype(BF16)
            states[pair] = state
    for pair in range(pairs):
        state_ref[:, pl.ds(pair * SPAN, SPAN)] = states[pair]


def scan_kernel(leads, tiles, piece_count, lead_at, base, *refs):
    offsets = refs[0]
    pieces = refs[1 : 1 + piece_count]
    tok_ref, taps_ref, cols_ref, rowsv_ref, lanes_ref, taps_bc_ref = refs[1 + piece_count : 7 + piece_count]
    rest = refs[7 + piece_count : -5]
    w_a, w_b, rows_a, rows_b, sems = refs[-5:]
    if leads:
        y_ref, state_ref, c_ref, bt_ref, scores_ref = rest
    else:
        c_ref, bt_ref, scores_ref, y_ref, state_ref = rest
    step = pl.program_id(0)
    items = tiles + leads
    w_refs, rows_refs = (w_a, w_b), (rows_a, rows_b)

    def fetch(item, slot):
        column = (item - leads + base) * TILE
        if leads:
            column = jnp.where(item == 0, lead_at, column)
        column = pl.multiple_of(column, TILE)
        index = 0
        rows = w_a.shape[0] // offsets.shape[0]
        for piece in pieces:
            for part in range(piece.shape[0] // rows):
                target = pl.multiple_of(offsets[index], 16)
                pltpu.make_async_copy(
                    piece.at[pl.ds(part * rows, rows), pl.ds(column, TILE)],
                    w_refs[slot].at[pl.ds(target, rows)],
                    sems.at[slot],
                ).start()
                index += 1

    def arrive(slot):
        pltpu.make_async_copy(w_refs[slot], w_refs[slot], sems.at[slot]).wait()

    def multiply(slot):
        project(tok_ref, w_refs[slot], rows_refs[slot])

    def finish(slot):
        scan_tile(taps_ref, c_ref, bt_ref, scores_ref, cols_ref, rowsv_ref, lanes_ref, y_ref, state_ref, rows_refs[slot])

    def lead(slot):
        scores_of(taps_bc_ref, c_ref, bt_ref, scores_ref, rows_refs[slot])

    @pl.when(step == 0)
    def _():
        fetch(0, 0)
        arrive(0)
        if items > 1:
            fetch(1, 1)
        multiply(0)

    if leads and items > 1:

        @pl.when(step == 1)
        def _():
            arrive(1)
            if items > 2:
                fetch(2, 0)
            multiply(1)
            lead(0)

    for slot in (0, 1):
        low = 1 + leads

        @pl.when((step >= low) & (step < items) & (lax.rem(step, 2) == slot))
        def _():
            arrive(slot)

            @pl.when(step + 1 < items)
            def _():
                fetch(step + 1, 1 - slot)

            multiply(slot)
            finish(1 - slot)

    @pl.when(step == items)
    def _():
        finish((items - 1) % 2)


def norm_kernel(count, *refs):
    y_ref, c_ref, cols_ref, lanes_ref, gather_ref = refs[:5]
    parts = refs[5 : 5 + count]
    out_ref = refs[-1]
    pairs = TILE // SPAN
    states = []
    for pair in range(pairs):
        lanes = pl.ds(pair * SPAN, SPAN)
        state = sum(lanes_ref[0, k + 1 : k + 2, lanes] * part[:, lanes].astype(F32) for k, part in enumerate(parts))
        states.append(state.astype(BF16))
    for block in range(c_ref.shape[0] // SPAN):
        here = pl.ds(block * SPAN, SPAN)
        for pair in range(pairs):
            lanes = pl.ds(pair * SPAN, SPAN)
            cols = cols_ref[0, here, :]
            cum = halves(spread(cols, 4 + 2 * pair), spread(cols, 5 + 2 * pair))
            carried = jnp.dot(c_ref[here, :], states[pair], preferred_element_type=F32)
            ssd = y_ref[here, lanes].astype(F32) + jnp.exp2(cum) * carried
            mean = jnp.dot((ssd * ssd).astype(BF16), gather_ref[...], preferred_element_type=F32)
            out_ref[here, lanes] = (ssd * lax.rsqrt(mean + 1e-05) * lanes_ref[0, 0:1, lanes]).astype(BF16)


def whole(shape):
    return pl.BlockSpec(shape, lambda *_: (0,) * len(shape))


def params():
    return pltpu.CompilerParams(vmem_limit_bytes=VMEM)


def run_scan(pieces, offsets, lead_at, base, tok_ext, taps, shared, cols, rowsv, lanes, first, tiles):
    rows, depth = tok_ext.shape
    tok_count = rows - RIM
    blocks = tok_count // SPAN
    leads = 1 if shared is None else 0
    behind = lambda i: jnp.clip(i - 1 - leads, 0, tiles - 1)
    per_tile = lambda array: pl.BlockSpec((1,) + array.shape[1:], lambda i: (behind(i) + first, 0, 0))
    ins = [offsets, *pieces, tok_ext, taps, cols, rowsv, lanes, taps]
    specs = [pl.BlockSpec(memory_space=pltpu.SMEM)]
    specs += [pl.BlockSpec(memory_space=pl.ANY)] * len(pieces)
    specs += [
        whole(tok_ext.shape),
        pl.BlockSpec((8, TILE), lambda i: (0, behind(i) + first)),
        per_tile(cols),
        per_tile(rowsv),
        per_tile(lanes),
        pl.BlockSpec((8, TILE), lambda i: (0, taps.shape[1] // TILE - 1)),
    ]
    out_shape = [
        jax.ShapeDtypeStruct((tok_count, tiles * TILE), BF16),
        jax.ShapeDtypeStruct((SPAN, tiles * TILE), F32),
    ]
    out_specs = [
        pl.BlockSpec((tok_count, TILE), lambda i: (0, behind(i))),
        pl.BlockSpec((SPAN, TILE), lambda i: (0, behind(i))),
    ]
    shared_shape = [
        jax.ShapeDtypeStruct((tok_count, SPAN), BF16),
        jax.ShapeDtypeStruct((SPAN, tok_count), F32),
        jax.ShapeDtypeStruct((blocks, SPAN, SPAN), F32),
    ]
    shared_specs = [whole(each.shape) for each in shared_shape]
    if leads:
        out_shape += shared_shape
        out_specs += shared_specs
    else:
        ins += shared
        specs += shared_specs
    outs = pl.pallas_call(
        lambda *refs: scan_kernel(leads, tiles, len(pieces), lead_at, base, *refs),
        grid=(tiles + leads + 1,),
        in_specs=specs,
        out_specs=out_specs,
        out_shape=out_shape,
        scratch_shapes=[pltpu.VMEM((depth, TILE), BF16)] * 2
        + [pltpu.VMEM((rows, TILE), F32)] * 2
        + [pltpu.SemaphoreType.DMA((2,))],
        compiler_params=params(),
        cost_estimate=pl.CostEstimate(
            flops=4 * rows * depth * TILE * (tiles + leads), bytes_accessed=2 * depth * (rows + TILE * tiles), transcendentals=0
        ),
        name="project_scan",
    )(*ins)
    return outs[0], outs[1], (list(outs[2:]) if leads else shared)


def run_norm(out, y, c_rows, cols, lanes, gather, parts, first, width):
    tok_count = c_rows.shape[0]
    tiles = y.shape[1] // TILE
    count = len(parts)
    ins = [y, c_rows, cols, lanes, gather, *parts]
    specs = [
        pl.BlockSpec((tok_count, TILE), lambda i: (0, i)),
        whole(c_rows.shape),
        pl.BlockSpec((1,) + cols.shape[1:], lambda i: (i + first, 0, 0)),
        pl.BlockSpec((1,) + lanes.shape[1:], lambda i: (i + first, 0, 0)),
        whole(gather.shape),
    ] + [pl.BlockSpec((SPAN, TILE), lambda i: (0, i))] * count
    aliases = {}
    if out is not None:
        aliases = {len(ins): 0}
        ins.append(out)
        specs.append(pl.BlockSpec(memory_space=pl.ANY))
    return pl.pallas_call(
        lambda *refs: norm_kernel(count, *refs),
        grid=(tiles,),
        in_specs=specs,
        out_specs=pl.BlockSpec((tok_count, TILE), lambda i: (0, i + first)),
        out_shape=jax.ShapeDtypeStruct((tok_count, width), BF16),
        input_output_aliases=aliases,
        compiler_params=params(),
        cost_estimate=pl.CostEstimate(
            flops=6 * tok_count * SPAN * TILE * tiles, bytes_accessed=8 * tok_count * TILE * tiles, transcendentals=0
        ),
        name="head_norm",
    )(*ins)


def shifted(value, z_by, y_by, z_count, y_count):
    pairs = []
    for z in range(z_count - z_by):
        for y in range(y_count):
            pairs.append((z * y_count + y, (z + z_by) * y_count + (y + y_by) % y_count))
    return lax.ppermute(value, "seq", pairs)


def expand(per_head, head_size):
    return jnp.repeat(per_head, head_size, axis=-1)


def local(tokens, w_xbc, conv_weight, conv_bias, a_log, dt_in, d_skip, norm_gain):
    token_rows = tokens[0]
    tok_count = token_rows.shape[0]
    heads = a_log.shape[0]
    width_x = norm_gain.shape[0]
    head_size = width_x // heads
    channels = w_xbc.shape[1]
    blocks = tok_count // SPAN
    tiles = width_x // TILE
    per_tile = TILE // head_size
    seq_count = lax.axis_size("seq")
    z_count = 4
    y_count = seq_count // z_count
    y_mine = lax.rem(lax.axis_index("seq"), y_count)

    w_full = lax.all_gather(w_xbc, ("dp", "seq"), axis=0, tiled=True)
    rim = lax.ppermute(token_rows[tok_count - RIM :], "seq", [(i, i + 1) for i in range(seq_count - 1)])
    tok_ext = jnp.concatenate([rim, token_rows], axis=0)
    taps = jnp.concatenate([conv_weight, conv_bias[None], jnp.zeros((3, channels), F32)], axis=0)

    step_size = jax.nn.softplus(dt_in[0])
    log_decay = (-LOG2E * jnp.exp(a_log))[:, None] * step_size
    cumul = jnp.cumsum(log_decay.reshape(heads, blocks, SPAN), axis=2)
    totals = cumul[:, :, -1]
    before = jnp.cumsum(totals, axis=1) - totals
    tail = (jnp.exp2(totals[:, :, None] - cumul) * step_size.reshape(heads, blocks, SPAN)).reshape(heads, tok_count)
    cum_full = (cumul + before[:, :, None]).reshape(heads, tok_count)
    own_decay = jnp.sum(totals, axis=1)
    cumul = cumul.reshape(heads, tok_count)
    by_tile = lambda rows: rows.reshape(tiles, per_tile, tok_count)
    cols = jnp.concatenate([by_tile(cumul), by_tile(cum_full)], axis=1).transpose(0, 2, 1)
    rowsv = jnp.concatenate([by_tile(cumul), by_tile(step_size), by_tile(tail), by_tile(jnp.zeros_like(tail))], axis=1)
    lane_tiles = lambda rows: rows.reshape(rows.shape[0], tiles, TILE).transpose(1, 0, 2)
    lane_rows = [expand(jnp.exp2(totals).T, head_size), expand(d_skip[None], head_size)]
    lane_rows.append(jnp.zeros((-(blocks + 1) % 8, width_x), F32))
    lanes = lane_tiles(jnp.concatenate(lane_rows, axis=0))

    side = jnp.broadcast_to(jnp.pad(own_decay, (0, SPAN - heads))[None], (8, SPAN))
    y_decay = [own_decay] + [shifted(side, 0, k, z_count, y_count)[0, :heads] for k in range(1, y_count)]
    y_place = [lax.rem(y_mine - k + y_count, y_count) for k in range(y_count)]
    z_own = jnp.broadcast_to(jnp.pad(sum(y_decay), (0, SPAN - heads))[None], (8, SPAN))
    z_decay = [shifted(z_own, k, 0, z_count, y_count)[0, :heads] for k in range(1, z_count - 1)]
    zero = jnp.zeros_like(own_decay)
    group_coef, own_coef = [], []
    for k in range(y_count):
        after = sum(jnp.where(y_place[m] > y_place[k], y_decay[m], zero) for m in range(y_count))
        until = sum(jnp.where((y_place[m] > y_place[k]) & (y_place[m] < y_mine), y_decay[m], zero) for m in range(y_count))
        group_coef.append(expand(jnp.exp2(after), head_size))
        own_coef.append(expand(jnp.where(y_place[k] < y_mine, jnp.exp2(until), zero), head_size))
    inside = sum(jnp.where(y_place[m] < y_mine, y_decay[m], zero) for m in range(y_count))
    z_coef = []
    for k in range(1, z_count):
        z_coef.append(expand(jnp.exp2(inside + sum(z_decay[: k - 1], zero)), head_size))
    coef_rows = [norm_gain] + own_coef[1:] + z_coef
    coef_rows += [jnp.zeros_like(norm_gain)] * (-len(coef_rows) % 8)
    coefs = lane_tiles(jnp.stack(coef_rows))
    head_of = jnp.arange(SPAN) // head_size
    gather = jnp.where(head_of[:, None] == head_of[None, :], 1.0 / head_size, 0.0).astype(BF16)

    shared = None
    cuts = [0, 4, 7, tiles]
    offsets = jnp.zeros((1,), jnp.int32)
    pending = []
    for first, last in zip(cuts[:-1], cuts[1:]):
        y, own, shared = run_scan(
            [w_full], offsets, tiles * TILE, first, tok_ext, taps, shared, cols, rowsv, lanes, first, last - first
        )
        lane = slice(first * TILE, last * TILE)
        sent = own.astype(BF16)
        y_parts = [shifted(sent, 0, k, z_count, y_count) for k in range(1, y_count)]
        group = group_coef[0][lane] * own
        for k, part in enumerate(y_parts):
            group = group + group_coef[k + 1][lane] * part.astype(F32)
        group = group.astype(BF16)
        z_parts = [shifted(group, k, 0, z_count, y_count) for k in range(1, z_count)]
        pending.append((y, y_parts + z_parts, first))
    out = None
    for y, parts, first in pending:
        out = run_norm(out, y, shared[0], cols, coefs, gather, parts, first, width_x)
    return out[None]


def solution(mesh):
    return jax.shard_map(
        local,
        mesh=mesh,
        in_specs=(
            P("dp", "seq", None),
            P(("dp", "seq"), None),
            P(),
            P(),
            P(),
            P("dp", None, "seq"),
            P(),
            P(),
        ),
        out_specs=P("dp", "seq", None),
        check_vma=False,
    )
```

time: 260 us -> 241 us (0.927); the launches traced: 256 us -> 240 us
  Pallas kernels: 75.4 us -> 56.7 us
  waiting for transfers between devices: 119 us -> 122 us
    pallas_call x4 -> x3, Pallas kernels: 54.5 us -> 40.9 us  [run_scan(): pl.pallas_call(lambda *refs: scan_kernel(leads, tiles, len(pieces), lead_...]
    ppermute x15, waiting for transfers between devices: 39.5 us -> 45.2 us  [shifted(): return lax.ppermute(value, 'seq', pairs)]
    pallas_call x3, Pallas kernels: 20.8 us -> 15.8 us  [run_norm(): pl.pallas_call(lambda *refs: norm_kernel(count, *refs), grid=(tiles,), in...]
    all_gather x1, waiting for transfers between devices: 79.1 us -> 76.1 us  [local(): w_full = lax.all_gather(w_xbc, ('dp', 'seq'), axis=0, tiled=True)]
  transfers between devices with their start and end apart: 17 -> 17, of which waited for: 5 -> 7; matrix products, arithmetic and copies ran while one was open for 10% -> 10% of each run, Pallas kernels for 27% -> 10%
where the time goes in v2:
time: 241 us; the launch traced here: 240 us
  waiting for transfers between devices  122 us (51%)
  Pallas kernels  56.7 us (24%)
  starting transfers between devices  21.4 us (9%)
  between operations  13.9 us (6%)
  other arithmetic  13.8 us (6%)
  local copies, waits for them, and re-layouts  12.5 us (5%)
    all_gather x1, waiting for transfers between devices, local(): w_full = lax.all_gather(w_xbc, ('dp', 'seq'), axis=0, tiled=True)  76.1 us
    ppermute x15, waiting for transfers between devices, shifted(): return lax.ppermute(value, 'seq', pairs)  45.2 us
    pallas_call x3, Pallas kernels, run_scan(): pl.pallas_call(lambda *refs: scan_kernel(leads, tiles, len(pieces), lead_...  40.9 us
    ppermute x15, starting transfers between devices, shifted(): return lax.ppermute(value, 'seq', pairs)  18 us
    pallas_call x3, Pallas kernels, run_norm(): pl.pallas_call(lambda *refs: norm_kernel(count, *refs), grid=(tiles,), in...  15.8 us
  transfers between devices with their start and end apart: 17, of which 7 were waited for; matrix products, arithmetic and copies ran while one was open for 10% of the time, Pallas kernels for 10%

profile of v2, /device:TPU:24, one launch (start us, length us, event | category | flops | bytes accessed | tf_op | source)
XLA Modules:
  0.0 240.2 jit_solution(15613962196495772255)
XLA Ops:
  6.5 0.7 all-gather.2.cloned.1.call-update
  7.3 0.9 slice_bitcast_fusion
  8.2 3.4 %collective-permute-start = (bf16[16,2560]{1,0:T(8,128)(2,1)S(1)}, bf16[16,2560]{1,0:T(8,128)(2,1)S(1)}, u32[]{:S(2)}, u32[]{:S(2)}) collective-permute-start(bf16[16,2560]{1,0:T(8,128)(2,1)S(1)} %slice_bitcast_fusion), channel_id=1, source_target_pairs={{0,1},{1,2},{2,3},{3,4},{4,5},{5,6},{6,7},{8,9},{9,10},{10,11},{11... | collective-permute-start | bytes 245768 | tf_op jit(solution)/shard_map/ppermute | solution.py:314
  11.6 0.9 squeeze.19
  12.5 0.7 exponential_multiply_fusion.1
  13.3 1.8 reduce_window_sum.22
  15.4 0.9 squeeze.20
  16.3 0.7 broadcast_in_dim.89
  18.0 0.7 broadcast_in_dim.92
  19.6 0.9 pad_maximum_fusion.1.refs_5_
  20.5 0.7 select_convert_fusion.refs_4_
  21.2 0.7 maximum_maximum_fusion.refs_3_.refs_7_
  21.9 0.7 maximum_bitcast_fusion.refs_6_
  22.5 2.5 %copy.42 = f32[10,8,768]{1,2,0:T(8,128)} copy(f32[10,8,768]{2,1,0:T(8,128)S(1)} %pad_maximum_fusion.2) | data formatting | bytes 491520 | tf_op jit(solution)/shard_map/concatenate | solution.py:328
  25.1 1.3 collective-permute-start.2
  26.4 1.3 collective-permute-start.3
  29.1 1.7 collective-permute-done.2
  30.9 2.5 %collective-permute-done.3 = f32[8,128]{1,0:T(8,128)S(1)} collective-permute-done((f32[8,128]{1,0:T(8,128)S(1)}, f32[8,128]{1,0:T(8,128)S(1)}, u32[]{:S(2)}, u32[]{:S(2)}) %collective-permute-start.3) | collective-permute-done | bytes 4128 | tf_op jit(solution)/shard_map/ppermute | solution.py:291
  33.5 4.3 %pad_maximum_fusion.refs_2_ = bf16[784,2560]{1,0:T(8,128)(2,1)} fusion(bf16[768,2560]{1,0:T(8,128)(2,1)} %bitcast.22, bf16[16,2560]{1,0:T(8,128)(2,1)S(1)} %collective-permute-done), kind=kLoop, calls=%fused_computation | loop fusion | flops 8028160 | bytes 8028160 | tf_op jit(solution)/shard_map/concatenate | solution.py:315
  37.7 76.1 %all-gather.2.cloned.1.call-done.refs_1_ = bf16[2560,2816]{1,0:T(8,128)(2,1)} async-done(((bf16[80,2816]{1,0:T(8,128)(2,1)}), bf16[2560,2816]{1,0:T(8,128)(2,1)}) %all-gather.2.cloned.1.call-update) | async-done | bytes 14417936 | tf_op jit(solution)/shard_map/all_gather | solution.py:313
  113.8 16.3 %project_scan.3 = (bf16[768,1024]{1,0:T(8,128)(2,1)}, f32[128,1024]{1,0:T(8,128)}, bf16[768,128]{1,0:T(8,128)(2,1)}, f32[128,768]{1,0:T(8,128)}, f32[6,128,128]{2,1,0:T(8,128)}) custom-call(s32[1]{0:T(128)} %constant.51.clone.1.refs_0_, bf16[2560,2816]{1,0:T(8,128)(2,1)} %all-gather.2.cloned.1.call-done.refs_1_, bf16[784,2560]{1,0:T(8,128)(2,1)} %pad_maximum_fusion.refs_2_, ...), custom_call_target="tpu_custom_call" | custom-call | flops 10276044800 | bytes 9256960 | tf_op jit(solution)/shard_map/project_scan/pallas_call | solution.py:236
  130.1 12.4 %project_scan.4 = (bf16[768,768]{1,0:T(8,128)(2,1)}, f32[128,768]{1,0:T(8,128)}) custom-call(s32[1]{0:T(128)} %constant.51.clone.1.refs_0_, bf16[2560,2816]{1,0:T(8,128)(2,1)} %all-gather.2.cloned.1.call-done.refs_1_, bf16[784,2560]{1,0:T(8,128)(2,1)} %pad_maximum_fusion.refs_2_, f32[8,2816]{1,0:T(8,128)} %maximum_maximum_fusion.refs_3_.refs_7_, ...), custom_call_target="tpu_custom_call" | custom-call | flops 6165626880 | bytes 7946240 | tf_op jit(solution)/shard_map/project_scan/pallas_call | solution.py:236
  142.5 1.0 convert_element_type.38
  143.6 1.5 collective-permute-start.4
  145.2 0.6 collective-permute-start.12
  145.8 12.2 %project_scan.5 = (bf16[768,768]{1,0:T(8,128)(2,1)}, f32[128,768]{1,0:T(8,128)}) custom-call(s32[1]{0:T(128)} %constant.51.clone.1.refs_0_, bf16[2560,2816]{1,0:T(8,128)(2,1)} %all-gather.2.cloned.1.call-done.refs_1_, bf16[784,2560]{1,0:T(8,128)(2,1)} %pad_maximum_fusion.refs_2_, f32[8,2816]{1,0:T(8,128)} %maximum_maximum_fusion.refs_3_.refs_7_, ...), custom_call_target="tpu_custom_call" | custom-call | flops 6165626880 | bytes 7946240 | tf_op jit(solution)/shard_map/project_scan/pallas_call | solution.py:236
  158.0 1.0 convert_element_type.41
  159.0 1.5 collective-permute-start.8
  160.7 1.3 collective-permute-start.13
  162.0 1.3 collective-permute-start.14
  163.3 1.3 collective-permute-start.15
  164.6 1.1 collective-permute-done.8.refs_5_
  165.7 1.1 add_convert_fusion.1
  166.8 1.3 collective-permute-start.9
  168.2 1.3 collective-permute-start.5
  169.5 8.7 %collective-permute-done.9.refs_6_ = bf16[128,768]{1,0:T(8,128)(2,1)S(1)} collective-permute-done((bf16[128,768]{1,0:T(8,128)(2,1)S(1)}, bf16[128,768]{1,0:T(8,128)(2,1)S(1)}, u32[]{:S(2)}, u32[]{:S(2)}) %collective-permute-start.9) | collective-permute-done | bytes 196640 | tf_op jit(solution)/shard_map/ppermute | solution.py:291
  178.2 1.3 collective-permute-start.6
  179.5 1.3 collective-permute-start.7
  180.8 8.9 %collective-permute-done.14.refs_7_ = bf16[128,1024]{1,0:T(8,128)(2,1)S(1)} collective-permute-done((bf16[128,1024]{1,0:T(8,128)(2,1)S(1)}, bf16[128,1024]{1,0:T(8,128)(2,1)S(1)}, u32[]{:S(2)}, u32[]{:S(2)}) %collective-permute-start.14) | collective-permute-done | bytes 262176 | tf_op jit(solution)/shard_map/ppermute | solution.py:291
  189.7 1.3 collective-permute-start.10
  191.0 1.3 collective-permute-start.11
  192.8 0.7 stack.11
  193.6 5.8 %head_norm.3.refs_9_ = bf16[768,2560]{1,0:T(8,128)(2,1)} custom-call(bf16[768,1024]{1,0:T(8,128)(2,1)} %get-tuple-element.21.refs_0_, bf16[768,128]{1,0:T(8,128)(2,1)} %get-tuple-element.14.refs_8_.refs_1_, f32[10,768,8]{2,1,0:T(8,128)} %bitcast.19, f32[10,8,256]{2,1,0:T(8,128)} %bitcast.23, bf16[128,128]{1,0:T(8,128)(2,1)} %select_convert_fusion.refs_4_, ...), custom_call_target="tpu_custom_call" | custom-call | flops 603979776 | bytes 6291456 | tf_op jit(solution)/shard_map/head_norm/pallas_call | solution.py:271
  199.4 22.4 %collective-permute-done.10.refs_7_ = bf16[128,768]{1,0:T(8,128)(2,1)S(1)} collective-permute-done((bf16[128,768]{1,0:T(8,128)(2,1)S(1)}, bf16[128,768]{1,0:T(8,128)(2,1)S(1)}, u32[]{:S(2)}, u32[]{:S(2)}) %collective-permute-start.10) | collective-permute-done | bytes 196640 | tf_op jit(solution)/shard_map/ppermute | solution.py:291
  221.8 0.7 copy-done.12
  222.5 5.0 %head_norm.4.refs_9_ = bf16[768,2560]{1,0:T(8,128)(2,1)} custom-call(bf16[768,768]{1,0:T(8,128)(2,1)} %get-tuple-element.19.refs_0_, bf16[768,128]{1,0:T(8,128)(2,1)} %get-tuple-element.14.refs_8_.refs_1_, f32[10,768,8]{2,1,0:T(8,128)} %bitcast.20, f32[10,8,256]{2,1,0:T(8,128)} %bitcast.24, ...), custom_call_target="tpu_custom_call", output_to_operand_aliasing={{}: (9, {})} | custom-call | flops 452984832 | bytes 4718592 | tf_op jit(solution)/shard_map/head_norm/pallas_call | solution.py:271
  227.6 0.6 copy-done.8
  228.4 5.0 %head_norm.5 = bf16[768,2560]{1,0:T(8,128)(2,1)} custom-call(bf16[768,768]{1,0:T(8,128)(2,1)} %get-tuple-element.17.refs_0_, bf16[768,128]{1,0:T(8,128)(2,1)} %get-tuple-element.14.refs_8_.refs_1_, f32[10,768,8]{2,1,0:T(8,128)} %bitcast.21, f32[10,8,256]{2,1,0:T(8,128)} %bitcast.25, ...), custom_call_target="tpu_custom_call", output_to_operand_aliasing={{}: (9, {})} | custom-call | flops 452984832 | bytes 4718592 | tf_op jit(solution)/shard_map/head_norm/pallas_call | solution.py:271
  (106 shorter events, 4.7 us)
Async XLA Ops:
  6.5 14.6 %copy-start.14 = (f32[4,2816]{1,0:T(4,128)S(1)}, f32[4,2816]{1,0:T(4,128)}, u32[]{:S(2)}) copy-start(f32[4,2816]{1,0:T(4,128)} %param.10) | copy-start | bytes 135172
  6.5 107.3 %all-gather.2.cloned.1.call-start = ((), (), s32[]{:S(2)}) async-start(), calls=%async_computation | async-start | bytes 14868480 | tf_op jit(solution)/shard_map/all_gather | solution.py:313
  8.2 25.3 %collective-permute-start = (bf16[16,2560]{1,0:T(8,128)(2,1)S(1)}, bf16[16,2560]{1,0:T(8,128)(2,1)S(1)}, u32[]{:S(2)}, u32[]{:S(2)}) collective-permute-start(bf16[16,2560]{1,0:T(8,128)(2,1)S(1)} %slice_bitcast_fusion), channel_id=1, source_target_pairs={{0,1},{1,2},{2,3},{3,4},{4,5},{5,6},{6,7},{8,9},{9,10},{10,11},{11... | collective-permute-start | bytes 245768 | tf_op jit(solution)/shard_map/ppermute | solution.py:314
  15.3 9.8 %collective-permute-start.1 = (f32[8,128]{1,0:T(8,128)S(1)}, f32[8,128]{1,0:T(8,128)S(1)}, u32[]{:S(2)}, u32[]{:S(2)}) collective-permute-start(f32[8,128]{1,0:T(8,128)S(1)} %broadcast_in_dim.98), channel_id=1, source_target_pairs={{0,1},{1,0},{2,3},{3,2},{4,5},{5,4},{6,7},{7,6},{8,9},{9,8},{10,11... | collective-permute-start | bytes 12296 | tf_op jit(solution)/shard_map/ppermute | solution.py:291
  18.0 7.1 %copy-start.15 = (f32[2560]{0:T(1024)S(1)}, f32[2560]{0:T(1024)}, u32[]{:S(2)}) copy-start(f32[2560]{0:T(1024)} %param.15) | copy-start | bytes 30724
  25.1 5.6 %collective-permute-start.2 = (f32[8,128]{1,0:T(8,128)S(1)}, f32[8,128]{1,0:T(8,128)S(1)}, u32[]{:S(2)}, u32[]{:S(2)}) collective-permute-start(f32[8,128]{1,0:T(8,128)S(1)} %broadcast_in_dim.102), channel_id=1, source_target_pairs={{0,2},{1,3},{2,4},{3,5},{4,6},{5,7},{8,10},{9,11},{10,12},{11,13},... | collective-permute-start | bytes 12296 | tf_op jit(solution)/shard_map/ppermute | solution.py:291
  26.4 6.9 %collective-permute-start.3 = (f32[8,128]{1,0:T(8,128)S(1)}, f32[8,128]{1,0:T(8,128)S(1)}, u32[]{:S(2)}, u32[]{:S(2)}) collective-permute-start(f32[8,128]{1,0:T(8,128)S(1)} %broadcast_in_dim.102), channel_id=1, source_target_pairs={{0,4},{1,5},{2,6},{3,7},{8,12},{9,13},{10,14},{11,15},{16,20},{17,... | collective-permute-start | bytes 12296 | tf_op jit(solution)/shard_map/ppermute | solution.py:291
  130.1 15.0 %copy-start = (f32[128,1024]{1,0:T(8,128)S(1)}, f32[128,1024]{1,0:T(8,128)}, u32[]{:S(2)}) copy-start(f32[128,1024]{1,0:T(8,128)} %get-tuple-element.22) | copy-start | bytes 1572868
  143.6 24.6 %collective-permute-start.4 = (bf16[128,768]{1,0:T(8,128)(2,1)S(1)}, bf16[128,768]{1,0:T(8,128)(2,1)S(1)}, u32[]{:S(2)}, u32[]{:S(2)}) collective-permute-start(bf16[128,768]{1,0:T(8,128)(2,1)S(1)} %convert_element_type.38), channel_id=1, source_target_pairs={{0,1},{1,0},{2,3},{3,2},{4,5},{5,4},{6,7},{7,6},{8,9},{9,8},{10,11... | collective-permute-start | bytes 589832 | tf_op jit(solution)/shard_map/ppermute | solution.py:291
  145.1 23.0 %copy-start.1 = (f32[128,768]{1,0:T(8,128)S(1)}, f32[128,768]{1,0:T(8,128)}, u32[]{:S(2)}) copy-start(f32[128,768]{1,0:T(8,128)} %get-tuple-element.18) | copy-start | bytes 1179652
  145.2 15.4 %collective-permute-start.12 = (bf16[128,1024]{1,0:T(8,128)(2,1)S(1)}, bf16[128,1024]{1,0:T(8,128)(2,1)S(1)}, u32[]{:S(2)}, u32[]{:S(2)}) collective-permute-start(bf16[128,1024]{1,0:T(8,128)(2,1)S(1)} %convert_element_type.44), channel_id=1, source_target_pairs={{0,1},{1,0},{2,3},{3,2},{4,5},{5,4},{6,7},{7,6},{8,9},{9,8},{10,11... | collective-permute-start | bytes 786440 | tf_op jit(solution)/shard_map/ppermute | solution.py:291
  159.0 6.7 %collective-permute-start.8 = (bf16[128,768]{1,0:T(8,128)(2,1)S(1)}, bf16[128,768]{1,0:T(8,128)(2,1)S(1)}, u32[]{:S(2)}, u32[]{:S(2)}) collective-permute-start(bf16[128,768]{1,0:T(8,128)(2,1)S(1)} %convert_element_type.41), channel_id=1, source_target_pairs={{0,1},{1,0},{2,3},{3,2},{4,5},{5,4},{6,7},{7,6},{8,9},{9,8},{10,11... | collective-permute-start | bytes 589832 | tf_op jit(solution)/shard_map/ppermute | solution.py:291
  160.6 33.0 %copy-start.2 = (bf16[128,1024]{1,0:T(8,128)(2,1)}, bf16[128,1024]{1,0:T(8,128)(2,1)S(1)}, u32[]{:S(2)}) copy-start(bf16[128,1024]{1,0:T(8,128)(2,1)S(1)} %collective-permute-done.12.refs_5_) | copy-start | bytes 786436
  160.7 18.8 %collective-permute-start.13 = (bf16[128,1024]{1,0:T(8,128)(2,1)S(1)}, bf16[128,1024]{1,0:T(8,128)(2,1)S(1)}, u32[]{:S(2)}, u32[]{:S(2)}) collective-permute-start(bf16[128,1024]{1,0:T(8,128)(2,1)S(1)} %add_convert_fusion), channel_id=1, source_target_pairs={{0,2},{1,3},{2,4},{3,5},{4,6},{5,7},{8,10},{9,11},{10,12},{11,13},... | collective-permute-start | bytes 786440 | tf_op jit(solution)/shard_map/ppermute | solution.py:291
  162.0 27.7 %collective-permute-start.14 = (bf16[128,1024]{1,0:T(8,128)(2,1)S(1)}, bf16[128,1024]{1,0:T(8,128)(2,1)S(1)}, u32[]{:S(2)}, u32[]{:S(2)}) collective-permute-start(bf16[128,1024]{1,0:T(8,128)(2,1)S(1)} %add_convert_fusion), channel_id=1, source_target_pairs={{0,4},{1,5},{2,6},{3,7},{8,12},{9,13},{10,14},{11,15},{16,20},{17,... | collective-permute-start | bytes 786440 | tf_op jit(solution)/shard_map/ppermute | solution.py:291
  163.3 27.7 %collective-permute-start.15 = (bf16[128,1024]{1,0:T(8,128)(2,1)S(1)}, bf16[128,1024]{1,0:T(8,128)(2,1)S(1)}, u32[]{:S(2)}, u32[]{:S(2)}) collective-permute-start(bf16[128,1024]{1,0:T(8,128)(2,1)S(1)} %add_convert_fusion), channel_id=1, source_target_pairs={{0,6},{1,7},{8,14},{9,15},{16,22},{17,23},{24,30},{25,31}} | collective-permute-start | bytes 786440 | tf_op jit(solution)/shard_map/ppermute | solution.py:291
  165.7 33.7 %copy-start.4 = (bf16[128,768]{1,0:T(8,128)(2,1)}, bf16[128,768]{1,0:T(8,128)(2,1)S(1)}, u32[]{:S(2)}) copy-start(bf16[128,768]{1,0:T(8,128)(2,1)S(1)} %collective-permute-done.8.refs_5_) | copy-start | bytes 589828
  166.8 11.4 %collective-permute-start.9 = (bf16[128,768]{1,0:T(8,128)(2,1)S(1)}, bf16[128,768]{1,0:T(8,128)(2,1)S(1)}, u32[]{:S(2)}, u32[]{:S(2)}) collective-permute-start(bf16[128,768]{1,0:T(8,128)(2,1)S(1)} %add_convert_fusion.1), channel_id=1, source_target_pairs={{0,2},{1,3},{2,4},{3,5},{4,6},{5,7},{8,10},{9,11},{10,12},{11,13},... | collective-permute-start | bytes 589832 | tf_op jit(solution)/shard_map/ppermute | solution.py:291
  168.2 31.2 %copy-start.3 = (bf16[128,768]{1,0:T(8,128)(2,1)}, bf16[128,768]{1,0:T(8,128)(2,1)S(1)}, u32[]{:S(2)}) copy-start(bf16[128,768]{1,0:T(8,128)(2,1)S(1)} %collective-permute-done.4.refs_5_) | copy-start | bytes 589828
  168.2 59.3 %collective-permute-start.5 = (bf16[128,768]{1,0:T(8,128)(2,1)S(1)}, bf16[128,768]{1,0:T(8,128)(2,1)S(1)}, u32[]{:S(2)}, u32[]{:S(2)}) collective-permute-start(bf16[128,768]{1,0:T(8,128)(2,1)S(1)} %add_convert_fusion.2), channel_id=1, source_target_pairs={{0,2},{1,3},{2,4},{3,5},{4,6},{5,7},{8,10},{9,11},{10,12},{11,13},... | collective-permute-start | bytes 589832 | tf_op jit(solution)/shard_map/ppermute | solution.py:291
  178.2 43.6 %copy-start.10 = (bf16[128,768]{1,0:T(8,128)(2,1)}, bf16[128,768]{1,0:T(8,128)(2,1)S(1)}, u32[]{:S(2)}) copy-start(bf16[128,768]{1,0:T(8,128)(2,1)S(1)} %collective-permute-done.9.refs_6_) | copy-start | bytes 589828
  178.2 49.3 %collective-permute-start.6 = (bf16[128,768]{1,0:T(8,128)(2,1)S(1)}, bf16[128,768]{1,0:T(8,128)(2,1)S(1)}, u32[]{:S(2)}, u32[]{:S(2)}) collective-permute-start(bf16[128,768]{1,0:T(8,128)(2,1)S(1)} %add_convert_fusion.2), channel_id=1, source_target_pairs={{0,4},{1,5},{2,6},{3,7},{8,12},{9,13},{10,14},{11,15},{16,20},{17,... | collective-permute-start | bytes 589832 | tf_op jit(solution)/shard_map/ppermute | solution.py:291
  179.5 14.1 %copy-start.5 = (bf16[128,1024]{1,0:T(8,128)(2,1)}, bf16[128,1024]{1,0:T(8,128)(2,1)S(1)}, u32[]{:S(2)}) copy-start(bf16[128,1024]{1,0:T(8,128)(2,1)S(1)} %collective-permute-done.13.refs_6_) | copy-start | bytes 786436
  179.5 48.0 %collective-permute-start.7 = (bf16[128,768]{1,0:T(8,128)(2,1)S(1)}, bf16[128,768]{1,0:T(8,128)(2,1)S(1)}, u32[]{:S(2)}, u32[]{:S(2)}) collective-permute-start(bf16[128,768]{1,0:T(8,128)(2,1)S(1)} %add_convert_fusion.2), channel_id=1, source_target_pairs={{0,6},{1,7},{8,14},{9,15},{16,22},{17,23},{24,30},{25,31}} | collective-permute-start | bytes 589832 | tf_op jit(solution)/shard_map/ppermute | solution.py:291
  189.7 3.9 %copy-start.6 = (bf16[128,1024]{1,0:T(8,128)(2,1)}, bf16[128,1024]{1,0:T(8,128)(2,1)S(1)}, u32[]{:S(2)}) copy-start(bf16[128,1024]{1,0:T(8,128)(2,1)S(1)} %collective-permute-done.14.refs_7_) | copy-start | bytes 786436
  189.7 32.1 %collective-permute-start.10 = (bf16[128,768]{1,0:T(8,128)(2,1)S(1)}, bf16[128,768]{1,0:T(8,128)(2,1)S(1)}, u32[]{:S(2)}, u32[]{:S(2)}) collective-permute-start(bf16[128,768]{1,0:T(8,128)(2,1)S(1)} %add_convert_fusion.1), channel_id=1, source_target_pairs={{0,4},{1,5},{2,6},{3,7},{8,12},{9,13},{10,14},{11,15},{16,20},{17,... | collective-permute-start | bytes 589832 | tf_op jit(solution)/shard_map/ppermute | solution.py:291
  191.0 2.6 %copy-start.7 = (bf16[128,1024]{1,0:T(8,128)(2,1)}, bf16[128,1024]{1,0:T(8,128)(2,1)S(1)}, u32[]{:S(2)}) copy-start(bf16[128,1024]{1,0:T(8,128)(2,1)S(1)} %collective-permute-done.15.refs_8_) | copy-start | bytes 786436
  191.0 30.8 %collective-permute-start.11 = (bf16[128,768]{1,0:T(8,128)(2,1)S(1)}, bf16[128,768]{1,0:T(8,128)(2,1)S(1)}, u32[]{:S(2)}, u32[]{:S(2)}) collective-permute-start(bf16[128,768]{1,0:T(8,128)(2,1)S(1)} %add_convert_fusion.1), channel_id=1, source_target_pairs={{0,6},{1,7},{8,14},{9,15},{16,22},{17,23},{24,30},{25,31}} | collective-permute-start | bytes 589832 | tf_op jit(solution)/shard_map/ppermute | solution.py:291
  221.8 0.7 copy-start.12
  221.8 0.8 copy-start.13
  227.5 0.7 copy-start.8
  227.5 0.8 copy-start.9
  227.6 0.8 copy-start.11
Sparse Core Ops, SparseCore 0:
  10.3 103.4 all-gather.1

commit v3 on v2

v3 whole, which is shorter than its diff:
```python
import math

import jax
import jax.numpy as jnp
from jax import lax
from jax.experimental import pallas as pl
from jax.experimental.pallas import tpu as pltpu
from jax.sharding import PartitionSpec as P

SPAN = 128
TILE = 256
RIM = 16
VMEM = 56 * 1024 * 1024
LOG2E = math.log2(math.e)
BF16 = jnp.bfloat16
F32 = jnp.float32


def halves(left, right):
    lane = lax.broadcasted_iota(jnp.int32, left.shape, 1)
    return jnp.where(lane < left.shape[1] // 2, left, right)


def spread(columns, index):
    return jnp.broadcast_to(columns[:, index : index + 1], (columns.shape[0], SPAN))


def convolve(rows_ref, taps_ref, base, left):
    cols = pl.ds(left, SPAN)
    accum = jnp.broadcast_to(taps_ref[4:5, cols], (SPAN, SPAN))
    for tap in range(4):
        accum = accum + taps_ref[tap : tap + 1, cols] * rows_ref[pl.ds(base + RIM - 3 + tap, SPAN), cols]
    half = 0.5 * accum
    return half * jnp.tanh(half) + half


def project(tok_ref, w_ref, rows_ref):
    out = jnp.dot(tok_ref[...], w_ref[...], preferred_element_type=F32)
    rows_ref[...] = out.astype(BF16).astype(F32)


def running_sum(row):
    place = lax.broadcasted_iota(jnp.int32, row.shape, 1)
    by = 1
    while by < row.shape[1]:
        row = row + jnp.where(place >= by, pltpu.roll(row, by, 1), 0.0)
        by *= 2
    return row


def decay_kernel(raw_ref, rate_ref, decay_ref, grow_ref, reach_ref, tails_ref):
    pairs = TILE // SPAN
    heads = 2 * pairs
    count = raw_ref.shape[1]
    blocks = count // heads
    raw = raw_ref[0]
    steps = jnp.maximum(raw, 0.0) + jnp.log1p(jnp.exp(-jnp.abs(raw)))
    rows = running_sum(rate_ref[0] * steps)
    totals = rows[:, SPAN - 1 :]
    tails = jnp.exp2(jnp.minimum(totals - rows, 0.0)) * steps
    before = [jnp.zeros((heads, 1), F32)]
    for block in range(blocks - 1):
        before.append(before[-1] + totals[block * heads : (block + 1) * heads])
    padding = jnp.zeros((SPAN - 2 * count, SPAN), F32)
    cols = jnp.concatenate([rows, rows + jnp.concatenate(before, axis=0), padding], axis=0).T
    for block in range(blocks):
        here = pl.ds(block * SPAN, SPAN)
        for pair in range(pairs):
            lanes = pl.ds(pair * SPAN, SPAN)
            first = block * heads + 2 * pair
            cums = [spread(cols, first), spread(cols, first + 1)]
            for head, cum in enumerate(cums):
                at = first + head
                decay = jnp.exp2(jnp.minimum(cum - rows[at : at + 1], 0.0)) * steps[at : at + 1]
                decay_ref[0, pair, here, pl.ds(head * SPAN, SPAN)] = decay.astype(BF16)
                row = block * pairs + pair
                tails_ref[0, row : row + 1, pl.ds(head * SPAN, SPAN)] = tails[at : at + 1]
            grow_ref[here, lanes] = jnp.exp2(halves(*cums)).astype(BF16)
            reach = halves(spread(cols, count + first), spread(cols, count + first + 1))
            reach_ref[here, lanes] = jnp.exp2(reach).astype(BF16)


def scores_of(taps_ref, c_ref, bt_ref, scores_ref, rows_ref):
    row = lax.broadcasted_iota(jnp.int32, (SPAN, SPAN), 0)
    col = lax.broadcasted_iota(jnp.int32, (SPAN, SPAN), 1)
    for block in range(scores_ref.shape[0]):
        here = pl.ds(block * SPAN, SPAN)
        b_t = convolve(rows_ref, taps_ref, block * SPAN, 0).astype(BF16).astype(F32).T
        c_rows = convolve(rows_ref, taps_ref, block * SPAN, SPAN).astype(BF16)
        bt_ref[:, here] = b_t
        c_ref[here, :] = c_rows
        scores = jnp.dot(c_rows, b_t.astype(BF16), preferred_element_type=F32)
        scores = jnp.where(row >= col, scores, 0.0).astype(BF16)
        scores_ref[block] = jnp.concatenate([scores, scores], axis=1)


def scan_tile(taps_ref, c_ref, bt_ref, scores_ref, decay_ref, grow_ref, tails_ref, lanes_ref, y_ref, state_ref, sent_ref, rows_ref):
    blocks = scores_ref.shape[0]
    pairs = TILE // SPAN
    states = [None] * pairs
    for block in range(blocks):
        here = pl.ds(block * SPAN, SPAN)
        for pair in range(pairs):
            lanes = pl.ds(pair * SPAN, SPAN)
            x = convolve(rows_ref, taps_ref, block * SPAN, pair * SPAN).astype(BF16).astype(F32)
            mix = decay_ref[0, pair, here, :] * scores_ref[block]
            b_t = bt_ref[:, here]
            at = block * pairs + pair
            tail = jnp.concatenate([b_t, b_t], axis=1) * tails_ref[0, at : at + 1, :]
            zero = jnp.zeros_like(x)
            stacked = jnp.concatenate([halves(x, zero), halves(zero, x)], axis=0).astype(BF16)
            weights = jnp.concatenate([mix, tail.astype(BF16)], axis=0)
            out = jnp.dot(weights, stacked, preferred_element_type=F32)
            y, state = out[:SPAN], out[SPAN:]
            if block > 0:
                carried = jnp.dot(c_ref[here, :], states[pair].astype(BF16), preferred_element_type=F32)
                y = y + grow_ref[here, lanes].astype(F32) * carried
                state = lanes_ref[0, block : block + 1, lanes] * states[pair] + state
            y_ref[here, lanes] = (y + lanes_ref[0, blocks : blocks + 1, lanes] * x).astype(BF16)
            states[pair] = state
    for pair in range(pairs):
        state_ref[:, pl.ds(pair * SPAN, SPAN)] = states[pair]
        sent_ref[:, pl.ds(pair * SPAN, SPAN)] = states[pair].astype(BF16)


def scan_kernel(leads, tiles, piece_count, lead_at, base, *refs):
    offsets = refs[0]
    pieces = refs[1 : 1 + piece_count]
    rim_ref, tokens_ref, taps_ref, decay_ref, grow_ref, tails_ref, lanes_ref, taps_bc_ref = refs[1 + piece_count : 9 + piece_count]
    rest = refs[9 + piece_count : -6]
    tok_ref, w_a, w_b, rows_a, rows_b, sems = refs[-6:]
    if leads:
        y_ref, state_ref, sent_ref, c_ref, bt_ref, scores_ref = rest
    else:
        c_ref, bt_ref, scores_ref, y_ref, state_ref, sent_ref = rest
    step = pl.program_id(0)
    items = tiles + leads
    w_refs, rows_refs = (w_a, w_b), (rows_a, rows_b)

    def fetch(item, slot):
        column = (item - leads + base) * TILE
        if leads:
            column = jnp.where(item == 0, lead_at, column)
        column = pl.multiple_of(column, TILE)
        index = 0
        rows = w_a.shape[0] // offsets.shape[0]
        for piece in pieces:
            for part in range(piece.shape[0] // rows):
                target = pl.multiple_of(offsets[index], 16)
                pltpu.make_async_copy(
                    piece.at[pl.ds(part * rows, rows), pl.ds(column, TILE)],
                    w_refs[slot].at[pl.ds(target, rows)],
                    sems.at[slot],
                ).start()
                index += 1

    def arrive(slot):
        pltpu.make_async_copy(w_refs[slot], w_refs[slot], sems.at[slot]).wait()

    def multiply(slot):
        project(tok_ref, w_refs[slot], rows_refs[slot])

    def finish(slot):
        scan_tile(
            taps_ref, c_ref, bt_ref, scores_ref, decay_ref, grow_ref, tails_ref, lanes_ref, y_ref, state_ref, sent_ref, rows_refs[slot]
        )

    def lead(slot):
        scores_of(taps_bc_ref, c_ref, bt_ref, scores_ref, rows_refs[slot])

    @pl.when(step == 0)
    def _():
        copies = [
            pltpu.make_async_copy(rim_ref, tok_ref.at[pl.ds(0, RIM)], sems.at[2]),
            pltpu.make_async_copy(tokens_ref, tok_ref.at[pl.ds(RIM, tokens_ref.shape[0])], sems.at[3]),
        ]
        for copy in copies:
            copy.start()
        fetch(0, 0)
        for copy in copies:
            copy.wait()
        arrive(0)
        if items > 1:
            fetch(1, 1)
        multiply(0)

    if leads and items > 1:

        @pl.when(step == 1)
        def _():
            arrive(1)
            if items > 2:
                fetch(2, 0)
            multiply(1)
            lead(0)

    for slot in (0, 1):
        low = 1 + leads

        @pl.when((step >= low) & (step < items) & (lax.rem(step, 2) == slot))
        def _():
            arrive(slot)

            @pl.when(step + 1 < items)
            def _():
                fetch(step + 1, 1 - slot)

            multiply(slot)
            finish(1 - slot)

    @pl.when(step == items)
    def _():
        finish((items - 1) % 2)


def norm_kernel(y_ref, c_ref, reach_ref, gain_ref, gather_ref, state_ref, *rest):
    out_ref = rest[-1]
    carried = jnp.dot(c_ref[...], state_ref[...], preferred_element_type=F32)
    ssd = y_ref[...].astype(F32) + reach_ref[...].astype(F32) * carried
    mean = jnp.dot((ssd * ssd).astype(BF16), gather_ref[...], preferred_element_type=F32)
    out_ref[...] = (ssd * lax.rsqrt(mean + 1e-05) * gain_ref[...]).astype(BF16)


def whole(shape):
    return pl.BlockSpec(shape, lambda *_: (0,) * len(shape))


def params():
    return pltpu.CompilerParams(vmem_limit_bytes=VMEM)


def run_decay(raw, rate):
    tiles, count = raw.shape[:2]
    pairs = TILE // SPAN
    tok_count = count // (2 * pairs) * SPAN
    rounds = pairs * tok_count // SPAN
    tail_rows = rounds + -rounds % 8
    return pl.pallas_call(
        decay_kernel,
        grid=(tiles,),
        in_specs=[
            pl.BlockSpec((1, count, SPAN), lambda i: (i, 0, 0)),
            pl.BlockSpec((1, count, 1), lambda i: (i, 0, 0)),
        ],
        out_specs=[
            pl.BlockSpec((1, pairs, tok_count, 2 * SPAN), lambda i: (i, 0, 0, 0)),
            pl.BlockSpec((tok_count, TILE), lambda i: (0, i)),
            pl.BlockSpec((tok_count, TILE), lambda i: (0, i)),
            pl.BlockSpec((1, tail_rows, 2 * SPAN), lambda i: (i, 0, 0)),
        ],
        out_shape=[
            jax.ShapeDtypeStruct((tiles, pairs, tok_count, 2 * SPAN), BF16),
            jax.ShapeDtypeStruct((tok_count, tiles * TILE), BF16),
            jax.ShapeDtypeStruct((tok_count, tiles * TILE), BF16),
            jax.ShapeDtypeStruct((tiles, tail_rows, 2 * SPAN), F32),
        ],
        compiler_params=params(),
        cost_estimate=pl.CostEstimate(flops=10_000_000_000, bytes_accessed=16_000_000, transcendentals=0),
        name="decays",
    )(raw, rate)


def run_scan(pieces, offsets, lead_at, base, rim, tokens, taps, shared, decay, grow, tails, lanes, first, tiles):
    tok_count, depth = tokens.shape
    rows = tok_count + RIM
    blocks = tok_count // SPAN
    leads = 1 if shared is None else 0
    behind = lambda i: jnp.clip(i - 1 - leads, 0, tiles - 1)
    per_tile = lambda array: pl.BlockSpec((1,) + array.shape[1:], lambda i: (behind(i) + first, 0, 0))
    ins = [offsets, *pieces, rim, tokens, taps, decay, grow, tails, lanes, taps]
    specs = [pl.BlockSpec(memory_space=pltpu.SMEM)]
    specs += [pl.BlockSpec(memory_space=pl.ANY)] * (len(pieces) + 2)
    specs += [
        pl.BlockSpec((8, TILE), lambda i: (0, behind(i) + first)),
        pl.BlockSpec((1,) + decay.shape[1:], lambda i: (behind(i) + first, 0, 0, 0)),
        pl.BlockSpec((tok_count, TILE), lambda i: (0, behind(i) + first)),
        per_tile(tails),
        per_tile(lanes),
        pl.BlockSpec((8, TILE), lambda i: (0, taps.shape[1] // TILE - 1)),
    ]
    out_shape = [
        jax.ShapeDtypeStruct((tok_count, tiles * TILE), BF16),
        jax.ShapeDtypeStruct((SPAN, tiles * TILE), F32),
        jax.ShapeDtypeStruct((SPAN, tiles * TILE), BF16),
    ]
    out_specs = [
        pl.BlockSpec((tok_count, TILE), lambda i: (0, behind(i))),
        pl.BlockSpec((SPAN, TILE), lambda i: (0, behind(i))),
        pl.BlockSpec((SPAN, TILE), lambda i: (0, behind(i))),
    ]
    shared_shape = [
        jax.ShapeDtypeStruct((tok_count, SPAN), BF16),
        jax.ShapeDtypeStruct((SPAN, tok_count), F32),
        jax.ShapeDtypeStruct((blocks, SPAN, 2 * SPAN), BF16),
    ]
    shared_specs = [whole(each.shape) for each in shared_shape]
    if leads:
        out_shape += shared_shape
        out_specs += shared_specs
    else:
        ins += shared
        specs += shared_specs
    outs = pl.pallas_call(
        lambda *refs: scan_kernel(leads, tiles, len(pieces), lead_at, base, *refs),
        grid=(tiles + leads + 1,),
        in_specs=specs,
        out_specs=out_specs,
        out_shape=out_shape,
        scratch_shapes=[pltpu.VMEM((rows, depth), BF16)]
        + [pltpu.VMEM((depth, TILE), BF16)] * 2
        + [pltpu.VMEM((rows, TILE), F32)] * 2
        + [pltpu.SemaphoreType.DMA((4,))],
        compiler_params=params(),
        cost_estimate=pl.CostEstimate(flops=1, bytes_accessed=1, transcendentals=0),
        name="project_scan",
    )(*ins)
    return *outs[:3], (list(outs[3:]) if leads else shared)


def run_norm(out, y, c_rows, reach, gain, gather, state, first, base, tiles, width):
    tok_count = c_rows.shape[0]
    ins = [y, c_rows, reach, gain, gather, state]
    specs = [
        pl.BlockSpec((tok_count, TILE), lambda i: (0, i + base)),
        whole(c_rows.shape),
        pl.BlockSpec((tok_count, TILE), lambda i: (0, i + first)),
        pl.BlockSpec((1, TILE), lambda i: (0, i + first)),
        whole(gather.shape),
        pl.BlockSpec((SPAN, TILE), lambda i: (0, i + base)),
    ]
    aliases = {}
    if out is not None:
        aliases = {len(ins): 0}
        ins.append(out)
        specs.append(pl.BlockSpec(memory_space=pl.ANY))
    return pl.pallas_call(
        norm_kernel,
        grid=(tiles,),
        in_specs=specs,
        out_specs=pl.BlockSpec((tok_count, TILE), lambda i: (0, i + first)),
        out_shape=jax.ShapeDtypeStruct((tok_count, width), BF16),
        input_output_aliases=aliases,
        compiler_params=params(),
        cost_estimate=pl.CostEstimate(flops=400_000_000 * tiles, bytes_accessed=5 * tok_count * TILE * tiles, transcendentals=0),
        name="head_norm",
    )(*ins)


def shifted(value, z_by, y_by, z_count, y_count):
    pairs = []
    for z in range(z_count - z_by):
        for y in range(y_count):
            pairs.append((z * y_count + y, (z + z_by) * y_count + (y + y_by) % y_count))
    return lax.ppermute(value, "seq", pairs)


def stack(*arrays):
    return jnp.concatenate(arrays, axis=0)


def together(*arrays):
    return lax.optimization_barrier(arrays)


class Links:
    def __init__(self, z_count, y_count):
        self.z_count, self.y_count = z_count, y_count

    def index(self, x, core, z, y):
        return (x * 2 + core) * self.z_count * self.y_count + z * self.y_count + y

    def send(self, value, target):
        pairs = []
        for x in range(2):
            for core in range(2):
                for z in range(self.z_count):
                    for y in range(self.y_count):
                        pairs.append((self.index(x, core, z, y), self.index(*target(x, core, z, y))))
        return lax.ppermute(value, ("dp", "seq"), pairs)

    def along_z(self, value, by):
        return self.send(value, lambda x, core, z, y: (x, core, (z + by) % self.z_count, y))

    def first(self, value):
        return self.send(value, lambda x, core, z, y: (x, core, z, 1 - y) if core else (1 - x, core, z, y))

    def second(self, value):
        return self.send(value, lambda x, core, z, y: (1 - x, core, z, y) if core else (x, core, z, 1 - y))

    def sibling(self, value):
        return self.send(value, lambda x, core, z, y: (x, 1 - core, z, y))

    def gather(self, own, early, decays, last):
        z1, z3, own_1, own_2 = together(self.along_z(own, 1), self.along_z(own, 3), self.first(own), self.second(own))
        near = stack(z1, z3)
        z2, near_1, near_2, own_12, *early = together(
            self.along_z(own, 2), self.first(near), self.second(near), self.second(own_1), *early
        )
        mine = stack(own, own_1, own_2, own_12)
        far_1, far_2, near_12, mine_other, *decays = together(
            self.first(z2), self.second(z2), self.second(near_1), self.sibling(mine), *decays(early)
        )
        beside = stack(near, near_1, near_2, near_12)
        far_12, beside_other, *last = together(self.second(far_1), self.sibling(beside), *last(early))
        far = stack(z2, far_1, far_2, far_12)
        return [mine, beside, far, mine_other, beside_other, self.sibling(far)], early, decays, last

    def owners(self):
        dp, seq = lax.axis_index("dp"), lax.axis_index("seq")
        x, core = dp // 2, dp % 2
        z, y = seq // self.y_count, seq % self.y_count
        places = []
        for at in (core, 1 - core):
            for hops in ((0,), (1, 3), (2,)):
                for by_first, by_second in ((0, 0), (1, 0), (0, 1), (1, 1)):
                    for hop in hops:
                        turn_x = jnp.where(at == 0, by_first, by_second)
                        turn_y = jnp.where(at == 0, by_second, by_first)
                        other = (z - hop + self.z_count) % self.z_count
                        places.append(self.index((x + turn_x) % 2, at, other, (y + turn_y) % 2))
        return jnp.stack(places).astype(jnp.int32)


def expand(per_head, head_size):
    return jnp.repeat(per_head, head_size, axis=-1)


def local(tokens, w_xbc, conv_weight, conv_bias, a_log, dt_in, d_skip, norm_gain):
    token_rows = tokens[0]
    tok_count = token_rows.shape[0]
    heads = a_log.shape[0]
    width_x = norm_gain.shape[0]
    head_size = width_x // heads
    channels = w_xbc.shape[1]
    blocks = tok_count // SPAN
    tiles = width_x // TILE
    per_tile = TILE // head_size
    seq_count = lax.axis_size("seq")
    z_count = 4
    y_count = seq_count // z_count
    y_mine = lax.rem(lax.axis_index("seq"), y_count)

    rim = lax.ppermute(token_rows[tok_count - RIM :], "seq", [(i, i + 1) for i in range(seq_count - 1)])
    taps = jnp.concatenate([conv_weight, conv_bias[None], jnp.zeros((3, channels), F32)], axis=0)
    rate = -LOG2E * jnp.exp(a_log)
    totals = rate[:, None] * jnp.sum(jax.nn.softplus(dt_in[0]).reshape(heads, blocks, SPAN), axis=2)
    head_of = jnp.arange(TILE) // head_size
    gather = jnp.where(head_of[:, None] == head_of[None, :], 1.0 / head_size, 0.0).astype(BF16)

    def lane_rows(totals):
        rows = jnp.concatenate([jnp.exp2(totals).T, d_skip[None]], axis=0)
        rows = jnp.pad(expand(rows, head_size), ((0, -(blocks + 1) % 8), (0, 0)))
        return rows.reshape(rows.shape[0], tiles, TILE).transpose(1, 0, 2)

    def along_y(totals):
        own = jnp.sum(totals, axis=1)
        side = jnp.broadcast_to(jnp.pad(own, (0, SPAN - heads))[None], (8, SPAN))
        return [own] + [shifted(side, 0, k, z_count, y_count)[0, :heads] for k in range(1, y_count)]

    def along_z(y_decay):
        own = jnp.broadcast_to(jnp.pad(sum(y_decay), (0, SPAN - heads))[None], (8, SPAN))
        return [shifted(own, k, 0, z_count, y_count)[0, :heads] for k in range(1, z_count - 1)]

    def z_weights(z_decay):
        reach = [jnp.zeros((heads,), F32)]
        for decay in z_decay:
            reach.append(reach[-1] + decay)
        return reach[1:]

    gathered = lambda rows: lax.all_gather(rows, ("dp", "seq"), axis=0, tiled=True)
    whole_rows = jnp.zeros((1,), jnp.int32)
    by_block = lambda rows: rows.reshape(tiles, per_tile, blocks, -1).swapaxes(1, 2).reshape(tiles, blocks * per_tile, -1)
    raw = by_block(dt_in[0])
    rates = by_block(jnp.broadcast_to(rate[:, None], (heads, blocks)))
    lanes = lane_rows(totals)
    if lax.axis_size("dp") == 4 and seq_count == 8:
        split = tiles // 2
        links = Links(z_count, y_count)
        late_w = gathered(w_xbc[:, : split * TILE])
        early_rows = links.owners() * w_xbc.shape[0]

        def coefs(y_decay):
            pair = [jnp.where(y_mine == 0, y_decay[k], y_decay[1 - k]) for k in (0, 1)]
            rows = jnp.stack(pair + z_weights(along_z(y_decay)))
            return [expand(jnp.exp2(rows), head_size)]

        early_w, prepared, (decay, grow, reach, tails), (weights,) = links.gather(
            w_xbc[:, split * TILE :],
            (rim, taps, lanes, gather, early_rows, raw, rates, *along_y(totals)),
            lambda ready: run_decay(*ready[5:7]),
            lambda ready: coefs(ready[7:]),
        )
        rim, taps, lanes, gather, early_rows = prepared[:5]
        calls = [(early_w, early_rows, split, 0, tiles - split), ([late_w], whole_rows, 0, 0, split)]
        lead_at = (tiles - split) * TILE

        def incoming(own, sent, lane):
            e0, e1, z2, z3 = weights[:, lane]
            half = own.shape[1] // 2
            upper = y_mine == 1
            of_mine = lambda value: jnp.where(upper, value[..., half:], value[..., :half])
            of_other = lambda value: jnp.where(upper, value[..., :half], value[..., half:])
            swap = lambda value: shifted(value, 0, 1, z_count, y_count)
            mine = of_mine(own)
            other = swap(of_other(sent)).astype(F32)
            e0, e1, z2, z3 = (of_mine(row) for row in (e0, e1, z2, z3))
            plane = jnp.where(upper, mine + e1 * other, e1 * mine + other).astype(BF16)
            below = [shifted(plane, k, 0, z_count, y_count).astype(F32) for k in range(1, z_count)]
            base = below[0] + z2 * below[1] + z3 * below[2]
            above = e0 * base + jnp.where(upper, other, mine)
            theirs = swap(jnp.where(upper, base, above).astype(BF16))
            ours = jnp.where(upper, above, base).astype(BF16)
            return jnp.where(upper, jnp.concatenate([theirs, ours], axis=1), jnp.concatenate([ours, theirs], axis=1))

    else:
        full = gathered(w_xbc)
        calls = [([full], whole_rows, first, first, min(5, tiles - first)) for first in range(0, tiles, 5)]
        lead_at = tiles * TILE
        decay, grow, reach, tails = run_decay(raw, rates)
        y_decay = along_y(totals)
        z_reach = z_weights(along_z(y_decay))

        def incoming(own, sent, lane):
            place = [lax.rem(y_mine - k + y_count, y_count) for k in range(y_count)]
            spread_lanes = lambda row: expand(row, head_size)[lane]
            inner = lambda keep: sum(jnp.where(keep(m), y_decay[m], 0.0) for m in range(y_count))
            parts = [own] + [shifted(sent, 0, k, z_count, y_count).astype(F32) for k in range(1, y_count)]
            plane, above = 0.0, 0.0
            for k, part in enumerate(parts):
                after = inner(lambda m: place[m] > place[k])
                until = inner(lambda m: (place[m] > place[k]) & (place[m] < y_mine))
                plane = plane + spread_lanes(jnp.exp2(after)) * part
                above = above + spread_lanes(jnp.where(place[k] < y_mine, jnp.exp2(until), 0.0)) * part
            inside = inner(lambda m: place[m] < y_mine)
            plane = plane.astype(BF16)
            for k in range(1, z_count):
                along = inside if k == 1 else inside + z_reach[k - 2]
                above = above + spread_lanes(jnp.exp2(along)) * shifted(plane, k, 0, z_count, y_count).astype(F32)
            return above.astype(BF16)

    shared = None
    pending = []
    for pieces, places, first, base, count in calls:
        y, own, sent, shared = run_scan(
            pieces, places, lead_at, base, rim, token_rows, taps, shared, decay, grow, tails, lanes, first, count
        )
        state = incoming(own, sent, slice(first * TILE, (first + count) * TILE))
        pending.append((y, state, first))
    out = None
    for y, state, first in pending:
        count = y.shape[1] // TILE
        cuts = (0, count // 2, count) if first + count == tiles else (0, count)
        for base, last in zip(cuts[:-1], cuts[1:]):
            out = run_norm(
                out, y, shared[0], reach, norm_gain[None], gather, state, first + base, base, last - base, width_x
            )
    return out[None]


def solution(mesh):
    return jax.shard_map(
        local,
        mesh=mesh,
        in_specs=(
            P("dp", "seq", None),
            P(("dp", "seq"), None),
            P(),
            P(),
            P(),
            P("dp", None, "seq"),
            P(),
            P(),
        ),
        out_specs=P("dp", "seq", None),
        check_vma=False,
    )
```

time: 241 us -> 192 us (0.80)
  waiting for transfers between devices: 122 us -> 47.3 us
  starting transfers between devices: 21.4 us -> 35 us
  Pallas kernels: 56.7 us -> 68.2 us
  local copies, waits for them, and re-layouts: 12.5 us -> 16.5 us
  other arithmetic: 13.8 us -> 10.5 us
    all_gather x1, waiting for transfers between devices: 76.1 us -> 0.02 us  [local(): lax.all_gather(rows, ('dp', 'seq'), axis=0, tiled=True)]
    pallas_call x3 -> x4, Pallas kernels: 15.8 us -> 34.1 us  [the longest x1 20.3 us: run_decay(): pl.pallas_call(decay_kernel, grid=(tiles,), in_specs=[pl.BlockSpec((1, co...]
    ppermute x15 -> x13, waiting for transfers between devices: 45.2 us -> 29.2 us  [shifted(): return lax.ppermute(value, 'seq', pairs)]
    ppermute x0 -> x15, starting transfers between devices: none -> 13.1 us  [send(): return lax.ppermute(value, ('dp', 'seq'), pairs)]
    ppermute x1, waiting for transfers between devices: 0.01 us -> 12 us  [local(): lax.ppermute(token_rows[tok_count - RIM:], 'seq', [(i, i + 1) for i in ra...]
    pallas_call x3 -> x2, Pallas kernels: 40.9 us -> 34.1 us  [run_scan(): pl.pallas_call(lambda *refs: scan_kernel(leads, tiles, len(pieces), lead_...]
    ppermute x0 -> x15, waiting for transfers between devices: none -> 6.03 us  [send(): return lax.ppermute(value, ('dp', 'seq'), pairs)]
    concatenate x3 -> x2, other arithmetic: 5.25 us -> 1.25 us  [the longest x1 1.24 us: stack(): return jnp.concatenate(arrays, axis=0)]
  transfers between devices with their start and end apart: 17 -> 30, of which waited for: 7 -> 10; matrix products, arithmetic and copies ran while one was open for 10% -> 12% of each run, Pallas kernels for 10% -> 32%
where the time goes in v3:
time: 192 us; the launch traced here: 191 us
  Pallas kernels  68.2 us (36%)
  waiting for transfers between devices  47.3 us (25%)
  starting transfers between devices  35 us (18%)
  local copies, waits for them, and re-layouts  16.5 us (9%)
  between operations  13.8 us (7%)
  other arithmetic  10.5 us (5%)
    pallas_call x2, Pallas kernels, run_scan(): pl.pallas_call(lambda *refs: scan_kernel(leads, tiles, len(pieces), lead_...  34.1 us
    ppermute x13, waiting for transfers between devices, shifted(): return lax.ppermute(value, 'seq', pairs)  29.2 us
    pallas_call x1, Pallas kernels, run_decay(): pl.pallas_call(decay_kernel, grid=(tiles,), in_specs=[pl.BlockSpec((1, co...  20.3 us
    ppermute x13, starting transfers between devices, shifted(): return lax.ppermute(value, 'seq', pairs)  18.8 us
    pallas_call x3, Pallas kernels, run_norm(): pl.pallas_call(norm_kernel, grid=(tiles,), in_specs=specs, out_specs=pl.B...  13.7 us
    ppermute x15, starting transfers between devices, send(): return lax.ppermute(value, ('dp', 'seq'), pairs)  13.1 us
    ppermute x1, waiting for transfers between devices, local(): lax.ppermute(token_rows[tok_count - RIM:], 'seq', [(i, i + 1) for i in ra...  12 us
    ppermute x15, waiting for transfers between devices, send(): return lax.ppermute(value, ('dp', 'seq'), pairs)  6.03 us
  transfers between devices with their start and end apart: 30, of which 10 were waited for; matrix products, arithmetic and copies ran while one was open for 12% of the time, Pallas kernels for 32%

profile of v3, /device:TPU:24, one launch (start us, length us, event | category | flops | bytes accessed | tf_op | source)
XLA Modules:
  0.0 191.3 jit_solution(1176429905924952370)
XLA Ops:
  6.5 1.6 slice.135
  8.2 1.0 slice.136
  9.3 2.0 %collective-permute-start.2 = (bf16[80,1536]{1,0:T(8,128)(2,1)S(1)}, bf16[80,1536]{1,0:T(8,128)(2,1)S(1)}, u32[]{:S(2)}, u32[]{:S(2)}) collective-permute-start(bf16[80,1536]{1,0:T(8,128)(2,1)S(1)} %slice.136), channel_id=1, source_target_pairs={{0,6},{1,7},{2,0},{3,1},{4,2},{5,3},{6,4},{7,5},{8,14},{9,15},{10,... | collective-permute-start | bytes 737288 | tf_op jit(solution)/shard_map/ppermute | solution.py:379
  11.3 1.5 collective-permute-start.3
  12.8 1.5 collective-permute-start.4
  17.4 1.5 maximum_maximum_fusion.refs_9_.refs_14_.refs_4_
  18.9 1.5 slice_bitcast_fusion
  21.8 2.9 %collective-permute-start.9 = (f32[8,128]{1,0:T(8,128)S(1)}, f32[8,128]{1,0:T(8,128)S(1)}, u32[]{:S(2)}, u32[]{:S(2)}) collective-permute-start(f32[8,128]{1,0:T(8,128)S(1)} %broadcast_in_dim.32), channel_id=1, source_target_pairs={{0,1},{1,0},{2,3},{3,2},{4,5},{5,4},{6,7},{7,6},{8,9},{9,8},{10,11... | collective-permute-start | bytes 12296 | tf_op jit(solution)/shard_map/ppermute | solution.py:354
  26.2 1.5 collective-permute-start.5
  27.7 1.3 collective-permute-start.6
  31.3 1.5 pad.11
  33.6 3.2 %collective-permute-start.8 = (bf16[16,2560]{1,0:T(8,128)(2,1)}, bf16[16,2560]{1,0:T(8,128)(2,1)S(1)}, u32[]{:S(2)}, u32[]{:S(2)}) collective-permute-start(bf16[16,2560]{1,0:T(8,128)(2,1)} %slice_bitcast_fusion), channel_id=1, source_target_pairs={{0,1},{1,2},{2,3},{3,4},{4,5},{5,6},{6,7},{8,9},{9,10},{10,11},{11... | collective-permute-start | bytes 245768 | tf_op jit(solution)/shard_map/ppermute | solution.py:443
  36.9 12.0 %collective-permute-done.8.refs_7_.refs_2_ = bf16[16,2560]{1,0:T(8,128)(2,1)S(1)} collective-permute-done((bf16[16,2560]{1,0:T(8,128)(2,1)}, bf16[16,2560]{1,0:T(8,128)(2,1)S(1)}, u32[]{:S(2)}, u32[]{:S(2)}) %collective-permute-start.8) | collective-permute-done | bytes 81952 | tf_op jit(solution)/shard_map/ppermute | solution.py:443
  49.9 1.2 pad_maximum_fusion.refs_1_
  51.3 2.1 %collective-permute-start.12 = (bf16[160,1536]{1,0:T(8,128)(2,1)S(1)}, bf16[160,1536]{1,0:T(8,128)(2,1)S(1)}, u32[]{:S(2)}, u32[]{:S(2)}) collective-permute-start(bf16[160,1536]{1,0:T(8,128)(2,1)S(1)} %collective-permute-done.5), channel_id=1, source_target_pairs={{0,1},{1,0},{2,3},{3,2},{4,5},{5,4},{6,7},{7,6},{8,24},{9,25},{10,... | collective-permute-start | bytes 1474568 | tf_op jit(solution)/shard_map/ppermute | solution.py:379
  53.4 20.3 %decays.1 = (bf16[10,2,768,256]{3,2,1,0:T(8,128)(2,1)}, bf16[768,2560]{1,0:T(8,128)(2,1)}, bf16[768,2560]{1,0:T(8,128)(2,1)}, f32[10,16,256]{2,1,0:T(8,128)}) custom-call(f32[10,24,128]{2,1,0:T(8,128)} %bitcast.56, f32[10,24,1]{2,1,0:T(8,128)} %copy.25.rate_ref), custom_call_target="tpu_custom_call" | custom-call | flops 10000000000 | bytes 16000000 | tf_op jit(solution)/shard_map/decays/pallas_call | solution.py:238
  73.9 1.0 copy-done.5
  75.0 1.3 collective-permute-start.16
  76.3 1.5 collective-permute-start.17
  77.7 1.0 constant_dynamic-update-slice_fusion.10
  78.7 5.9 %collective-permute-done.16 = f32[8,128]{1,0:T(8,128)S(1)} collective-permute-done((f32[8,128]{1,0:T(8,128)S(1)}, f32[8,128]{1,0:T(8,128)S(1)}, u32[]{:S(2)}, u32[]{:S(2)}) %collective-permute-start.16) | collective-permute-done | bytes 4128 | tf_op jit(solution)/shard_map/ppermute | solution.py:354
  84.7 2.5 %collective-permute-done.17 = f32[8,128]{1,0:T(8,128)S(1)} collective-permute-done((f32[8,128]{1,0:T(8,128)S(1)}, f32[8,128]{1,0:T(8,128)S(1)}, u32[]{:S(2)}, u32[]{:S(2)}) %collective-permute-start.17) | collective-permute-done | bytes 4128 | tf_op jit(solution)/shard_map/ppermute | solution.py:354
  87.4 1.7 collective-permute-start.14
  89.1 1.0 constant_dynamic-update-slice_fusion.9
  90.1 1.0 constant_dynamic-update-slice_fusion.8
  91.0 2.8 %collective-permute-done.14 = bf16[80,1536]{1,0:T(8,128)(2,1)S(1)} collective-permute-done((bf16[80,1536]{1,0:T(8,128)(2,1)}, bf16[80,1536]{1,0:T(8,128)(2,1)S(1)}, u32[]{:S(2)}, u32[]{:S(2)}) %collective-permute-start.14) | collective-permute-done | bytes 245792 | tf_op jit(solution)/shard_map/ppermute | solution.py:379
  94.0 2.7 %collective-permute-done.18.refs_6_ = bf16[320,1536]{1,0:T(8,128)(2,1)} collective-permute-done((bf16[320,1536]{1,0:T(8,128)(2,1)S(1)}, bf16[320,1536]{1,0:T(8,128)(2,1)}, u32[]{:S(2)}, u32[]{:S(2)}) %collective-permute-start.18) | collective-permute-done | bytes 983072 | tf_op jit(solution)/shard_map/ppermute | solution.py:379
  96.7 18.2 %project_scan.2 = (bf16[768,1280]{1,0:T(8,128)(2,1)}, f32[128,1280]{1,0:T(8,128)}, bf16[128,1280]{1,0:T(8,128)(2,1)}, bf16[768,128]{1,0:T(8,128)(2,1)}, f32[128,...) custom-call(s32[32]{0:T(128)} %broadcast_multiply_fusion.refs_0_, bf16[320,1536]{1,0:T(8,128)(2,1)} %copy-done, ...), custom_call_target="tpu_custom_call" | custom-call | flops 1 | bytes 1 | tf_op jit(solution)/shard_map/project_scan/pallas_call | solution.py:303
  114.9 1.0 slice_select_fusion.2
  115.9 1.7 collective-permute-start.24
  118.2 3.9 %collective-permute-done.24 = bf16[128,640]{1,0:T(8,128)(2,1)S(1)} collective-permute-done((bf16[128,640]{1,0:T(8,128)(2,1)S(1)}, bf16[128,640]{1,0:T(8,128)(2,1)S(1)}, u32[]{:S(2)}, u32[]{:S(2)}) %collective-permute-start.24) | collective-permute-done | bytes 163872 | tf_op jit(solution)/shard_map/ppermute | solution.py:354
  122.2 1.2 fusion.6
  123.3 1.3 collective-permute-start.25
  124.6 1.3 collective-permute-start.26
  125.9 1.5 collective-permute-start.27
  127.5 16.0 %project_scan.3 = (bf16[768,1280]{1,0:T(8,128)(2,1)}, f32[128,1280]{1,0:T(8,128)}, bf16[128,1280]{1,0:T(8,128)(2,1)}) custom-call(s32[1]{0:T(128)} %constant.308.clone.1.refs_0_, bf16[2560,1280]{1,0:T(8,128)(2,1)} %all-gather.2.cloned.1.call-done.refs_1_, bf16[16,2560]{1,0:T(8,128)(2,1)} %copy-done.7, bf16[768,2560]{1,0:T(8,128)(2,1)} %bitcast.52, ...), custom_call_target="tpu_custom_call" | custom-call | flops 1 | bytes 1 | tf_op jit(solution)/shard_map/project_scan/pallas_call | solution.py:303
  143.5 1.1 slice_select_fusion.3
  144.5 1.7 collective-permute-start.19
  146.9 4.8 %collective-permute-done.19 = bf16[128,640]{1,0:T(8,128)(2,1)S(1)} collective-permute-done((bf16[128,640]{1,0:T(8,128)(2,1)S(1)}, bf16[128,640]{1,0:T(8,128)(2,1)S(1)}, u32[]{:S(2)}, u32[]{:S(2)}) %collective-permute-start.19) | collective-permute-done | bytes 163872 | tf_op jit(solution)/shard_map/ppermute | solution.py:354
  151.8 1.3 collective-permute-start.20
  153.1 1.3 collective-permute-start.21
  154.4 1.3 collective-permute-start.22
  156.6 2.7 %collective-permute-done.20 = bf16[128,640]{1,0:T(8,128)(2,1)S(1)} collective-permute-done((bf16[128,640]{1,0:T(8,128)(2,1)S(1)}, bf16[128,640]{1,0:T(8,128)(2,1)S(1)}, u32[]{:S(2)}, u32[]{:S(2)}) %collective-permute-start.20) | collective-permute-done | bytes 163872 | tf_op jit(solution)/shard_map/ppermute | solution.py:354
  159.3 9.2 %collective-permute-done.21 = bf16[128,640]{1,0:T(8,128)(2,1)S(1)} collective-permute-done((bf16[128,640]{1,0:T(8,128)(2,1)S(1)}, bf16[128,640]{1,0:T(8,128)(2,1)S(1)}, u32[]{:S(2)}, u32[]{:S(2)}) %collective-permute-start.21) | collective-permute-done | bytes 163872 | tf_op jit(solution)/shard_map/ppermute | solution.py:354
  168.7 1.3 collective-permute-start.23
  169.9 3.1 %head_norm.3.rest_0_ = bf16[768,2560]{1,0:T(8,128)(2,1)} custom-call(bf16[768,1280]{1,0:T(8,128)(2,1)} %get-tuple-element.84.y_ref, bf16[768,128]{1,0:T(8,128)(2,1)} %get-tuple-element.75.refs_10_.c_ref, bf16[768,2560]{1,0:T(8,128)(2,1)} %get-tuple-element.79.reach_ref, f32[1,2560]{1,0:T(1,128)} %broadcast_in_dim.35.gain_ref, ...), custom_call_target="tpu_custom_call" | custom-call | flops 800000000 | bytes 1966080 | tf_op jit(solution)/shard_map/head_norm/pallas_call | solution.py:336
  173.1 4.4 %head_norm.4.rest_0_ = bf16[768,2560]{1,0:T(8,128)(2,1)} custom-call(bf16[768,1280]{1,0:T(8,128)(2,1)} %get-tuple-element.84.y_ref, bf16[768,128]{1,0:T(8,128)(2,1)} %get-tuple-element.75.refs_10_.c_ref, bf16[768,2560]{1,0:T(8,128)(2,1)} %get-tuple-element.79.reach_ref, f32[1,2560]{1,0:T(1,128)} %broadcast_in_dim.35.gain_ref, ...), custom_call_target="tpu_custom_call", output_to_operand_aliasing={{}: (6, {})} | custom-call | flops 1200000000 | bytes 2949120 | tf_op jit(solution)/shard_map/head_norm/pallas_call | solution.py:336
  178.3 6.2 %head_norm.5 = bf16[768,2560]{1,0:T(8,128)(2,1)} custom-call(bf16[768,1280]{1,0:T(8,128)(2,1)} %get-tuple-element.78.y_ref, bf16[768,128]{1,0:T(8,128)(2,1)} %get-tuple-element.75.refs_10_.c_ref, bf16[768,2560]{1,0:T(8,128)(2,1)} %get-tuple-element.79.reach_ref, f32[1,2560]{1,0:T(1,128)} %broadcast_in_dim.35.gain_ref, ...), custom_call_target="tpu_custom_call", output_to_operand_aliasing={{}: (6, {})} | custom-call | flops 2000000000 | bytes 4915200 | tf_op jit(solution)/shard_map/head_norm/pallas_call | solution.py:336
  (95 shorter events, 14.0 us)
Async XLA Ops:
  6.5 120.9 %all-gather.2.cloned.1.call-start = ((), (), s32[]{:S(2)}) async-start(), calls=%async_computation | async-start | bytes 6758400 | tf_op jit(solution)/shard_map/all_gather | solution.py:470
  8.2 22.2 %copy-start.9 = (f32[40]{0:T(128)S(1)}, f32[40]{0:T(128)}, u32[]{:S(2)}) copy-start(f32[40]{0:T(128)} %param.14) | copy-start | bytes 484
  8.2 22.3 %copy-start.6 = (f32[1,40,768]{2,1,0:T(8,128)S(1)}, f32[1,40,768]{2,1,0:T(8,128)}, u32[]{:S(2)}) copy-start(f32[1,40,768]{2,1,0:T(8,128)} %param.13) | copy-start | bytes 368644
  9.2 12.6 %collective-permute-start.1 = (bf16[80,1536]{1,0:T(8,128)(2,1)S(1)}, bf16[80,1536]{1,0:T(8,128)(2,1)S(1)}, u32[]{:S(2)}, u32[]{:S(2)}) collective-permute-start(bf16[80,1536]{1,0:T(8,128)(2,1)S(1)} %slice.136), channel_id=1, source_target_pairs={{0,2},{1,3},{2,4},{3,5},{4,6},{5,7},{6,0},{7,1},{8,10},{9,11},{10,... | collective-permute-start | bytes 737288 | tf_op jit(solution)/shard_map/ppermute | solution.py:379
  9.3 15.5 %collective-permute-start.2 = (bf16[80,1536]{1,0:T(8,128)(2,1)S(1)}, bf16[80,1536]{1,0:T(8,128)(2,1)S(1)}, u32[]{:S(2)}, u32[]{:S(2)}) collective-permute-start(bf16[80,1536]{1,0:T(8,128)(2,1)S(1)} %slice.136), channel_id=1, source_target_pairs={{0,6},{1,7},{2,0},{3,1},{4,2},{5,3},{6,4},{7,5},{8,14},{9,15},{10,... | collective-permute-start | bytes 737288 | tf_op jit(solution)/shard_map/ppermute | solution.py:379
  11.3 13.5 %collective-permute-start.3 = (bf16[80,1536]{1,0:T(8,128)(2,1)S(1)}, bf16[80,1536]{1,0:T(8,128)(2,1)}, u32[]{:S(2)}, u32[]{:S(2)}) collective-permute-start(bf16[80,1536]{1,0:T(8,128)(2,1)S(1)} %slice.136), channel_id=1, source_target_pairs={{0,16},{1,17},{2,18},{3,19},{4,20},{5,21},{6,22},{7,23},{8,9},{9,8... | collective-permute-start | bytes 737288 | tf_op jit(solution)/shard_map/ppermute | solution.py:379
  12.8 12.0 %collective-permute-start.4 = (bf16[80,1536]{1,0:T(8,128)(2,1)S(1)}, bf16[80,1536]{1,0:T(8,128)(2,1)}, u32[]{:S(2)}, u32[]{:S(2)}) collective-permute-start(bf16[80,1536]{1,0:T(8,128)(2,1)S(1)} %slice.136), channel_id=1, source_target_pairs={{0,1},{1,0},{2,3},{3,2},{4,5},{5,4},{6,7},{7,6},{8,24},{9,25},{10,... | collective-permute-start | bytes 737288 | tf_op jit(solution)/shard_map/ppermute | solution.py:379
  14.3 34.6 %collective-permute-start = (bf16[80,1536]{1,0:T(8,128)(2,1)S(1)}, bf16[80,1536]{1,0:T(8,128)(2,1)}, u32[]{:S(2)}, u32[]{:S(2)}) collective-permute-start(bf16[80,1536]{1,0:T(8,128)(2,1)S(1)} %slice.136), channel_id=1, source_target_pairs={{0,4},{1,5},{2,6},{3,7},{4,0},{5,1},{6,2},{7,3},{8,12},{9,13},{10,... | collective-permute-start | bytes 737288 | tf_op jit(solution)/shard_map/ppermute | solution.py:379
  21.8 11.8 %collective-permute-start.9 = (f32[8,128]{1,0:T(8,128)S(1)}, f32[8,128]{1,0:T(8,128)S(1)}, u32[]{:S(2)}, u32[]{:S(2)}) collective-permute-start(f32[8,128]{1,0:T(8,128)S(1)} %broadcast_in_dim.32), channel_id=1, source_target_pairs={{0,1},{1,0},{2,3},{3,2},{4,5},{5,4},{6,7},{7,6},{8,9},{9,8},{10,11... | collective-permute-start | bytes 12296 | tf_op jit(solution)/shard_map/ppermute | solution.py:354
  26.2 22.6 %collective-permute-start.5 = (bf16[160,1536]{1,0:T(8,128)(2,1)}, bf16[160,1536]{1,0:T(8,128)(2,1)S(1)}, u32[]{:S(2)}, u32[]{:S(2)}) collective-permute-start(bf16[160,1536]{1,0:T(8,128)(2,1)} %get-tuple-element.100), channel_id=1, source_target_pairs={{0,16},{1,17},{2,18},{3,19},{4,20},{5,21},{6,22},{7,23},{8,9},{9,8... | collective-permute-start | bytes 1474568 | tf_op jit(solution)/shard_map/ppermute | solution.py:379
  27.7 21.1 %collective-permute-start.6 = (bf16[160,1536]{1,0:T(8,128)(2,1)}, bf16[160,1536]{1,0:T(8,128)(2,1)S(1)}, u32[]{:S(2)}, u32[]{:S(2)}) collective-permute-start(bf16[160,1536]{1,0:T(8,128)(2,1)} %get-tuple-element.100), channel_id=1, source_target_pairs={{0,1},{1,0},{2,3},{3,2},{4,5},{5,4},{6,7},{7,6},{8,24},{9,25},{10,... | collective-permute-start | bytes 1474568 | tf_op jit(solution)/shard_map/ppermute | solution.py:379
  29.6 19.2 %collective-permute-start.7 = (bf16[80,1536]{1,0:T(8,128)(2,1)}, bf16[80,1536]{1,0:T(8,128)(2,1)}, u32[]{:S(2)}, u32[]{:S(2)}) collective-permute-start(bf16[80,1536]{1,0:T(8,128)(2,1)} %collective-permute-done.3), channel_id=1, source_target_pairs={{0,1},{1,0},{2,3},{3,2},{4,5},{5,4},{6,7},{7,6},{8,24},{9,25},{10,... | collective-permute-start | bytes 737288 | tf_op jit(solution)/shard_map/ppermute | solution.py:379
  33.6 15.2 %collective-permute-start.8 = (bf16[16,2560]{1,0:T(8,128)(2,1)}, bf16[16,2560]{1,0:T(8,128)(2,1)S(1)}, u32[]{:S(2)}, u32[]{:S(2)}) collective-permute-start(bf16[16,2560]{1,0:T(8,128)(2,1)} %slice_bitcast_fusion), channel_id=1, source_target_pairs={{0,1},{1,2},{2,3},{3,4},{4,5},{5,6},{6,7},{8,9},{9,10},{10,11},{11... | collective-permute-start | bytes 245768 | tf_op jit(solution)/shard_map/ppermute | solution.py:443
  48.8 24.9 %copy-start.7 = (bf16[16,2560]{1,0:T(8,128)(2,1)}, bf16[16,2560]{1,0:T(8,128)(2,1)S(1)}, u32[]{:S(2)}) copy-start(bf16[16,2560]{1,0:T(8,128)(2,1)S(1)} %collective-permute-done.8.refs_7_.refs_2_) | copy-start | bytes 245764
  48.9 24.9 %collective-permute-start.10 = (bf16[80,1536]{1,0:T(8,128)(2,1)}, bf16[80,1536]{1,0:T(8,128)(2,1)}, u32[]{:S(2)}, u32[]{:S(2)}) collective-permute-start(bf16[80,1536]{1,0:T(8,128)(2,1)} %collective-permute-done), channel_id=1, source_target_pairs={{0,16},{1,17},{2,18},{3,19},{4,20},{5,21},{6,22},{7,23},{8,9},{9,8... | collective-permute-start | bytes 737288 | tf_op jit(solution)/shard_map/ppermute | solution.py:379
  49.0 24.8 %collective-permute-start.11 = (bf16[80,1536]{1,0:T(8,128)(2,1)}, bf16[80,1536]{1,0:T(8,128)(2,1)}, u32[]{:S(2)}, u32[]{:S(2)}) collective-permute-start(bf16[80,1536]{1,0:T(8,128)(2,1)} %collective-permute-done), channel_id=1, source_target_pairs={{0,1},{1,0},{2,3},{3,2},{4,5},{5,4},{6,7},{7,6},{8,24},{9,25},{10,... | collective-permute-start | bytes 737288 | tf_op jit(solution)/shard_map/ppermute | solution.py:379
  51.2 22.5 %copy-start = (bf16[320,1536]{1,0:T(8,128)(2,1)}, bf16[320,1536]{1,0:T(8,128)(2,1)S(1)}, u32[]{:S(2)}) copy-start(bf16[320,1536]{1,0:T(8,128)(2,1)S(1)} %pad_maximum_fusion.refs_1_) | copy-start | bytes 2949124
  51.2 22.6 %collective-permute-start.13 = (bf16[320,1536]{1,0:T(8,128)(2,1)S(1)}, bf16[320,1536]{1,0:T(8,128)(2,1)S(1)}, u32[]{:S(2)}, u32[]{:S(2)}) collective-permute-start(bf16[320,1536]{1,0:T(8,128)(2,1)S(1)} %pad_maximum_fusion.refs_1_), channel_id=1, source_target_pairs={{0,8},{1,9},{2,10},{3,11},{4,12},{5,13},{6,14},{7,15},{8,0},{9,1},... | collective-permute-start | bytes 2949128 | tf_op jit(solution)/shard_map/ppermute | solution.py:379
  51.3 22.5 %collective-permute-start.12 = (bf16[160,1536]{1,0:T(8,128)(2,1)S(1)}, bf16[160,1536]{1,0:T(8,128)(2,1)S(1)}, u32[]{:S(2)}, u32[]{:S(2)}) collective-permute-start(bf16[160,1536]{1,0:T(8,128)(2,1)S(1)} %collective-permute-done.5), channel_id=1, source_target_pairs={{0,1},{1,0},{2,3},{3,2},{4,5},{5,4},{6,7},{7,6},{8,24},{9,25},{10,... | collective-permute-start | bytes 1474568 | tf_op jit(solution)/shard_map/ppermute | solution.py:379
  73.8 1.0 copy-start.5
  74.9 21.8 %copy-start.3 = (bf16[640,1536]{1,0:T(8,128)(2,1)}, bf16[640,1536]{1,0:T(8,128)(2,1)S(1)}, u32[]{:S(2)}) copy-start(bf16[640,1536]{1,0:T(8,128)(2,1)S(1)} %constant_dynamic-update-slice_fusion.2.refs_2_) | copy-start | bytes 5898244
  74.9 19.0 %collective-permute-start.15 = (bf16[640,1536]{1,0:T(8,128)(2,1)S(1)}, bf16[640,1536]{1,0:T(8,128)(2,1)}, u32[]{:S(2)}, u32[]{:S(2)}) collective-permute-start(bf16[640,1536]{1,0:T(8,128)(2,1)S(1)} %constant_dynamic-update-slice_fusion.2.refs_2_), channel_id=1, source_target_pairs={{0,8},{1,9},{2,10},{3,11},{4,12},{5,13},{6,14},{7,15},{8,0},{9,1},... | collective-permute-start | bytes 5898248 | tf_op jit(solution)/shard_map/ppermute | solution.py:379
  75.0 9.7 %collective-permute-start.16 = (f32[8,128]{1,0:T(8,128)S(1)}, f32[8,128]{1,0:T(8,128)S(1)}, u32[]{:S(2)}, u32[]{:S(2)}) collective-permute-start(f32[8,128]{1,0:T(8,128)S(1)} %broadcast_in_dim.33), channel_id=1, source_target_pairs={{0,2},{1,3},{2,4},{3,5},{4,6},{5,7},{8,10},{9,11},{10,12},{11,13},... | collective-permute-start | bytes 12296 | tf_op jit(solution)/shard_map/ppermute | solution.py:354
  76.3 10.9 %collective-permute-start.17 = (f32[8,128]{1,0:T(8,128)S(1)}, f32[8,128]{1,0:T(8,128)S(1)}, u32[]{:S(2)}, u32[]{:S(2)}) collective-permute-start(f32[8,128]{1,0:T(8,128)S(1)} %broadcast_in_dim.33), channel_id=1, source_target_pairs={{0,4},{1,5},{2,6},{3,7},{8,12},{9,13},{10,14},{11,15},{16,20},{17,... | collective-permute-start | bytes 12296 | tf_op jit(solution)/shard_map/ppermute | solution.py:354
  87.4 6.5 %collective-permute-start.14 = (bf16[80,1536]{1,0:T(8,128)(2,1)}, bf16[80,1536]{1,0:T(8,128)(2,1)S(1)}, u32[]{:S(2)}, u32[]{:S(2)}) collective-permute-start(bf16[80,1536]{1,0:T(8,128)(2,1)} %collective-permute-done.10), channel_id=1, source_target_pairs={{0,1},{1,0},{2,3},{3,2},{4,5},{5,4},{6,7},{7,6},{8,24},{9,25},{10,... | collective-permute-start | bytes 737288 | tf_op jit(solution)/shard_map/ppermute | solution.py:379
  93.9 2.8 %copy-start.4 = (bf16[320,1536]{1,0:T(8,128)(2,1)}, bf16[320,1536]{1,0:T(8,128)(2,1)S(1)}, u32[]{:S(2)}) copy-start(bf16[320,1536]{1,0:T(8,128)(2,1)S(1)} %constant_dynamic-update-slice_fusion.7.refs_3_) | copy-start | bytes 2949124
  93.9 2.8 %collective-permute-start.18 = (bf16[320,1536]{1,0:T(8,128)(2,1)S(1)}, bf16[320,1536]{1,0:T(8,128)(2,1)}, u32[]{:S(2)}, u32[]{:S(2)}) collective-permute-start(bf16[320,1536]{1,0:T(8,128)(2,1)S(1)} %constant_dynamic-update-slice_fusion.7.refs_3_), channel_id=1, source_target_pairs={{0,8},{1,9},{2,10},{3,11},{4,12},{5,13},{6,14},{7,15},{8,0},{9,1},... | collective-permute-start | bytes 2949128 | tf_op jit(solution)/shard_map/ppermute | solution.py:379
  96.7 20.9 %copy-start.8 = (f32[2560]{0:T(1024)S(1)}, f32[2560]{0:T(1024)}, u32[]{:S(2)}) copy-start(f32[2560]{0:T(1024)} %param.15) | copy-start | bytes 30724
  115.9 6.3 %collective-permute-start.24 = (bf16[128,640]{1,0:T(8,128)(2,1)S(1)}, bf16[128,640]{1,0:T(8,128)(2,1)S(1)}, u32[]{:S(2)}, u32[]{:S(2)}) collective-permute-start(bf16[128,640]{1,0:T(8,128)(2,1)S(1)} %slice_select_fusion.2), channel_id=1, source_target_pairs={{0,1},{1,0},{2,3},{3,2},{4,5},{5,4},{6,7},{7,6},{8,9},{9,8},{10,11... | collective-permute-start | bytes 491528 | tf_op jit(solution)/shard_map/ppermute | solution.py:354
  123.3 22.9 %collective-permute-start.25 = (bf16[128,640]{1,0:T(8,128)(2,1)S(1)}, bf16[128,640]{1,0:T(8,128)(2,1)S(1)}, u32[]{:S(2)}, u32[]{:S(2)}) collective-permute-start(bf16[128,640]{1,0:T(8,128)(2,1)S(1)} %fusion.6), channel_id=1, source_target_pairs={{0,2},{1,3},{2,4},{3,5},{4,6},{5,7},{8,10},{9,11},{10,12},{11,13},... | collective-permute-start | bytes 491528 | tf_op jit(solution)/shard_map/ppermute | solution.py:354
  124.6 21.6 %collective-permute-start.26 = (bf16[128,640]{1,0:T(8,128)(2,1)S(1)}, bf16[128,640]{1,0:T(8,128)(2,1)S(1)}, u32[]{:S(2)}, u32[]{:S(2)}) collective-permute-start(bf16[128,640]{1,0:T(8,128)(2,1)S(1)} %fusion.6), channel_id=1, source_target_pairs={{0,4},{1,5},{2,6},{3,7},{8,12},{9,13},{10,14},{11,15},{16,20},{17,... | collective-permute-start | bytes 491528 | tf_op jit(solution)/shard_map/ppermute | solution.py:354
  125.9 20.3 %collective-permute-start.27 = (bf16[128,640]{1,0:T(8,128)(2,1)S(1)}, bf16[128,640]{1,0:T(8,128)(2,1)S(1)}, u32[]{:S(2)}, u32[]{:S(2)}) collective-permute-start(bf16[128,640]{1,0:T(8,128)(2,1)S(1)} %fusion.6), channel_id=1, source_target_pairs={{0,6},{1,7},{8,14},{9,15},{16,22},{17,23},{24,30},{25,31}} | collective-permute-start | bytes 491528 | tf_op jit(solution)/shard_map/ppermute | solution.py:354
  127.5 18.7 %copy-start.2 = (f32[128,1280]{1,0:T(8,128)S(1)}, f32[128,1280]{1,0:T(8,128)}, u32[]{:S(2)}) copy-start(f32[128,1280]{1,0:T(8,128)} %get-tuple-element.85) | copy-start | bytes 1966084
  143.5 8.3 %copy-start.1 = (f32[128,1280]{1,0:T(8,128)S(1)}, f32[128,1280]{1,0:T(8,128)}, u32[]{:S(2)}) copy-start(f32[128,1280]{1,0:T(8,128)} %get-tuple-element.81) | copy-start | bytes 1966084
  144.5 7.2 %collective-permute-start.19 = (bf16[128,640]{1,0:T(8,128)(2,1)S(1)}, bf16[128,640]{1,0:T(8,128)(2,1)S(1)}, u32[]{:S(2)}, u32[]{:S(2)}) collective-permute-start(bf16[128,640]{1,0:T(8,128)(2,1)S(1)} %slice_select_fusion.3), channel_id=1, source_target_pairs={{0,1},{1,0},{2,3},{3,2},{4,5},{5,4},{6,7},{7,6},{8,9},{9,8},{10,11... | collective-permute-start | bytes 491528 | tf_op jit(solution)/shard_map/ppermute | solution.py:354
  146.4 9.3 %collective-permute-start.28 = (bf16[128,640]{1,0:T(8,128)(2,1)S(1)}, bf16[128,640]{1,0:T(8,128)(2,1)S(1)}, u32[]{:S(2)}, u32[]{:S(2)}) collective-permute-start(bf16[128,640]{1,0:T(8,128)(2,1)S(1)} %get-tuple-element.95), channel_id=1, source_target_pairs={{0,1},{1,0},{2,3},{3,2},{4,5},{5,4},{6,7},{7,6},{8,9},{9,8},{10,11... | collective-permute-start | bytes 491528 | tf_op jit(solution)/shard_map/ppermute | solution.py:354
  151.8 7.4 %collective-permute-start.20 = (bf16[128,640]{1,0:T(8,128)(2,1)S(1)}, bf16[128,640]{1,0:T(8,128)(2,1)S(1)}, u32[]{:S(2)}, u32[]{:S(2)}) collective-permute-start(bf16[128,640]{1,0:T(8,128)(2,1)S(1)} %fusion.2), channel_id=1, source_target_pairs={{0,2},{1,3},{2,4},{3,5},{4,6},{5,7},{8,10},{9,11},{10,12},{11,13},... | collective-permute-start | bytes 491528 | tf_op jit(solution)/shard_map/ppermute | solution.py:354
  153.1 15.3 %collective-permute-start.21 = (bf16[128,640]{1,0:T(8,128)(2,1)S(1)}, bf16[128,640]{1,0:T(8,128)(2,1)S(1)}, u32[]{:S(2)}, u32[]{:S(2)}) collective-permute-start(bf16[128,640]{1,0:T(8,128)(2,1)S(1)} %fusion.2), channel_id=1, source_target_pairs={{0,4},{1,5},{2,6},{3,7},{8,12},{9,13},{10,14},{11,15},{16,20},{17,... | collective-permute-start | bytes 491528 | tf_op jit(solution)/shard_map/ppermute | solution.py:354
  154.4 14.0 %collective-permute-start.22 = (bf16[128,640]{1,0:T(8,128)(2,1)S(1)}, bf16[128,640]{1,0:T(8,128)(2,1)S(1)}, u32[]{:S(2)}, u32[]{:S(2)}) collective-permute-start(bf16[128,640]{1,0:T(8,128)(2,1)S(1)} %fusion.2), channel_id=1, source_target_pairs={{0,6},{1,7},{8,14},{9,15},{16,22},{17,23},{24,30},{25,31}} | collective-permute-start | bytes 491528 | tf_op jit(solution)/shard_map/ppermute | solution.py:354
  168.7 8.9 %collective-permute-start.23 = (bf16[128,640]{1,0:T(8,128)(2,1)S(1)}, bf16[128,640]{1,0:T(8,128)(2,1)S(1)}, u32[]{:S(2)}, u32[]{:S(2)}) collective-permute-start(bf16[128,640]{1,0:T(8,128)(2,1)S(1)} %get-tuple-element.97), channel_id=1, source_target_pairs={{0,1},{1,0},{2,3},{3,2},{4,5},{5,4},{6,7},{7,6},{8,9},{9,8},{10,11... | collective-permute-start | bytes 491528 | tf_op jit(solution)/shard_map/ppermute | solution.py:354
Sparse Core Ops, SparseCore 0:
  10.3 79.9 all-gather.1

commit v4 on v3

--- a/solution.py
+++ b/solution.py
@@ -11,6 +11,7 @@
 TILE = 256
 RIM = 16
 VMEM = 56 * 1024 * 1024
+SMALL = 16 * 1024 * 1024
 LOG2E = math.log2(math.e)
 BF16 = jnp.bfloat16
 F32 = jnp.float32
@@ -48,21 +49,38 @@
     return row
 
 
-def decay_kernel(raw_ref, rate_ref, decay_ref, grow_ref, reach_ref, tails_ref):
+def decay_kernel(raw_ref, rate_ref, decay_ref, grow_ref, reach_ref, tails_ref, steps_ref, rows_ref, tail_ref, cols_ref):
     pairs = TILE // SPAN
     heads = 2 * pairs
-    count = raw_ref.shape[1]
+    tiles = cols_ref.shape[0]
+    count = raw_ref.shape[0] // tiles
     blocks = count // heads
-    raw = raw_ref[0]
-    steps = jnp.maximum(raw, 0.0) + jnp.log1p(jnp.exp(-jnp.abs(raw)))
-    rows = running_sum(rate_ref[0] * steps)
-    totals = rows[:, SPAN - 1 :]
-    tails = jnp.exp2(jnp.minimum(totals - rows, 0.0)) * steps
-    before = [jnp.zeros((heads, 1), F32)]
-    for block in range(blocks - 1):
-        before.append(before[-1] + totals[block * heads : (block + 1) * heads])
-    padding = jnp.zeros((SPAN - 2 * count, SPAN), F32)
-    cols = jnp.concatenate([rows, rows + jnp.concatenate(before, axis=0), padding], axis=0).T
+    tile = pl.program_id(0)
+
+    @pl.when(tile == 0)
+    def _():
+        raw = raw_ref[...]
+        steps = jnp.maximum(raw, 0.0) + jnp.log1p(jnp.exp(-jnp.abs(raw)))
+        rows = running_sum(rate_ref[...] * steps)
+        totals = jnp.broadcast_to(rows[:, SPAN - 1 :], rows.shape)
+        steps_ref[...] = steps
+        rows_ref[...] = rows
+        tail_ref[...] = jnp.exp2(jnp.minimum(totals - rows, 0.0)) * steps
+        block = lax.rem(lax.broadcasted_iota(jnp.int32, rows.shape, 0), count) // heads
+        before = jnp.where(block >= 1, pltpu.roll(totals, heads, 0), 0.0)
+        by = 1
+        while by < blocks:
+            before = before + jnp.where(block >= by, pltpu.roll(before, by * heads, 0), 0.0)
+            by *= 2
+        full = rows + before
+        padding = jnp.zeros((SPAN - 2 * count, SPAN), F32)
+        for each in range(tiles):
+            mine = slice(each * count, (each + 1) * count)
+            cols_ref[each] = jnp.concatenate([rows[mine], full[mine], padding], axis=0).T
+
+    mine = pl.ds(pl.multiple_of(tile * count, 8), count)
+    cols = cols_ref[tile]
+    rows, steps, tails = rows_ref[mine, :], steps_ref[mine, :], tail_ref[mine, :]
     for block in range(blocks):
         here = pl.ds(block * SPAN, SPAN)
         for pair in range(pairs):
@@ -75,9 +93,9 @@
                 decay_ref[0, pair, here, pl.ds(head * SPAN, SPAN)] = decay.astype(BF16)
                 row = block * pairs + pair
                 tails_ref[0, row : row + 1, pl.ds(head * SPAN, SPAN)] = tails[at : at + 1]
-            grow_ref[here, lanes] = jnp.exp2(halves(*cums)).astype(BF16)
+            grow_ref[0, here, lanes] = jnp.exp2(halves(*cums)).astype(BF16)
             reach = halves(spread(cols, count + first), spread(cols, count + first + 1))
-            reach_ref[here, lanes] = jnp.exp2(reach).astype(BF16)
+            reach_ref[0, here, lanes] = jnp.exp2(reach).astype(BF16)
 
 
 def scores_of(taps_ref, c_ref, bt_ref, scores_ref, rows_ref):
@@ -94,7 +112,7 @@
         scores_ref[block] = jnp.concatenate([scores, scores], axis=1)
 
 
-def scan_tile(taps_ref, c_ref, bt_ref, scores_ref, decay_ref, grow_ref, tails_ref, lanes_ref, y_ref, state_ref, sent_ref, rows_ref):
+def scan_tile(taps_ref, c_ref, bt_ref, scores_ref, decay_ref, grow_ref, tails_ref, lanes_ref, y_ref, state_ref, sent_ref, rows_ref, upper, extra_ref):
     blocks = scores_ref.shape[0]
     pairs = TILE // SPAN
     states = [None] * pairs
@@ -114,21 +132,34 @@
             y, state = out[:SPAN], out[SPAN:]
             if block > 0:
                 carried = jnp.dot(c_ref[here, :], states[pair].astype(BF16), preferred_element_type=F32)
-                y = y + grow_ref[here, lanes].astype(F32) * carried
+                y = y + grow_ref[0, here, lanes].astype(F32) * carried
                 state = lanes_ref[0, block : block + 1, lanes] * states[pair] + state
-            y_ref[here, lanes] = (y + lanes_ref[0, blocks : blocks + 1, lanes] * x).astype(BF16)
+            y_ref[0, here, lanes] = (y + lanes_ref[0, blocks : blocks + 1, lanes] * x).astype(BF16)
             states[pair] = state
     for pair in range(pairs):
-        state_ref[:, pl.ds(pair * SPAN, SPAN)] = states[pair]
-        sent_ref[:, pl.ds(pair * SPAN, SPAN)] = states[pair].astype(BF16)
-
-
-def scan_kernel(leads, tiles, piece_count, lead_at, base, *refs):
-    offsets = refs[0]
+        lanes = pl.ds(pair * SPAN, SPAN)
+        if upper is None:
+            state_ref[:, lanes] = states[pair]
+            sent_ref[:, lanes] = states[pair].astype(BF16)
+            continue
+        half = SPAN // 2
+        low, high = states[pair][:half], states[pair][half:]
+        state_ref[:, lanes] = jnp.where(upper, high, low)
+        sent_ref[:half, lanes] = jnp.where(upper, low, high).astype(BF16)
+    if extra_ref is not None:
+        sent_ref[SPAN // 2 :, :] = extra_ref[...]
+
+
+def scan_kernel(leads, extras, tiles, piece_count, lead_at, base, *refs):
+    offsets, place = refs[:2]
+    refs = refs[1:]
     pieces = refs[1 : 1 + piece_count]
     rim_ref, tokens_ref, taps_ref, decay_ref, grow_ref, tails_ref, lanes_ref, taps_bc_ref = refs[1 + piece_count : 9 + piece_count]
     rest = refs[9 + piece_count : -6]
     tok_ref, w_a, w_b, rows_a, rows_b, sems = refs[-6:]
+    extra_ref = None
+    if extras:
+        extra_ref, *rest = rest
     if leads:
         y_ref, state_ref, sent_ref, c_ref, bt_ref, scores_ref = rest
     else:
@@ -138,19 +169,16 @@
     w_refs, rows_refs = (w_a, w_b), (rows_a, rows_b)
 
     def fetch(item, slot):
-        column = (item - leads + base) * TILE
+        tile = item - leads + base
         if leads:
-            column = jnp.where(item == 0, lead_at, column)
-        column = pl.multiple_of(column, TILE)
+            tile = jnp.where(item == 0, lead_at, tile)
         index = 0
-        rows = w_a.shape[0] // offsets.shape[0]
         for piece in pieces:
-            for part in range(piece.shape[0] // rows):
+            rows = piece.shape[2]
+            for part in range(piece.shape[0]):
                 target = pl.multiple_of(offsets[index], 16)
                 pltpu.make_async_copy(
-                    piece.at[pl.ds(part * rows, rows), pl.ds(column, TILE)],
-                    w_refs[slot].at[pl.ds(target, rows)],
-                    sems.at[slot],
+                    piece.at[part, tile], w_refs[slot].at[pl.ds(target, rows)], sems.at[slot]
                 ).start()
                 index += 1
 
@@ -162,7 +190,9 @@
 
     def finish(slot):
         scan_tile(
-            taps_ref, c_ref, bt_ref, scores_ref, decay_ref, grow_ref, tails_ref, lanes_ref, y_ref, state_ref, sent_ref, rows_refs[slot]
+            taps_ref, c_ref, bt_ref, scores_ref, decay_ref, grow_ref, tails_ref, lanes_ref, y_ref, state_ref, sent_ref, rows_refs[slot],
+            place[0] == 1 if state_ref.shape[0] < SPAN else None,
+            extra_ref,
         )
 
     def lead(slot):
@@ -213,10 +243,16 @@
         finish((items - 1) % 2)
 
 
-def norm_kernel(y_ref, c_ref, reach_ref, gain_ref, gather_ref, state_ref, *rest):
+def norm_kernel(count, place_ref, y_ref, c_ref, reach_ref, gain_ref, gather_ref, *rest):
     out_ref = rest[-1]
-    carried = jnp.dot(c_ref[...], state_ref[...], preferred_element_type=F32)
-    ssd = y_ref[...].astype(F32) + reach_ref[...].astype(F32) * carried
+    state = rest[0][...]
+    if count == 2:
+        ours, theirs = state, rest[1][...]
+        upper = place_ref[0] == 1
+        low, high = jnp.where(upper, theirs, ours), jnp.where(upper, ours, theirs)
+        state = jnp.concatenate([low, high], axis=0)
+    carried = jnp.dot(c_ref[...], state, preferred_element_type=F32)
+    ssd = y_ref[0].astype(F32) + reach_ref[0].astype(F32) * carried
     mean = jnp.dot((ssd * ssd).astype(BF16), gather_ref[...], preferred_element_type=F32)
     out_ref[...] = (ssd * lax.rsqrt(mean + 1e-05) * gain_ref[...]).astype(BF16)
 
@@ -225,13 +261,14 @@
     return pl.BlockSpec(shape, lambda *_: (0,) * len(shape))
 
 
-def params():
-    return pltpu.CompilerParams(vmem_limit_bytes=VMEM)
+def params(limit=VMEM):
+    return pltpu.CompilerParams(vmem_limit_bytes=limit)
 
 
 def run_decay(raw, rate):
     tiles, count = raw.shape[:2]
     pairs = TILE // SPAN
+    table = pltpu.VMEM((tiles * count, SPAN), F32)
     tok_count = count // (2 * pairs) * SPAN
     rounds = pairs * tok_count // SPAN
     tail_rows = rounds + -rounds % 8
@@ -239,54 +276,57 @@
         decay_kernel,
         grid=(tiles,),
         in_specs=[
-            pl.BlockSpec((1, count, SPAN), lambda i: (i, 0, 0)),
-            pl.BlockSpec((1, count, 1), lambda i: (i, 0, 0)),
+            whole((tiles * count, SPAN)),
+            whole((tiles * count, 1)),
         ],
         out_specs=[
             pl.BlockSpec((1, pairs, tok_count, 2 * SPAN), lambda i: (i, 0, 0, 0)),
-            pl.BlockSpec((tok_count, TILE), lambda i: (0, i)),
-            pl.BlockSpec((tok_count, TILE), lambda i: (0, i)),
+            pl.BlockSpec((1, tok_count, TILE), lambda i: (i, 0, 0)),
+            pl.BlockSpec((1, tok_count, TILE), lambda i: (i, 0, 0)),
             pl.BlockSpec((1, tail_rows, 2 * SPAN), lambda i: (i, 0, 0)),
         ],
         out_shape=[
             jax.ShapeDtypeStruct((tiles, pairs, tok_count, 2 * SPAN), BF16),
-            jax.ShapeDtypeStruct((tok_count, tiles * TILE), BF16),
-            jax.ShapeDtypeStruct((tok_count, tiles * TILE), BF16),
+            jax.ShapeDtypeStruct((tiles, tok_count, TILE), BF16),
+            jax.ShapeDtypeStruct((tiles, tok_count, TILE), BF16),
             jax.ShapeDtypeStruct((tiles, tail_rows, 2 * SPAN), F32),
         ],
+        scratch_shapes=[table, table, table, pltpu.VMEM((tiles, SPAN, SPAN), F32)],
         compiler_params=params(),
         cost_estimate=pl.CostEstimate(flops=10_000_000_000, bytes_accessed=16_000_000, transcendentals=0),
         name="decays",
-    )(raw, rate)
-
-
-def run_scan(pieces, offsets, lead_at, base, rim, tokens, taps, shared, decay, grow, tails, lanes, first, tiles):
+    )(raw.reshape(tiles * count, SPAN), rate.reshape(tiles * count, 1))
+
+
+def run_scan(pieces, offsets, place, lead_at, base, rim, tokens, taps, shared, decay, grow, tails, lanes, first, tiles, extra=None):
     tok_count, depth = tokens.shape
     rows = tok_count + RIM
     blocks = tok_count // SPAN
     leads = 1 if shared is None else 0
     behind = lambda i: jnp.clip(i - 1 - leads, 0, tiles - 1)
     per_tile = lambda array: pl.BlockSpec((1,) + array.shape[1:], lambda i: (behind(i) + first, 0, 0))
-    ins = [offsets, *pieces, rim, tokens, taps, decay, grow, tails, lanes, taps]
-    specs = [pl.BlockSpec(memory_space=pltpu.SMEM)]
+    held = SPAN // 2 if place is not None else SPAN
+    place = jnp.zeros((1,), jnp.int32) if place is None else place
+    ins = [offsets, place, *pieces, rim, tokens, taps, decay, grow, tails, lanes, taps]
+    specs = [pl.BlockSpec(memory_space=pltpu.SMEM)] * 2
     specs += [pl.BlockSpec(memory_space=pl.ANY)] * (len(pieces) + 2)
     specs += [
         pl.BlockSpec((8, TILE), lambda i: (0, behind(i) + first)),
         pl.BlockSpec((1,) + decay.shape[1:], lambda i: (behind(i) + first, 0, 0, 0)),
-        pl.BlockSpec((tok_count, TILE), lambda i: (0, behind(i) + first)),
+        per_tile(grow),
         per_tile(tails),
         per_tile(lanes),
         pl.BlockSpec((8, TILE), lambda i: (0, taps.shape[1] // TILE - 1)),
     ]
     out_shape = [
-        jax.ShapeDtypeStruct((tok_count, tiles * TILE), BF16),
-        jax.ShapeDtypeStruct((SPAN, tiles * TILE), F32),
-        jax.ShapeDtypeStruct((SPAN, tiles * TILE), BF16),
+        jax.ShapeDtypeStruct((tiles, tok_count, TILE), BF16),
+        jax.ShapeDtypeStruct((held, tiles * TILE), F32),
+        jax.ShapeDtypeStruct((held + (0 if extra is None else extra.shape[0]), tiles * TILE), BF16),
     ]
     out_specs = [
-        pl.BlockSpec((tok_count, TILE), lambda i: (0, behind(i))),
-        pl.BlockSpec((SPAN, TILE), lambda i: (0, behind(i))),
-        pl.BlockSpec((SPAN, TILE), lambda i: (0, behind(i))),
+        pl.BlockSpec((1, tok_count, TILE), lambda i: (behind(i), 0, 0)),
+        pl.BlockSpec((held, TILE), lambda i: (0, behind(i))),
+        pl.BlockSpec((out_shape[2].shape[0], TILE), lambda i: (0, behind(i))),
     ]
     shared_shape = [
         jax.ShapeDtypeStruct((tok_count, SPAN), BF16),
@@ -294,6 +334,10 @@
         jax.ShapeDtypeStruct((blocks, SPAN, 2 * SPAN), BF16),
     ]
     shared_specs = [whole(each.shape) for each in shared_shape]
+    extras = 0 if extra is None else extra.shape[0]
+    if extras:
+        ins.append(extra)
+        specs.append(pl.BlockSpec((extras, TILE), lambda i: (0, behind(i))))
     if leads:
         out_shape += shared_shape
         out_specs += shared_specs
@@ -301,7 +345,7 @@
         ins += shared
         specs += shared_specs
     outs = pl.pallas_call(
-        lambda *refs: scan_kernel(leads, tiles, len(pieces), lead_at, base, *refs),
+        lambda *refs: scan_kernel(leads, extras, tiles, len(pieces), lead_at, base, *refs),
         grid=(tiles + leads + 1,),
         in_specs=specs,
         out_specs=out_specs,
@@ -311,36 +355,37 @@
         + [pltpu.VMEM((rows, TILE), F32)] * 2
         + [pltpu.SemaphoreType.DMA((4,))],
         compiler_params=params(),
-        cost_estimate=pl.CostEstimate(flops=1, bytes_accessed=1, transcendentals=0),
+        cost_estimate=pl.CostEstimate(flops=3_000_000_000 * tiles, bytes_accessed=3_000_000 * tiles, transcendentals=0),
         name="project_scan",
     )(*ins)
     return *outs[:3], (list(outs[3:]) if leads else shared)
 
 
-def run_norm(out, y, c_rows, reach, gain, gather, state, first, base, tiles, width):
+def run_norm(out, place, y, c_rows, reach, gain, gather, state, first, base, tiles, width):
     tok_count = c_rows.shape[0]
-    ins = [y, c_rows, reach, gain, gather, state]
+    ins = [place, y, c_rows, reach, gain, gather, *state]
     specs = [
-        pl.BlockSpec((tok_count, TILE), lambda i: (0, i + base)),
+        pl.BlockSpec(memory_space=pltpu.SMEM),
+        pl.BlockSpec((1, tok_count, TILE), lambda i: (i + base, 0, 0)),
         whole(c_rows.shape),
-        pl.BlockSpec((tok_count, TILE), lambda i: (0, i + first)),
+        pl.BlockSpec((1, tok_count, TILE), lambda i: (i + first, 0, 0)),
         pl.BlockSpec((1, TILE), lambda i: (0, i + first)),
         whole(gather.shape),
-        pl.BlockSpec((SPAN, TILE), lambda i: (0, i + base)),
     ]
+    specs += [pl.BlockSpec((part.shape[0], TILE), lambda i: (0, i + base)) for part in state]
     aliases = {}
     if out is not None:
         aliases = {len(ins): 0}
         ins.append(out)
         specs.append(pl.BlockSpec(memory_space=pl.ANY))
     return pl.pallas_call(
-        norm_kernel,
+        lambda *refs: norm_kernel(len(state), *refs),
         grid=(tiles,),
         in_specs=specs,
         out_specs=pl.BlockSpec((tok_count, TILE), lambda i: (0, i + first)),
         out_shape=jax.ShapeDtypeStruct((tok_count, width), BF16),
         input_output_aliases=aliases,
-        compiler_params=params(),
+        compiler_params=params(SMALL),
         cost_estimate=pl.CostEstimate(flops=400_000_000 * tiles, bytes_accessed=5 * tok_count * TILE * tiles, transcendentals=0),
         name="head_norm",
     )(*ins)
@@ -390,8 +435,10 @@
     def sibling(self, value):
         return self.send(value, lambda x, core, z, y: (x, 1 - core, z, y))
 
-    def gather(self, own, early, decays, last):
-        z1, z3, own_1, own_2 = together(self.along_z(own, 1), self.along_z(own, 3), self.first(own), self.second(own))
+    def gather(self, own, early, decays):
+        z1, z3, own_1, own_2, own = together(
+            self.along_z(own, 1), self.along_z(own, 3), self.first(own), self.second(own), own
+        )
         near = stack(z1, z3)
         z2, near_1, near_2, own_12, *early = together(
             self.along_z(own, 2), self.first(near), self.second(near), self.second(own_1), *early
@@ -401,9 +448,9 @@
             self.first(z2), self.second(z2), self.second(near_1), self.sibling(mine), *decays(early)
         )
         beside = stack(near, near_1, near_2, near_12)
-        far_12, beside_other, *last = together(self.second(far_1), self.sibling(beside), *last(early))
-        far = stack(z2, far_1, far_2, far_12)
-        return [mine, beside, far, mine_other, beside_other, self.sibling(far)], early, decays, last
+        far = stack(z2, far_1, far_2)
+        far_12, beside_other, far_other = together(self.second(far_1), self.sibling(beside), self.sibling(far))
+        return [mine, beside, far, far_12, mine_other, beside_other, far_other, self.sibling(far_12)], early, decays
 
     def owners(self):
         dp, seq = lax.axis_index("dp"), lax.axis_index("seq")
@@ -440,7 +487,8 @@
     y_count = seq_count // z_count
     y_mine = lax.rem(lax.axis_index("seq"), y_count)
 
-    rim = lax.ppermute(token_rows[tok_count - RIM :], "seq", [(i, i + 1) for i in range(seq_count - 1)])
+    after = lambda rows: lax.ppermute(rows, "seq", [(i, i + 1) for i in range(seq_count - 1)])
+    rim_rows = token_rows[tok_count - RIM :]
     taps = jnp.concatenate([conv_weight, conv_bias[None], jnp.zeros((3, channels), F32)], axis=0)
     rate = -LOG2E * jnp.exp(a_log)
     totals = rate[:, None] * jnp.sum(jax.nn.softplus(dt_in[0]).reshape(heads, blocks, SPAN), axis=2)
@@ -467,8 +515,6 @@
             reach.append(reach[-1] + decay)
         return reach[1:]
 
-    gathered = lambda rows: lax.all_gather(rows, ("dp", "seq"), axis=0, tiled=True)
-    whole_rows = jnp.zeros((1,), jnp.int32)
     by_block = lambda rows: rows.reshape(tiles, per_tile, blocks, -1).swapaxes(1, 2).reshape(tiles, blocks * per_tile, -1)
     raw = by_block(dt_in[0])
     rates = by_block(jnp.broadcast_to(rate[:, None], (heads, blocks)))
@@ -476,55 +522,71 @@
     if lax.axis_size("dp") == 4 and seq_count == 8:
         split = tiles // 2
         links = Links(z_count, y_count)
-        late_w = gathered(w_xbc[:, : split * TILE])
-        early_rows = links.owners() * w_xbc.shape[0]
-
-        def coefs(y_decay):
-            pair = [jnp.where(y_mine == 0, y_decay[k], y_decay[1 - k]) for k in (0, 1)]
-            rows = jnp.stack(pair + z_weights(along_z(y_decay)))
-            return [expand(jnp.exp2(rows), head_size)]
-
-        early_w, prepared, (decay, grow, reach, tails), (weights,) = links.gather(
-            w_xbc[:, split * TILE :],
-            (rim, taps, lanes, gather, early_rows, raw, rates, *along_y(totals)),
-            lambda ready: run_decay(*ready[5:7]),
-            lambda ready: coefs(ready[7:]),
+        row_count = w_xbc.shape[0]
+        by_column = w_xbc.reshape(row_count, channels // TILE, TILE).swapaxes(0, 1)[None]
+        late_w = lax.all_gather(by_column[:, :split], ("dp", "seq"), axis=0, tiled=True)
+        late_rows = jnp.arange(lax.axis_size("dp") * seq_count, dtype=jnp.int32) * row_count
+        early_rows = links.owners() * row_count
+
+        kept = expand(jnp.exp2(jnp.sum(totals, axis=1)), head_size)
+        wide = (tiles - split) * TILE
+        rest = jnp.pad(kept[: split * TILE], (0, -(split * TILE) % wide)).reshape(-1, wide)
+        own_kept = jnp.concatenate([kept[None, split * TILE :], rest], axis=0)
+        extra = jnp.pad(own_kept, ((0, 16 - own_kept.shape[0]), (0, 0))).astype(BF16)
+
+        early_w, prepared, (decay, grow, reach, tails) = links.gather(
+            by_column[:, split:],
+            (taps, lanes, gather, early_rows, late_rows, after(rim_rows), own_kept, extra, raw, rates),
+            lambda ready: run_decay(*ready[8:]),
         )
-        rim, taps, lanes, gather, early_rows = prepared[:5]
-        calls = [(early_w, early_rows, split, 0, tiles - split), ([late_w], whole_rows, 0, 0, split)]
-        lead_at = (tiles - split) * TILE
-
-        def incoming(own, sent, lane):
-            e0, e1, z2, z3 = weights[:, lane]
-            half = own.shape[1] // 2
-            upper = y_mine == 1
-            of_mine = lambda value: jnp.where(upper, value[..., half:], value[..., :half])
-            of_other = lambda value: jnp.where(upper, value[..., :half], value[..., half:])
-            swap = lambda value: shifted(value, 0, 1, z_count, y_count)
-            mine = of_mine(own)
-            other = swap(of_other(sent)).astype(F32)
-            e0, e1, z2, z3 = (of_mine(row) for row in (e0, e1, z2, z3))
-            plane = jnp.where(upper, mine + e1 * other, e1 * mine + other).astype(BF16)
-            below = [shifted(plane, k, 0, z_count, y_count).astype(F32) for k in range(1, z_count)]
-            base = below[0] + z2 * below[1] + z3 * below[2]
-            above = e0 * base + jnp.where(upper, other, mine)
+        taps, lanes, gather, early_rows, late_rows, rim, own_kept, extra = prepared[:8]
+        calls = [(early_w, early_rows, split, 0, tiles - split), ([late_w], late_rows, 0, 0, split)]
+        lead_at = tiles - split
+        halved = y_mine.astype(jnp.int32)[None]
+
+        upper = y_mine == 1
+        swap = lambda value: shifted(value, 0, 1, z_count, y_count)
+
+        half = SPAN // 2
+
+        def plane_of(own, other, upper_kept, rows=None):
+            other = other[:half].astype(F32)
+            plane = jnp.where(upper, own + upper_kept * other, upper_kept * own + other)
+            if rows is not None:
+                plane = jnp.concatenate([plane, jnp.pad(rows, ((0, 16 - rows.shape[0]), (0, 0)))], axis=0)
+            plane = plane.astype(BF16)
+            return [shifted(plane, k, 0, z_count, y_count) for k in range(1, z_count)]
+
+        def halves_of(own, other, below, lower_kept, z_kept):
+            base = below[0][:half].astype(F32)
+            through = 1.0
+            for kept, part in zip(z_kept, below[1:]):
+                through = through * kept
+                base = base + through * part[:half].astype(F32)
+            above = lower_kept * base + jnp.where(upper, other[:half].astype(F32), own)
             theirs = swap(jnp.where(upper, base, above).astype(BF16))
-            ours = jnp.where(upper, above, base).astype(BF16)
-            return jnp.where(upper, jnp.concatenate([theirs, ours], axis=1), jnp.concatenate([ours, theirs], axis=1))
+            return [jnp.where(upper, above, base).astype(BF16), theirs]
 
     else:
-        full = gathered(w_xbc)
-        calls = [([full], whole_rows, first, first, min(5, tiles - first)) for first in range(0, tiles, 5)]
-        lead_at = tiles * TILE
+        full = lax.all_gather(w_xbc, ("dp", "seq"), axis=0, tiled=True)
+        full = full.reshape(full.shape[0], channels // TILE, TILE).swapaxes(0, 1)[None]
+        first_row = jnp.zeros((1,), jnp.int32)
+        calls = [([full], first_row, first, first, min(5, tiles - first)) for first in range(0, tiles, 5)]
+        lead_at = tiles
+        rim = after(rim_rows)
+        halved = None
         decay, grow, reach, tails = run_decay(raw, rates)
         y_decay = along_y(totals)
         z_reach = z_weights(along_z(y_decay))
 
-        def incoming(own, sent, lane):
+        def beside(sent):
+            return [shifted(sent, 0, k, z_count, y_count) for k in range(1, y_count)]
+
+        def incoming(own, parts, lane):
             place = [lax.rem(y_mine - k + y_count, y_count) for k in range(y_count)]
             spread_lanes = lambda row: expand(row, head_size)[lane]
             inner = lambda keep: sum(jnp.where(keep(m), y_decay[m], 0.0) for m in range(y_count))
-            parts = [own] + [shifted(sent, 0, k, z_count, y_count).astype(F32) for k in range(1, y_count)]
+            parts = [own] + [part.astype(F32) for part in parts]
             plane, above = 0.0, 0.0
             for k, part in enumerate(parts):
                 after = inner(lambda m: place[m] > place[k])
@@ -536,24 +598,52 @@
             for k in range(1, z_count):
                 along = inside if k == 1 else inside + z_reach[k - 2]
                 above = above + spread_lanes(jnp.exp2(along)) * shifted(plane, k, 0, z_count, y_count).astype(F32)
-            return above.astype(BF16)
-
-    shared = None
-    pending = []
-    for pieces, places, first, base, count in calls:
-        y, own, sent, shared = run_scan(
-            pieces, places, lead_at, base, rim, token_rows, taps, shared, decay, grow, tails, lanes, first, count
+            return [above.astype(BF16)]
+
+    def scan(call, shared, extra=None):
+        pieces, places, first, base, count = call
+        return run_scan(
+            pieces, places, halved, lead_at, base, rim, token_rows, taps, shared, decay, grow, tails, lanes, first, count, extra
         )
-        state = incoming(own, sent, slice(first * TILE, (first + count) * TILE))
-        pending.append((y, state, first))
-    out = None
-    for y, state, first in pending:
-        count = y.shape[1] // TILE
-        cuts = (0, count // 2, count) if first + count == tiles else (0, count)
-        for base, last in zip(cuts[:-1], cuts[1:]):
-            out = run_norm(
-                out, y, shared[0], reach, norm_gain[None], gather, state, first + base, base, last - base, width_x
-            )
+
+    def norm(out, y, state, first, base, count):
+        place = y_mine.astype(jnp.int32)[None]
+        return run_norm(
+            out, place, y, shared[0], reach, norm_gain[None], gather, state, first + base, base, count, width_x
+        )
+
+    if halved is None:
+        shared, out = None, None
+        pending = []
+        for call in calls:
+            y, own, sent, shared = scan(call, shared)
+            first, count = call[2], call[4]
+            pending.append((y, incoming(own, beside(sent), slice(first * TILE, (first + count) * TILE)), first, 0, count))
+        for each in pending:
+            out = norm(out, *each)
+        return out[None]
+
+    (_, _, first_a, _, count_a), (_, _, first_b, _, count_b) = calls
+    y_a, own_a, sent_a, shared = scan(calls[0], None, extra)
+    other_a = swap(sent_a)
+    kept_rows = slice(half, half + own_kept.shape[0])
+    later = lambda rows: rows[1:].reshape(-1)[: count_b * TILE]
+    other_kept = other_a[kept_rows].astype(F32)
+    lower_kept = jnp.where(upper, other_kept, own_kept)
+    upper_kept = jnp.where(upper, own_kept, other_kept)
+    pieces, other_a = together(calls[1][0], other_a)
+    below_a = plane_of(own_a, other_a, upper_kept[0], lower_kept * upper_kept)
+    y_b, own_b, sent_b, _ = scan((pieces, *calls[1][1:]), shared)
+    sent_b, *below_a = together(sent_b, *below_a)
+    other_b = swap(sent_b)
+    z_kept = [part[kept_rows].astype(F32) for part in below_a]
+    state_a = halves_of(own_a, other_a, below_a, lower_kept[0], [kept[0] for kept in z_kept])
+    below_b = plane_of(own_b, other_b, later(upper_kept))
+    out = norm(None, y_a, state_a, first_a, 0, count_a // 2)
+    out = norm(out, y_a, state_a, first_a, count_a // 2, count_a - count_a // 2)
+    out, *below_b = together(out, *below_b)
+    state_b = halves_of(own_b, other_b, below_b, later(lower_kept), [later(kept) for kept in z_kept])
+    out = norm(out, y_b, state_b, first_b, 0, count_b)
     return out[None]
 
 

time: 192 us -> 158 us (0.82)
  Pallas kernels: 68.2 us -> 55.6 us
  local copies, waits for them, and re-layouts: 16.5 us -> 10.1 us
  other arithmetic: 10.5 us -> 4.29 us
  starting transfers between devices: 35 us -> 29.5 us
  waiting for transfers between devices: 47.3 us -> 43.4 us
    ppermute x15 -> x16, waiting for transfers between devices: 6.03 us -> 19.1 us  [send(): return lax.ppermute(value, ('dp', 'seq'), pairs)]
    pallas_call x6, Pallas kernels: 68.2 us -> 55.6 us  [the longest x2 34.3 us: run_scan(): pl.pallas_call(lambda *refs: scan_kernel(leads, extras, tiles, len(pieces...]
    ppermute x1, waiting for transfers between devices: 12 us -> 0.01 us  [local(): lax.ppermute(rows, 'seq', [(i, i + 1) for i in range(seq_count - 1)])]
    ppermute x13 -> x10, starting transfers between devices: 18.8 us -> 11.3 us  [shifted(): return lax.ppermute(value, 'seq', pairs)]
    ppermute x13 -> x10, waiting for transfers between devices: 29.2 us -> 24.3 us  [shifted(): return lax.ppermute(value, 'seq', pairs)]
    select_n x5 -> x0, other arithmetic: 3.8 us -> none  [the longest x2 2.1 us: incoming(): jnp.where(upper, value[..., :half], value[..., half:])]
    ppermute x15 -> x16, starting transfers between devices: 13.1 us -> 15.7 us  [send(): return lax.ppermute(value, ('dp', 'seq'), pairs)]
    slice x3 -> x6, local copies, waits for them, and re-layouts: 4.15 us -> 1.75 us  [the longest x1 0.89 us: local(): rim_rows = token_rows[tok_count - RIM:]]
  transfers between devices with their start and end apart: 30 -> 28, of which waited for: 10 -> 8; matrix products, arithmetic and copies ran while one was open for 12% -> 6% of each run, Pallas kernels for 32% -> 33%
where the time goes in v4:
time: 158 us; the launch traced here: 157 us
  Pallas kernels  55.6 us (35%)
  waiting for transfers between devices  43.4 us (27%)
  starting transfers between devices  29.5 us (19%)
  between operations  14.1 us (9%)
  local copies, waits for them, and re-layouts  10.1 us (6%)
  other arithmetic  4.29 us (3%)
    pallas_call x2, Pallas kernels, run_scan(): pl.pallas_call(lambda *refs: scan_kernel(leads, extras, tiles, len(pieces...  34.3 us
    ppermute x10, waiting for transfers between devices, shifted(): return lax.ppermute(value, 'seq', pairs)  24.3 us
    ppermute x16, waiting for transfers between devices, send(): return lax.ppermute(value, ('dp', 'seq'), pairs)  19.1 us
    ppermute x16, starting transfers between devices, send(): return lax.ppermute(value, ('dp', 'seq'), pairs)  15.7 us
    pallas_call x1, Pallas kernels, run_decay(): pl.pallas_call(decay_kernel, grid=(tiles,), in_specs=[whole((tiles * coun...  13.3 us
    ppermute x10, starting transfers between devices, shifted(): return lax.ppermute(value, 'seq', pairs)  11.3 us
    pallas_call x3, Pallas kernels, run_norm(): pl.pallas_call(lambda *refs: norm_kernel(len(state), *refs), grid=(tiles,...  8.06 us
    unnamed x51, local copies, waits for them, and re-layouts  3.37 us
  transfers between devices with their start and end apart: 28, of which 8 were waited for; matrix products, arithmetic and copies ran while one was open for 6% of the time, Pallas kernels for 33%

profile of v4, /device:TPU:24, one launch (start us, length us, event | category | flops | bytes accessed | tf_op | source)
XLA Modules:
  0.0 157.1 jit_solution(5784282239451361829)
XLA Ops:
  6.6 1.1 copy.40
  7.7 0.7 slice.90
  8.5 2.0 %collective-permute-start.1 = (bf16[1,6,80,256]{3,2,1,0:T(8,128)(2,1)S(1)}, bf16[1,6,80,256]{3,2,1,0:T(8,128)(2,1)S(1)}, u32[]{:S(2)}, u32[]{:S(2)}) collective-permute-start(bf16[1,6,80,256]{3,2,1,0:T(8,128)(2,1)S(1)} %slice.89), channel_id=1, source_target_pairs={{0,6},{1,7},{2,0},{3,1},{4,2},{5,3},{6,4},{7,5},{8,14},{9,15},{10,... | collective-permute-start | bytes 737288 | tf_op jit(solution)/shard_map/ppermute | solution.py:424
  10.5 1.5 collective-permute-start.2
  12.0 1.5 collective-permute-start.3
  13.6 0.9 slice_bitcast_fusion
  14.4 2.4 %collective-permute-start.8 = (bf16[16,2560]{1,0:T(8,128)(2,1)S(1)}, bf16[16,2560]{1,0:T(8,128)(2,1)}, u32[]{:S(2)}, u32[]{:S(2)}) collective-permute-start(bf16[16,2560]{1,0:T(8,128)(2,1)S(1)} %slice_bitcast_fusion), channel_id=1, source_target_pairs={{0,1},{1,2},{2,3},{3,4},{4,5},{5,6},{6,7},{8,9},{9,10},{10,11},{11... | collective-permute-start | bytes 245768 | tf_op jit(solution)/shard_map/ppermute | solution.py:490
  17.9 0.7 maximum_maximum_fusion.refs_12_.refs_17_.refs_5_.refs_10_
  19.1 0.6 pad.13
  19.8 0.7 copy.34
  20.5 0.6 pad.14.refs_18_
  21.5 0.7 constant_dynamic-update-slice_fusion.10
  22.2 0.7 constant_dynamic-update-slice_fusion.9
  23.0 1.5 collective-permute-start.5
  24.5 2.9 %collective-permute-start.6 = (bf16[2,6,80,256]{3,2,1,0:T(8,128)(2,1)S(1)}, bf16[2,6,80,256]{3,2,1,0:T(8,128)(2,1)S(1)}, u32[]{:S(2)}, u32[]{:S(2)}) collective-permute-start(bf16[2,6,80,256]{3,2,1,0:T(8,128)(2,1)S(1)} %get-tuple-element.127), channel_id=1, source_target_pairs={{0,1},{1,0},{2,3},{3,2},{4,5},{5,4},{6,7},{7,6},{8,24},{9,25},{10,... | collective-permute-start | bytes 1474568 | tf_op jit(solution)/shard_map/ppermute | solution.py:424
  28.3 11.8 %collective-permute-done.4 = bf16[1,6,80,256]{3,2,1,0:T(8,128)(2,1)S(1)} collective-permute-done((bf16[1,6,80,256]{3,2,1,0:T(8,128)(2,1)S(1)}, bf16[1,6,80,256]{3,2,1,0:T(8,128)(2,1)S(1)}, u32[]{:S(2)}, u32[]{:S(2)}) %collective-permute-start.4) | collective-permute-done | bytes 245792 | tf_op jit(solution)/shard_map/ppermute | solution.py:424
  40.1 0.8 collective-permute-start.10
  41.0 1.2 collective-permute-start.9
  42.2 0.8 reshape.75.rate_ref
  43.1 0.9 collective-permute-start.11
  44.0 13.3 %decays.1 = (bf16[10,2,768,256]{3,2,1,0:T(8,128)(2,1)}, bf16[10,768,256]{2,1,0:T(8,128)(2,1)}, bf16[10,768,256]{2,1,0:T(8,128)(2,1)}, f32[10,16,256]{2,1,0:T(8,128)}) custom-call(f32[240,128]{1,0:T(8,128)} %bitcast.62, f32[240,1]{1,0:T(8,128)} %reshape.75.rate_ref), custom_call_target="tpu_custom_call" | custom-call | flops 10000000000 | bytes 16000000 | tf_op jit(solution)/shard_map/decays/pallas_call | solution.py:275
  57.4 1.0 copy-done.16
  58.4 1.8 %collective-permute-start.14 = (bf16[8,6,80,256]{3,2,1,0:T(8,128)(2,1)S(1)}, bf16[8,6,80,256]{3,2,1,0:T(8,128)(2,1)S(1)}, u32[]{:S(2)}, u32[]{:S(2)}) collective-permute-start(bf16[8,6,80,256]{3,2,1,0:T(8,128)(2,1)S(1)} %constant_dynamic-update-slice_fusion.6.refs_3_), channel_id=1, source_target_pairs={{0,8},{1,9},{2,10},{3,11},{4,12},{5,13},{6,14},{7,15},{8,0},{9,1},... | collective-permute-start | bytes 5898248 | tf_op jit(solution)/shard_map/ppermute | solution.py:424
  60.5 1.0 collective-permute-start.13
  61.4 5.3 %collective-permute-done.13.refs_5_ = bf16[1,6,80,256]{3,2,1,0:T(8,128)(2,1)S(1)} collective-permute-done((bf16[1,6,80,256]{3,2,1,0:T(8,128)(2,1)S(1)}, bf16[1,6,80,256]{3,2,1,0:T(8,128)(2,1)S(1)}, u32[]{:S(2)}, u32[]{:S(2)}) %collective-permute-start.13) | collective-permute-done | bytes 245792 | tf_op jit(solution)/shard_map/ppermute | solution.py:424
  66.8 1.8 %collective-permute-done.16.refs_9_ = bf16[1,6,80,256]{3,2,1,0:T(8,128)(2,1)S(1)} collective-permute-done((bf16[1,6,80,256]{3,2,1,0:T(8,128)(2,1)S(1)}, bf16[1,6,80,256]{3,2,1,0:T(8,128)(2,1)S(1)}, u32[]{:S(2)}, u32[]{:S(2)}) %collective-permute-start.16) | collective-permute-done | bytes 245792 | tf_op jit(solution)/shard_map/ppermute | solution.py:424
  68.7 0.7 copy-done.19
  69.4 18.1 %project_scan.2 = (bf16[5,768,256]{2,1,0:T(8,128)(2,1)}, f32[64,1280]{1,0:T(8,128)}, bf16[80,1280]{1,0:T(8,128)(2,1)}, bf16[768,128]{1,0:T(8,128)(2,1)}, f32[128...) custom-call(s32[32]{0:T(128)} %get-tuple-element.63.refs_0_, s32[1]{0:T(128)} %bitcast.refs_1_.refs_0_, ...), custom_call_target="tpu_custom_call" | custom-call | flops 15000000512 | bytes 15000000 | tf_op jit(solution)/shard_map/project_scan/pallas_call | solution.py:347
  87.4 0.6 collective-permute-start.17
  88.1 6.7 %collective-permute-done.17 = bf16[80,1280]{1,0:T(8,128)(2,1)S(1)} collective-permute-done((bf16[80,1280]{1,0:T(8,128)(2,1)}, bf16[80,1280]{1,0:T(8,128)(2,1)S(1)}, u32[]{:S(2)}, u32[]{:S(2)}) %collective-permute-start.17) | collective-permute-done | bytes 204832 | tf_op jit(solution)/shard_map/ppermute | solution.py:399
  94.9 1.1 fusion.3
  96.0 1.5 collective-permute-start.18
  97.5 1.3 collective-permute-start.19
  98.8 1.3 collective-permute-start.20
  100.1 16.3 %project_scan.3 = (bf16[5,768,256]{2,1,0:T(8,128)(2,1)}, f32[64,1280]{1,0:T(8,128)}, bf16[64,1280]{1,0:T(8,128)(2,1)}) custom-call(s32[32]{0:T(128)} %get-tuple-element.62.refs_0_, s32[1]{0:T(128)} %bitcast.refs_1_.refs_0_, bf16[32,5,80,256]{3,2,1,0:T(8,128)(2,1)} %all-gather.2.cloned.1.call-done.refs_2_, ...), custom_call_target="tpu_custom_call" | custom-call | flops 15000000512 | bytes 15000000 | tf_op jit(solution)/shard_map/project_scan/pallas_call | solution.py:347
  116.4 0.6 collective-permute-start.22
  117.3 1.5 collective-permute-start.21
  118.8 5.0 %collective-permute-done.22 = bf16[64,1280]{1,0:T(8,128)(2,1)S(1)} collective-permute-done((bf16[64,1280]{1,0:T(8,128)(2,1)}, bf16[64,1280]{1,0:T(8,128)(2,1)S(1)}, u32[]{:S(2)}, u32[]{:S(2)}) %collective-permute-start.22) | collective-permute-done | bytes 163872 | tf_op jit(solution)/shard_map/ppermute | solution.py:399
  123.8 1.1 fusion.7
  124.9 1.3 collective-permute-start.23
  126.2 1.3 collective-permute-start.24
  127.5 1.3 collective-permute-start.25
  128.8 1.8 %head_norm.3.refs_8_ = bf16[768,2560]{1,0:T(8,128)(2,1)} custom-call(s32[1]{0:T(128)} %bitcast.refs_1_.refs_0_, bf16[5,768,256]{2,1,0:T(8,128)(2,1)S(1)} %copy-done.1, bf16[768,128]{1,0:T(8,128)(2,1)S(1)} %copy-done.3, bf16[10,768,256]{2,1,0:T(8,128)(2,1)S(1)} %copy-done, f32[1,2560]{1,0:T(1,128)S(1)} %broadcast_in_dim.65.refs_4_, ...), custom_call_target="tpu_custom_call" | custom-call | flops 800000000 | bytes 1966080 | tf_op jit(solution)/shard_map/head_norm/pallas_call | solution.py:381
  130.6 2.5 %head_norm.4.refs_8_ = bf16[768,2560]{1,0:T(8,128)(2,1)} custom-call(s32[1]{0:T(128)} %bitcast.refs_1_.refs_0_, bf16[5,768,256]{2,1,0:T(8,128)(2,1)S(1)} %copy-done.1, bf16[768,128]{1,0:T(8,128)(2,1)S(1)} %copy-done.3, bf16[10,768,256]{2,1,0:T(8,128)(2,1)S(1)} %copy-done, f32[1,2560]{1,0:T(1,128)S(1)} %broadcast_in_dim.65.refs_4_, ...), custom_call_target="tpu_custom_call", output_to_operand_aliasing={{}: (8, {})} | custom-call | flops 1200000000 | bytes 2949120 | tf_op jit(solution)/shard_map/head_norm/pallas_call | solution.py:381
  133.2 7.8 %collective-permute-done.24 = bf16[64,1280]{1,0:T(8,128)(2,1)S(1)} collective-permute-done((bf16[64,1280]{1,0:T(8,128)(2,1)S(1)}, bf16[64,1280]{1,0:T(8,128)(2,1)S(1)}, u32[]{:S(2)}, u32[]{:S(2)}) %collective-permute-start.24) | collective-permute-done | bytes 163872 | tf_op jit(solution)/shard_map/ppermute | solution.py:399
  141.1 0.6 collective-permute-start.26
  141.8 4.7 %collective-permute-done.26.refs_7_ = bf16[64,1280]{1,0:T(8,128)(2,1)S(1)} collective-permute-done((bf16[64,1280]{1,0:T(8,128)(2,1)S(1)}, bf16[64,1280]{1,0:T(8,128)(2,1)S(1)}, u32[]{:S(2)}, u32[]{:S(2)}) %collective-permute-start.26) | collective-permute-done | bytes 163872 | tf_op jit(solution)/shard_map/ppermute | solution.py:399
  146.5 3.7 %head_norm.5 = bf16[768,2560]{1,0:T(8,128)(2,1)} custom-call(s32[1]{0:T(128)} %bitcast.refs_1_.refs_0_, bf16[5,768,256]{2,1,0:T(8,128)(2,1)S(1)} %copy-done.2, bf16[768,128]{1,0:T(8,128)(2,1)S(1)} %copy-done.3, bf16[10,768,256]{2,1,0:T(8,128)(2,1)S(1)} %copy-done, f32[1,2560]{1,0:T(1,128)S(1)} %broadcast_in_dim.65.refs_4_, ...), custom_call_target="tpu_custom_call", output_to_operand_aliasing={{}: (8, {})} | custom-call | flops 2000000000 | bytes 4915200 | tf_op jit(solution)/shard_map/head_norm/pallas_call | solution.py:381
  (118 shorter events, 3.9 us)
Async XLA Ops:
  6.5 10.3 %copy-start.6 = (f32[1,40,768]{2,1,0:T(8,128)S(1)}, f32[1,40,768]{2,1,0:T(8,128)}, u32[]{:S(2)}) copy-start(f32[1,40,768]{2,1,0:T(8,128)} %param.13) | copy-start | bytes 368644
  6.5 10.5 %copy-start.20 = (f32[40]{0:T(128)S(1)}, f32[40]{0:T(128)}, u32[]{:S(2)}) copy-start(f32[40]{0:T(128)} %param.12) | copy-start | bytes 484
  6.5 11.2 %copy-start.12 = (f32[2816]{0:T(1024)S(1)}, f32[2816]{0:T(1024)}, u32[]{:S(2)}) copy-start(f32[2816]{0:T(1024)} %param.11) | copy-start | bytes 33796
  6.5 11.3 %copy-start.14 = (f32[40]{0:T(128)S(1)}, f32[40]{0:T(128)}, u32[]{:S(2)}) copy-start(f32[40]{0:T(128)} %param.14) | copy-start | bytes 484
  6.5 11.4 %copy-start.9 = (f32[4,2816]{1,0:T(4,128)S(1)}, f32[4,2816]{1,0:T(4,128)}, u32[]{:S(2)}) copy-start(f32[4,2816]{1,0:T(4,128)} %param.10) | copy-start | bytes 135172
  6.5 88.4 %all-gather.2.cloned.1.call-start = ((), (), s32[]{:S(2)}) async-start(), calls=%async_computation | async-start | bytes 6758400 | tf_op jit(solution)/shard_map/all_gather | solution.py:527
  8.5 13.0 %collective-permute-start = (bf16[1,6,80,256]{3,2,1,0:T(8,128)(2,1)S(1)}, bf16[1,6,80,256]{3,2,1,0:T(8,128)(2,1)S(1)}, u32[]{:S(2)}, u32[]{:S(2)}) collective-permute-start(bf16[1,6,80,256]{3,2,1,0:T(8,128)(2,1)S(1)} %slice.89), channel_id=1, source_target_pairs={{0,2},{1,3},{2,4},{3,5},{4,6},{5,7},{6,0},{7,1},{8,10},{9,11},{10,... | collective-permute-start | bytes 737288 | tf_op jit(solution)/shard_map/ppermute | solution.py:424
  8.5 13.0 %collective-permute-start.1 = (bf16[1,6,80,256]{3,2,1,0:T(8,128)(2,1)S(1)}, bf16[1,6,80,256]{3,2,1,0:T(8,128)(2,1)S(1)}, u32[]{:S(2)}, u32[]{:S(2)}) collective-permute-start(bf16[1,6,80,256]{3,2,1,0:T(8,128)(2,1)S(1)} %slice.89), channel_id=1, source_target_pairs={{0,6},{1,7},{2,0},{3,1},{4,2},{5,3},{6,4},{7,5},{8,14},{9,15},{10,... | collective-permute-start | bytes 737288 | tf_op jit(solution)/shard_map/ppermute | solution.py:424
  10.5 10.9 %collective-permute-start.2 = (bf16[1,6,80,256]{3,2,1,0:T(8,128)(2,1)S(1)}, bf16[1,6,80,256]{3,2,1,0:T(8,128)(2,1)S(1)}, u32[]{:S(2)}, u32[]{:S(2)}) collective-permute-start(bf16[1,6,80,256]{3,2,1,0:T(8,128)(2,1)S(1)} %slice.89), channel_id=1, source_target_pairs={{0,16},{1,17},{2,18},{3,19},{4,20},{5,21},{6,22},{7,23},{8,9},{9,8... | collective-permute-start | bytes 737288 | tf_op jit(solution)/shard_map/ppermute | solution.py:424
  12.0 9.5 %collective-permute-start.3 = (bf16[1,6,80,256]{3,2,1,0:T(8,128)(2,1)S(1)}, bf16[1,6,80,256]{3,2,1,0:T(8,128)(2,1)S(1)}, u32[]{:S(2)}, u32[]{:S(2)}) collective-permute-start(bf16[1,6,80,256]{3,2,1,0:T(8,128)(2,1)S(1)} %slice.89), channel_id=1, source_target_pairs={{0,1},{1,0},{2,3},{3,2},{4,5},{5,4},{6,7},{7,6},{8,24},{9,25},{10,... | collective-permute-start | bytes 737288 | tf_op jit(solution)/shard_map/ppermute | solution.py:424
  14.4 13.8 %collective-permute-start.8 = (bf16[16,2560]{1,0:T(8,128)(2,1)S(1)}, bf16[16,2560]{1,0:T(8,128)(2,1)}, u32[]{:S(2)}, u32[]{:S(2)}) collective-permute-start(bf16[16,2560]{1,0:T(8,128)(2,1)S(1)} %slice_bitcast_fusion), channel_id=1, source_target_pairs={{0,1},{1,2},{2,3},{3,4},{4,5},{5,6},{6,7},{8,9},{9,10},{10,11},{11... | collective-permute-start | bytes 245768 | tf_op jit(solution)/shard_map/ppermute | solution.py:490
  23.0 17.2 %collective-permute-start.5 = (bf16[2,6,80,256]{3,2,1,0:T(8,128)(2,1)S(1)}, bf16[2,6,80,256]{3,2,1,0:T(8,128)(2,1)S(1)}, u32[]{:S(2)}, u32[]{:S(2)}) collective-permute-start(bf16[2,6,80,256]{3,2,1,0:T(8,128)(2,1)S(1)} %get-tuple-element.127), channel_id=1, source_target_pairs={{0,16},{1,17},{2,18},{3,19},{4,20},{5,21},{6,22},{7,23},{8,9},{9,8... | collective-permute-start | bytes 1474568 | tf_op jit(solution)/shard_map/ppermute | solution.py:424
  24.5 15.7 %collective-permute-start.6 = (bf16[2,6,80,256]{3,2,1,0:T(8,128)(2,1)S(1)}, bf16[2,6,80,256]{3,2,1,0:T(8,128)(2,1)S(1)}, u32[]{:S(2)}, u32[]{:S(2)}) collective-permute-start(bf16[2,6,80,256]{3,2,1,0:T(8,128)(2,1)S(1)} %get-tuple-element.127), channel_id=1, source_target_pairs={{0,1},{1,0},{2,3},{3,2},{4,5},{5,4},{6,7},{7,6},{8,24},{9,25},{10,... | collective-permute-start | bytes 1474568 | tf_op jit(solution)/shard_map/ppermute | solution.py:424
  27.9 12.3 %collective-permute-start.4 = (bf16[1,6,80,256]{3,2,1,0:T(8,128)(2,1)S(1)}, bf16[1,6,80,256]{3,2,1,0:T(8,128)(2,1)S(1)}, u32[]{:S(2)}, u32[]{:S(2)}) collective-permute-start(bf16[1,6,80,256]{3,2,1,0:T(8,128)(2,1)S(1)} %slice.89), channel_id=1, source_target_pairs={{0,4},{1,5},{2,6},{3,7},{4,0},{5,1},{6,2},{7,3},{8,12},{9,13},{10,... | collective-permute-start | bytes 737288 | tf_op jit(solution)/shard_map/ppermute | solution.py:424
  27.9 12.3 %collective-permute-start.7 = (bf16[1,6,80,256]{3,2,1,0:T(8,128)(2,1)S(1)}, bf16[1,6,80,256]{3,2,1,0:T(8,128)(2,1)S(1)}, u32[]{:S(2)}, u32[]{:S(2)}) collective-permute-start(bf16[1,6,80,256]{3,2,1,0:T(8,128)(2,1)S(1)} %collective-permute-done.2), channel_id=1, source_target_pairs={{0,1},{1,0},{2,3},{3,2},{4,5},{5,4},{6,7},{7,6},{8,24},{9,25},{10,... | collective-permute-start | bytes 737288 | tf_op jit(solution)/shard_map/ppermute | solution.py:424
  40.1 17.2 %collective-permute-start.10 = (bf16[1,6,80,256]{3,2,1,0:T(8,128)(2,1)S(1)}, bf16[1,6,80,256]{3,2,1,0:T(8,128)(2,1)S(1)}, u32[]{:S(2)}, u32[]{:S(2)}) collective-permute-start(bf16[1,6,80,256]{3,2,1,0:T(8,128)(2,1)S(1)} %collective-permute-done.4), channel_id=1, source_target_pairs={{0,1},{1,0},{2,3},{3,2},{4,5},{5,4},{6,7},{7,6},{8,24},{9,25},{10,... | collective-permute-start | bytes 737288 | tf_op jit(solution)/shard_map/ppermute | solution.py:424
  41.0 16.4 %collective-permute-start.9 = (bf16[1,6,80,256]{3,2,1,0:T(8,128)(2,1)S(1)}, bf16[1,6,80,256]{3,2,1,0:T(8,128)(2,1)S(1)}, u32[]{:S(2)}, u32[]{:S(2)}) collective-permute-start(bf16[1,6,80,256]{3,2,1,0:T(8,128)(2,1)S(1)} %collective-permute-done.4), channel_id=1, source_target_pairs={{0,16},{1,17},{2,18},{3,19},{4,20},{5,21},{6,22},{7,23},{8,9},{9,8... | collective-permute-start | bytes 737288 | tf_op jit(solution)/shard_map/ppermute | solution.py:424
  43.0 14.3 %copy-start.8 = (bf16[4,6,80,256]{3,2,1,0:T(8,128)(2,1)}, bf16[4,6,80,256]{3,2,1,0:T(8,128)(2,1)S(1)}, u32[]{:S(2)}) copy-start(bf16[4,6,80,256]{3,2,1,0:T(8,128)(2,1)S(1)} %constant_dynamic-update-slice_fusion.2.refs_2_) | copy-start | bytes 2949124
  43.0 14.4 %collective-permute-start.12 = (bf16[4,6,80,256]{3,2,1,0:T(8,128)(2,1)S(1)}, bf16[4,6,80,256]{3,2,1,0:T(8,128)(2,1)S(1)}, u32[]{:S(2)}, u32[]{:S(2)}) collective-permute-start(bf16[4,6,80,256]{3,2,1,0:T(8,128)(2,1)S(1)} %constant_dynamic-update-slice_fusion.2.refs_2_), channel_id=1, source_target_pairs={{0,8},{1,9},{2,10},{3,11},{4,12},{5,13},{6,14},{7,15},{8,0},{9,1},... | collective-permute-start | bytes 2949128 | tf_op jit(solution)/shard_map/ppermute | solution.py:424
  43.1 14.3 %collective-permute-start.11 = (bf16[2,6,80,256]{3,2,1,0:T(8,128)(2,1)S(1)}, bf16[2,6,80,256]{3,2,1,0:T(8,128)(2,1)S(1)}, u32[]{:S(2)}, u32[]{:S(2)}) collective-permute-start(bf16[2,6,80,256]{3,2,1,0:T(8,128)(2,1)S(1)} %collective-permute-done.5), channel_id=1, source_target_pairs={{0,1},{1,0},{2,3},{3,2},{4,5},{5,4},{6,7},{7,6},{8,24},{9,25},{10,... | collective-permute-start | bytes 1474568 | tf_op jit(solution)/shard_map/ppermute | solution.py:424
  44.0 13.3 %copy-start.10 = (bf16[8,6,80,256]{3,2,1,0:T(8,128)(2,1)S(1)}, bf16[8,6,80,256]{3,2,1,0:T(8,128)(2,1)}, u32[]{:S(2)}) copy-start(bf16[8,6,80,256]{3,2,1,0:T(8,128)(2,1)} %get-tuple-element.126) | copy-start | bytes 5898244
  57.4 1.0 copy-start.16
  58.4 10.2 %copy-start.11 = (bf16[8,6,80,256]{3,2,1,0:T(8,128)(2,1)}, bf16[8,6,80,256]{3,2,1,0:T(8,128)(2,1)S(1)}, u32[]{:S(2)}) copy-start(bf16[8,6,80,256]{3,2,1,0:T(8,128)(2,1)S(1)} %constant_dynamic-update-slice_fusion.6.refs_3_) | copy-start | bytes 5898244
  58.4 8.3 %collective-permute-start.14 = (bf16[8,6,80,256]{3,2,1,0:T(8,128)(2,1)S(1)}, bf16[8,6,80,256]{3,2,1,0:T(8,128)(2,1)S(1)}, u32[]{:S(2)}, u32[]{:S(2)}) collective-permute-start(bf16[8,6,80,256]{3,2,1,0:T(8,128)(2,1)S(1)} %constant_dynamic-update-slice_fusion.6.refs_3_), channel_id=1, source_target_pairs={{0,8},{1,9},{2,10},{3,11},{4,12},{5,13},{6,14},{7,15},{8,0},{9,1},... | collective-permute-start | bytes 5898248 | tf_op jit(solution)/shard_map/ppermute | solution.py:424
  60.4 8.3 %copy-start.7 = (bf16[3,6,80,256]{3,2,1,0:T(8,128)(2,1)}, bf16[3,6,80,256]{3,2,1,0:T(8,128)(2,1)S(1)}, u32[]{:S(2)}) copy-start(bf16[3,6,80,256]{3,2,1,0:T(8,128)(2,1)S(1)} %constant_dynamic-update-slice_fusion.11.refs_4_) | copy-start | bytes 2211844
  60.4 6.3 %collective-permute-start.15 = (bf16[3,6,80,256]{3,2,1,0:T(8,128)(2,1)S(1)}, bf16[3,6,80,256]{3,2,1,0:T(8,128)(2,1)S(1)}, u32[]{:S(2)}, u32[]{:S(2)}) collective-permute-start(bf16[3,6,80,256]{3,2,1,0:T(8,128)(2,1)S(1)} %constant_dynamic-update-slice_fusion.11.refs_4_), channel_id=1, source_target_pairs={{0,8},{1,9},{2,10},{3,11},{4,12},{5,13},{6,14},{7,15},{8,0},{9,1},... | collective-permute-start | bytes 2211848 | tf_op jit(solution)/shard_map/ppermute | solution.py:424
  60.5 6.3 %collective-permute-start.13 = (bf16[1,6,80,256]{3,2,1,0:T(8,128)(2,1)S(1)}, bf16[1,6,80,256]{3,2,1,0:T(8,128)(2,1)S(1)}, u32[]{:S(2)}, u32[]{:S(2)}) collective-permute-start(bf16[1,6,80,256]{3,2,1,0:T(8,128)(2,1)S(1)} %collective-permute-done.9), channel_id=1, source_target_pairs={{0,1},{1,0},{2,3},{3,2},{4,5},{5,4},{6,7},{7,6},{8,24},{9,25},{10,... | collective-permute-start | bytes 737288 | tf_op jit(solution)/shard_map/ppermute | solution.py:424
  66.7 2.0 %copy-start.18 = (bf16[1,6,80,256]{3,2,1,0:T(8,128)(2,1)}, bf16[1,6,80,256]{3,2,1,0:T(8,128)(2,1)S(1)}, u32[]{:S(2)}) copy-start(bf16[1,6,80,256]{3,2,1,0:T(8,128)(2,1)S(1)} %collective-permute-done.13.refs_5_) | copy-start | bytes 737284
  66.7 2.0 %copy-start.17 = (bf16[3,6,80,256]{3,2,1,0:T(8,128)(2,1)}, bf16[3,6,80,256]{3,2,1,0:T(8,128)(2,1)S(1)}, u32[]{:S(2)}) copy-start(bf16[3,6,80,256]{3,2,1,0:T(8,128)(2,1)S(1)} %collective-permute-done.15.refs_8_) | copy-start | bytes 2211844
  66.7 2.0 %copy-start.15 = (bf16[8,6,80,256]{3,2,1,0:T(8,128)(2,1)}, bf16[8,6,80,256]{3,2,1,0:T(8,128)(2,1)S(1)}, u32[]{:S(2)}) copy-start(bf16[8,6,80,256]{3,2,1,0:T(8,128)(2,1)S(1)} %collective-permute-done.14.refs_7_) | copy-start | bytes 5898244
  66.7 1.9 %collective-permute-start.16 = (bf16[1,6,80,256]{3,2,1,0:T(8,128)(2,1)S(1)}, bf16[1,6,80,256]{3,2,1,0:T(8,128)(2,1)S(1)}, u32[]{:S(2)}, u32[]{:S(2)}) collective-permute-start(bf16[1,6,80,256]{3,2,1,0:T(8,128)(2,1)S(1)} %collective-permute-done.13.refs_5_), channel_id=1, source_target_pairs={{0,8},{1,9},{2,10},{3,11},{4,12},{5,13},{6,14},{7,15},{8,0},{9,1},... | collective-permute-start | bytes 737288 | tf_op jit(solution)/shard_map/ppermute | solution.py:424
  69.4 18.7 %copy-start.13 = (f32[2560]{0:T(1024)S(1)}, f32[2560]{0:T(1024)}, u32[]{:S(2)}) copy-start(f32[2560]{0:T(1024)} %param.15) | copy-start | bytes 30724
  87.4 7.4 %collective-permute-start.17 = (bf16[80,1280]{1,0:T(8,128)(2,1)}, bf16[80,1280]{1,0:T(8,128)(2,1)S(1)}, u32[]{:S(2)}, u32[]{:S(2)}) collective-permute-start(bf16[80,1280]{1,0:T(8,128)(2,1)} %get-tuple-element.89), channel_id=1, source_target_pairs={{0,1},{1,0},{2,3},{3,2},{4,5},{5,4},{6,7},{7,6},{8,9},{9,8},{10,11... | collective-permute-start | bytes 614408 | tf_op jit(solution)/shard_map/ppermute | solution.py:399
  96.0 20.4 %collective-permute-start.18 = (bf16[80,1280]{1,0:T(8,128)(2,1)S(1)}, bf16[80,1280]{1,0:T(8,128)(2,1)S(1)}, u32[]{:S(2)}, u32[]{:S(2)}) collective-permute-start(bf16[80,1280]{1,0:T(8,128)(2,1)S(1)} %fusion.9), channel_id=1, source_target_pairs={{0,2},{1,3},{2,4},{3,5},{4,6},{5,7},{8,10},{9,11},{10,12},{11,13},... | collective-permute-start | bytes 614408 | tf_op jit(solution)/shard_map/ppermute | solution.py:399
  97.5 18.9 %collective-permute-start.19 = (bf16[80,1280]{1,0:T(8,128)(2,1)S(1)}, bf16[80,1280]{1,0:T(8,128)(2,1)S(1)}, u32[]{:S(2)}, u32[]{:S(2)}) collective-permute-start(bf16[80,1280]{1,0:T(8,128)(2,1)S(1)} %fusion.9), channel_id=1, source_target_pairs={{0,4},{1,5},{2,6},{3,7},{8,12},{9,13},{10,14},{11,15},{16,20},{17,... | collective-permute-start | bytes 614408 | tf_op jit(solution)/shard_map/ppermute | solution.py:399
  98.8 17.7 %collective-permute-start.20 = (bf16[80,1280]{1,0:T(8,128)(2,1)S(1)}, bf16[80,1280]{1,0:T(8,128)(2,1)S(1)}, u32[]{:S(2)}, u32[]{:S(2)}) collective-permute-start(bf16[80,1280]{1,0:T(8,128)(2,1)S(1)} %fusion.9), channel_id=1, source_target_pairs={{0,6},{1,7},{8,14},{9,15},{16,22},{17,23},{24,30},{25,31}} | collective-permute-start | bytes 614408 | tf_op jit(solution)/shard_map/ppermute | solution.py:399
  100.1 17.1 %copy-start.4 = (f32[64,1280]{1,0:T(8,128)S(1)}, f32[64,1280]{1,0:T(8,128)}, u32[]{:S(2)}) copy-start(f32[64,1280]{1,0:T(8,128)} %get-tuple-element.100) | copy-start | bytes 983044
  100.1 28.7 %copy-start = (bf16[10,768,256]{2,1,0:T(8,128)(2,1)S(1)}, bf16[10,768,256]{2,1,0:T(8,128)(2,1)}, u32[]{:S(2)}) copy-start(bf16[10,768,256]{2,1,0:T(8,128)(2,1)} %get-tuple-element.95.refs_3_) | copy-start | bytes 11796484
  100.1 28.7 %copy-start.3 = (bf16[768,128]{1,0:T(8,128)(2,1)S(1)}, bf16[768,128]{1,0:T(8,128)(2,1)}, u32[]{:S(2)}) copy-start(bf16[768,128]{1,0:T(8,128)(2,1)} %get-tuple-element.91.refs_11_.refs_2_) | copy-start | bytes 589828
  116.4 12.4 %copy-start.1 = (bf16[5,768,256]{2,1,0:T(8,128)(2,1)S(1)}, bf16[5,768,256]{2,1,0:T(8,128)(2,1)}, u32[]{:S(2)}) copy-start(bf16[5,768,256]{2,1,0:T(8,128)(2,1)} %get-tuple-element.98.refs_1_) | copy-start | bytes 5898244
  116.4 7.4 %collective-permute-start.22 = (bf16[64,1280]{1,0:T(8,128)(2,1)}, bf16[64,1280]{1,0:T(8,128)(2,1)S(1)}, u32[]{:S(2)}, u32[]{:S(2)}) collective-permute-start(bf16[64,1280]{1,0:T(8,128)(2,1)} %get-tuple-element.106), channel_id=1, source_target_pairs={{0,1},{1,0},{2,3},{3,2},{4,5},{5,4},{6,7},{7,6},{8,9},{9,8},{10,11... | collective-permute-start | bytes 491528 | tf_op jit(solution)/shard_map/ppermute | solution.py:399
  117.3 11.5 %collective-permute-start.21 = (bf16[64,1280]{1,0:T(8,128)(2,1)S(1)}, bf16[64,1280]{1,0:T(8,128)(2,1)S(1)}, u32[]{:S(2)}, u32[]{:S(2)}) collective-permute-start(bf16[64,1280]{1,0:T(8,128)(2,1)S(1)} %get-tuple-element.122), channel_id=1, source_target_pairs={{0,1},{1,0},{2,3},{3,2},{4,5},{5,4},{6,7},{7,6},{8,9},{9,8},{10,11... | collective-permute-start | bytes 491528 | tf_op jit(solution)/shard_map/ppermute | solution.py:399
  124.9 8.3 %collective-permute-start.23 = (bf16[64,1280]{1,0:T(8,128)(2,1)S(1)}, bf16[64,1280]{1,0:T(8,128)(2,1)S(1)}, u32[]{:S(2)}, u32[]{:S(2)}) collective-permute-start(bf16[64,1280]{1,0:T(8,128)(2,1)S(1)} %fusion.7), channel_id=1, source_target_pairs={{0,2},{1,3},{2,4},{3,5},{4,6},{5,7},{8,10},{9,11},{10,12},{11,13},... | collective-permute-start | bytes 491528 | tf_op jit(solution)/shard_map/ppermute | solution.py:399
  126.2 14.8 %collective-permute-start.24 = (bf16[64,1280]{1,0:T(8,128)(2,1)S(1)}, bf16[64,1280]{1,0:T(8,128)(2,1)S(1)}, u32[]{:S(2)}, u32[]{:S(2)}) collective-permute-start(bf16[64,1280]{1,0:T(8,128)(2,1)S(1)} %fusion.7), channel_id=1, source_target_pairs={{0,4},{1,5},{2,6},{3,7},{8,12},{9,13},{10,14},{11,15},{16,20},{17,... | collective-permute-start | bytes 491528 | tf_op jit(solution)/shard_map/ppermute | solution.py:399
  127.5 13.5 %collective-permute-start.25 = (bf16[64,1280]{1,0:T(8,128)(2,1)S(1)}, bf16[64,1280]{1,0:T(8,128)(2,1)S(1)}, u32[]{:S(2)}, u32[]{:S(2)}) collective-permute-start(bf16[64,1280]{1,0:T(8,128)(2,1)S(1)} %fusion.7), channel_id=1, source_target_pairs={{0,6},{1,7},{8,14},{9,15},{16,22},{17,23},{24,30},{25,31}} | collective-permute-start | bytes 491528 | tf_op jit(solution)/shard_map/ppermute | solution.py:399
  130.6 10.3 %copy-start.5 = (f32[64,1280]{1,0:T(8,128)S(1)}, f32[64,1280]{1,0:T(8,128)}, u32[]{:S(2)}) copy-start(f32[64,1280]{1,0:T(8,128)} %get-tuple-element.105) | copy-start | bytes 983044
  130.6 15.9 %copy-start.2 = (bf16[5,768,256]{2,1,0:T(8,128)(2,1)S(1)}, bf16[5,768,256]{2,1,0:T(8,128)(2,1)}, u32[]{:S(2)}) copy-start(bf16[5,768,256]{2,1,0:T(8,128)(2,1)} %get-tuple-element.94.refs_1_) | copy-start | bytes 5898244
  141.1 5.4 %collective-permute-start.26 = (bf16[64,1280]{1,0:T(8,128)(2,1)S(1)}, bf16[64,1280]{1,0:T(8,128)(2,1)S(1)}, u32[]{:S(2)}, u32[]{:S(2)}) collective-permute-start(bf16[64,1280]{1,0:T(8,128)(2,1)S(1)} %get-tuple-element.124), channel_id=1, source_target_pairs={{0,1},{1,0},{2,3},{3,2},{4,5},{5,4},{6,7},{7,6},{8,9},{9,8},{10,11... | collective-permute-start | bytes 491528 | tf_op jit(solution)/shard_map/ppermute | solution.py:399
  (1 other events, 0.7 us)
Sparse Core Ops, SparseCore 0:
  10.3 80.5 all-gather.1

commit v5 on v4

--- a/solution.py
+++ b/solution.py
@@ -10,7 +10,7 @@
 SPAN = 128
 TILE = 256
 RIM = 16
-VMEM = 56 * 1024 * 1024
+VMEM = 50 * 1024 * 1024
 SMALL = 16 * 1024 * 1024
 LOG2E = math.log2(math.e)
 BF16 = jnp.bfloat16
@@ -253,7 +253,8 @@
         state = jnp.concatenate([low, high], axis=0)
     carried = jnp.dot(c_ref[...], state, preferred_element_type=F32)
     ssd = y_ref[0].astype(F32) + reach_ref[0].astype(F32) * carried
-    mean = jnp.dot((ssd * ssd).astype(BF16), gather_ref[...], preferred_element_type=F32)
+    square = jnp.minimum(ssd * ssd, 1e38).astype(BF16)
+    mean = jnp.dot(square, gather_ref[...], preferred_element_type=F32)
     out_ref[...] = (ssd * lax.rsqrt(mean + 1e-05) * gain_ref[...]).astype(BF16)
 
 

time: 158 us -> 154 us (0.975)
  local copies, waits for them, and re-layouts: 10.1 us -> 6.54 us
  other arithmetic: 4.29 us -> 1.16 us
  starting transfers between devices: 29.5 us -> 31.3 us
    ppermute x16, waiting for transfers between devices: 19.1 us -> 21.3 us  [send(): return lax.ppermute(value, ('dp', 'seq'), pairs)]
    unnamed x51 -> x35, local copies, waits for them, and re-layouts: 3.37 us -> 1.67 us
  transfers between devices with their start and end apart: 28 -> 28, of which waited for: 8 -> 11; matrix products, arithmetic and copies ran while one was open for 6% -> 4% of each run, Pallas kernels for 33% -> 34%
where the time goes in v5:
time: 154 us
  Pallas kernels  56.1 us (36%)
  waiting for transfers between devices  44.2 us (29%)
  starting transfers between devices  31.3 us (20%)
  between operations  14.3 us (9%)
  local copies, waits for them, and re-layouts  6.54 us (4%)
    pallas_call x2, Pallas kernels, run_scan(): pl.pallas_call(lambda *refs: scan_kernel(leads, extras, tiles, len(pieces...  35.8 us
    ppermute x10, waiting for transfers between devices, shifted(): return lax.ppermute(value, 'seq', pairs)  22.9 us
    ppermute x16, waiting for transfers between devices, send(): return lax.ppermute(value, ('dp', 'seq'), pairs)  21.3 us
    ppermute x16, starting transfers between devices, send(): return lax.ppermute(value, ('dp', 'seq'), pairs)  16.7 us
    ppermute x10, starting transfers between devices, shifted(): return lax.ppermute(value, 'seq', pairs)  12.2 us
    pallas_call x1, Pallas kernels, run_decay(): pl.pallas_call(decay_kernel, grid=(tiles,), in_specs=[whole((tiles * coun...  12.2 us
    pallas_call x3, Pallas kernels, run_norm(): pl.pallas_call(lambda *refs: norm_kernel(len(state), *refs), grid=(tiles,...  8.14 us
  transfers between devices with their start and end apart: 28, of which 11 were waited for; matrix products, arithmetic and copies ran while one was open for 4% of the time, Pallas kernels for 34%

profile of v5, /device:TPU:24, one launch (start us, length us, event | category | flops | bytes accessed | tf_op | source)
XLA Modules:
  0.0 153.7 jit_solution(12344301752144940996)
XLA Ops:
  6.6 1.1 copy.40
  7.7 0.7 slice.90
  8.5 2.0 %collective-permute-start.1 = (bf16[1,6,80,256]{3,2,1,0:T(8,128)(2,1)S(1)}, bf16[1,6,80,256]{3,2,1,0:T(8,128)(2,1)S(1)}, u32[]{:S(2)}, u32[]{:S(2)}) collective-permute-start(bf16[1,6,80,256]{3,2,1,0:T(8,128)(2,1)S(1)} %slice.89), channel_id=1, source_target_pairs={{0,6},{1,7},{2,0},{3,1},{4,2},{5,3},{6,4},{7,5},{8,14},{9,15},{10,... | collective-permute-start | bytes 737288 | tf_op jit(solution)/shard_map/ppermute | solution.py:425
  10.5 1.5 collective-permute-start.2
  12.0 1.5 collective-permute-start.3
  13.6 0.9 slice_bitcast_fusion
  14.4 2.4 %collective-permute-start.8 = (bf16[16,2560]{1,0:T(8,128)(2,1)S(1)}, bf16[16,2560]{1,0:T(8,128)(2,1)S(1)}, u32[]{:S(2)}, u32[]{:S(2)}) collective-permute-start(bf16[16,2560]{1,0:T(8,128)(2,1)S(1)} %slice_bitcast_fusion), channel_id=1, source_target_pairs={{0,1},{1,2},{2,3},{3,4},{4,5},{5,6},{6,7},{8,9},{9,10},{10,11},{11... | collective-permute-start | bytes 245768 | tf_op jit(solution)/shard_map/ppermute | solution.py:491
  16.9 0.2 fusion.10
  17.1 0.2 multiply_reduce_fusion
  19.1 2.4 %collective-permute-done = bf16[1,6,80,256]{3,2,1,0:T(8,128)(2,1)S(1)} collective-permute-done((bf16[1,6,80,256]{3,2,1,0:T(8,128)(2,1)S(1)}, bf16[1,6,80,256]{3,2,1,0:T(8,128)(2,1)S(1)}, u32[]{:S(2)}, u32[]{:S(2)}) %collective-permute-start) | collective-permute-done | bytes 245792 | tf_op jit(solution)/shard_map/ppermute | solution.py:425
  21.5 0.7 constant_dynamic-update-slice_fusion.10
  22.2 0.7 constant_dynamic-update-slice_fusion.9
  23.0 1.5 collective-permute-start.5
  24.4 2.9 %collective-permute-start.6 = (bf16[2,6,80,256]{3,2,1,0:T(8,128)(2,1)S(1)}, bf16[2,6,80,256]{3,2,1,0:T(8,128)(2,1)S(1)}, u32[]{:S(2)}, u32[]{:S(2)}) collective-permute-start(bf16[2,6,80,256]{3,2,1,0:T(8,128)(2,1)S(1)} %get-tuple-element.127), channel_id=1, source_target_pairs={{0,1},{1,0},{2,3},{3,2},{4,5},{5,4},{6,7},{7,6},{8,24},{9,25},{10,... | collective-permute-start | bytes 1474568 | tf_op jit(solution)/shard_map/ppermute | solution.py:425
  27.3 0.3 collective-permute-start.7
  27.7 11.9 %collective-permute-done.4 = bf16[1,6,80,256]{3,2,1,0:T(8,128)(2,1)S(1)} collective-permute-done((bf16[1,6,80,256]{3,2,1,0:T(8,128)(2,1)S(1)}, bf16[1,6,80,256]{3,2,1,0:T(8,128)(2,1)S(1)}, u32[]{:S(2)}, u32[]{:S(2)}) %collective-permute-start.4) | collective-permute-done | bytes 245792 | tf_op jit(solution)/shard_map/ppermute | solution.py:425
  39.7 1.2 collective-permute-start.10
  40.9 0.9 collective-permute-start.9
  42.0 0.7 constant_dynamic-update-slice_fusion.2.refs_2_
  42.7 1.2 collective-permute-start.11
  43.9 12.2 %decays.1 = (bf16[10,2,768,256]{3,2,1,0:T(8,128)(2,1)}, bf16[10,768,256]{2,1,0:T(8,128)(2,1)}, bf16[10,768,256]{2,1,0:T(8,128)(2,1)}, f32[10,16,256]{2,1,0:T(8,128)S(1)}) custom-call(f32[240,128]{1,0:T(8,128)S(1)} %bitcast.58, f32[240,1]{1,0:T(8,128)S(1)} %reshape.75.rate_ref), custom_call_target="tpu_custom_call" | custom-call | flops 10000000000 | bytes 16000000 | tf_op jit(solution)/shard_map/decays/pallas_call | solution.py:276
  56.1 0.5 collective-permute-done.11
  56.6 2.2 %collective-permute-start.14 = (bf16[8,6,80,256]{3,2,1,0:T(8,128)(2,1)S(1)}, bf16[8,6,80,256]{3,2,1,0:T(8,128)(2,1)S(1)}, u32[]{:S(2)}, u32[]{:S(2)}) collective-permute-start(bf16[8,6,80,256]{3,2,1,0:T(8,128)(2,1)S(1)} %constant_dynamic-update-slice_fusion.6.refs_3_), channel_id=1, source_target_pairs={{0,8},{1,9},{2,10},{3,11},{4,12},{5,13},{6,14},{7,15},{8,0},{9,1},... | collective-permute-start | bytes 5898248 | tf_op jit(solution)/shard_map/ppermute | solution.py:425
  59.0 1.2 collective-permute-start.13
  60.3 5.0 %collective-permute-done.13.refs_5_ = bf16[1,6,80,256]{3,2,1,0:T(8,128)(2,1)S(1)} collective-permute-done((bf16[1,6,80,256]{3,2,1,0:T(8,128)(2,1)S(1)}, bf16[1,6,80,256]{3,2,1,0:T(8,128)(2,1)S(1)}, u32[]{:S(2)}, u32[]{:S(2)}) %collective-permute-start.13) | collective-permute-done | bytes 245792 | tf_op jit(solution)/shard_map/ppermute | solution.py:425
  65.4 1.5 collective-permute-done.16.refs_9_
  66.9 20.4 %project_scan.2 = (bf16[5,768,256]{2,1,0:T(8,128)(2,1)}, f32[64,1280]{1,0:T(8,128)S(1)}, bf16[80,1280]{1,0:T(8,128)(2,1)S(1)}, bf16[768,128]{1,0:T(8,128)(2,1)S(...) custom-call(s32[32]{0:T(128)S(1)} %get-tuple-element.63.refs_0_, s32[1]{0:T(128)} %bitcast.refs_1_.refs_0_, ...), custom_call_target="tpu_custom_call" | custom-call | flops 15000000512 | bytes 15000000 | tf_op jit(solution)/shard_map/project_scan/pallas_call | solution.py:348
  87.3 1.2 collective-permute-start.17
  88.6 6.0 %collective-permute-done.17 = bf16[80,1280]{1,0:T(8,128)(2,1)S(1)} collective-permute-done((bf16[80,1280]{1,0:T(8,128)(2,1)S(1)}, bf16[80,1280]{1,0:T(8,128)(2,1)S(1)}, u32[]{:S(2)}, u32[]{:S(2)}) %collective-permute-start.17) | collective-permute-done | bytes 204832 | tf_op jit(solution)/shard_map/ppermute | solution.py:400
  94.8 1.3 collective-permute-start.18
  96.1 1.3 collective-permute-start.19
  97.4 1.3 collective-permute-start.20
  98.7 15.4 %project_scan.3 = (bf16[5,768,256]{2,1,0:T(8,128)(2,1)S(1)}, f32[64,1280]{1,0:T(8,128)S(1)}, bf16[64,1280]{1,0:T(8,128)(2,1)S(1)}) custom-call(s32[32]{0:T(128)S(1)} %get-tuple-element.62.refs_0_, s32[1]{0:T(128)} %bitcast.refs_1_.refs_0_, bf16[32,5,80,256]{3,2,1,0:T(8,128)(2,1)} %all-gather.2.cloned.1.call-done.refs_2_, ...), custom_call_target="tpu_custom_call" | custom-call | flops 15000000512 | bytes 15000000 | tf_op jit(solution)/shard_map/project_scan/pallas_call | solution.py:348
  114.1 0.9 collective-permute-done.19
  115.0 1.2 collective-permute-start.22
  116.3 0.2 select_convert_fusion.2
  116.5 0.9 collective-permute-start.21
  117.4 4.6 %collective-permute-done.22 = bf16[64,1280]{1,0:T(8,128)(2,1)S(1)} collective-permute-done((bf16[64,1280]{1,0:T(8,128)(2,1)S(1)}, bf16[64,1280]{1,0:T(8,128)(2,1)S(1)}, u32[]{:S(2)}, u32[]{:S(2)}) %collective-permute-start.22) | collective-permute-done | bytes 163872 | tf_op jit(solution)/shard_map/ppermute | solution.py:400
  122.1 1.3 collective-permute-start.23
  123.4 1.3 collective-permute-start.24
  124.7 1.3 collective-permute-start.25
  126.0 1.8 %head_norm.3.refs_8_ = bf16[768,2560]{1,0:T(8,128)(2,1)} custom-call(s32[1]{0:T(128)} %bitcast.refs_1_.refs_0_, bf16[5,768,256]{2,1,0:T(8,128)(2,1)S(1)} %copy-done.1, bf16[768,128]{1,0:T(8,128)(2,1)S(1)} %get-tuple-element.91.refs_11_.refs_2_, bf16[10,768,256]{2,1,0:T(8,128)(2,1)S(1)} %copy-done, f32[1,2560]{1,0:T(1,128)S(1)} %broadcast_in_dim.65.refs_4_, ...), custom_call_target="tpu_custom_call" | custom-call | flops 800000000 | bytes 1966080 | tf_op jit(solution)/shard_map/head_norm/pallas_call | solution.py:382
  127.9 2.5 %head_norm.4.refs_8_ = bf16[768,2560]{1,0:T(8,128)(2,1)} custom-call(s32[1]{0:T(128)} %bitcast.refs_1_.refs_0_, bf16[5,768,256]{2,1,0:T(8,128)(2,1)S(1)} %copy-done.1, bf16[768,128]{1,0:T(8,128)(2,1)S(1)} %get-tuple-element.91.refs_11_.refs_2_, bf16[10,768,256]{2,1,0:T(8,128)(2,1)S(1)} %copy-done, ...), custom_call_target="tpu_custom_call", output_to_operand_aliasing={{}: (8, {})} | custom-call | flops 1200000000 | bytes 2949120 | tf_op jit(solution)/shard_map/head_norm/pallas_call | solution.py:382
  130.4 0.3 collective-permute-done.23
  130.7 6.8 %collective-permute-done.24 = bf16[64,1280]{1,0:T(8,128)(2,1)S(1)} collective-permute-done((bf16[64,1280]{1,0:T(8,128)(2,1)S(1)}, bf16[64,1280]{1,0:T(8,128)(2,1)S(1)}, u32[]{:S(2)}, u32[]{:S(2)}) %collective-permute-start.24) | collective-permute-done | bytes 163872 | tf_op jit(solution)/shard_map/ppermute | solution.py:400
  137.7 1.2 collective-permute-start.26
  138.8 4.2 %collective-permute-done.26.refs_7_ = bf16[64,1280]{1,0:T(8,128)(2,1)S(1)} collective-permute-done((bf16[64,1280]{1,0:T(8,128)(2,1)S(1)}, bf16[64,1280]{1,0:T(8,128)(2,1)S(1)}, u32[]{:S(2)}, u32[]{:S(2)}) %collective-permute-start.26) | collective-permute-done | bytes 163872 | tf_op jit(solution)/shard_map/ppermute | solution.py:400
  143.0 3.8 %head_norm.5 = bf16[768,2560]{1,0:T(8,128)(2,1)} custom-call(s32[1]{0:T(128)} %bitcast.refs_1_.refs_0_, bf16[5,768,256]{2,1,0:T(8,128)(2,1)S(1)} %get-tuple-element.94.refs_1_, bf16[768,128]{1,0:T(8,128)(2,1)S(1)} %get-tuple-element.91.refs_11_.refs_2_, bf16[10,768,256]{2,1,0:T(8,128)(2,1)S(1)} %copy-done, ...), custom_call_target="tpu_custom_call", output_to_operand_aliasing={{}: (8, {})} | custom-call | flops 2000000000 | bytes 4915200 | tf_op jit(solution)/shard_map/head_norm/pallas_call | solution.py:382
  (102 shorter events, 2.6 us)
Async XLA Ops:
  6.5 10.3 %copy-start.2 = (f32[1,40,768]{2,1,0:T(8,128)S(1)}, f32[1,40,768]{2,1,0:T(8,128)}, u32[]{:S(2)}) copy-start(f32[1,40,768]{2,1,0:T(8,128)} %param.13) | copy-start | bytes 368644
  6.5 10.5 %copy-start.12 = (f32[40]{0:T(128)S(1)}, f32[40]{0:T(128)}, u32[]{:S(2)}) copy-start(f32[40]{0:T(128)} %param.12) | copy-start | bytes 484
  6.5 11.2 %copy-start.7 = (f32[2816]{0:T(1024)S(1)}, f32[2816]{0:T(1024)}, u32[]{:S(2)}) copy-start(f32[2816]{0:T(1024)} %param.11) | copy-start | bytes 33796
  6.5 11.3 %copy-start.9 = (f32[40]{0:T(128)S(1)}, f32[40]{0:T(128)}, u32[]{:S(2)}) copy-start(f32[40]{0:T(128)} %param.14) | copy-start | bytes 484
  6.5 11.4 %copy-start.4 = (f32[4,2816]{1,0:T(4,128)S(1)}, f32[4,2816]{1,0:T(4,128)}, u32[]{:S(2)}) copy-start(f32[4,2816]{1,0:T(4,128)} %param.10) | copy-start | bytes 135172
  6.5 88.1 %all-gather.2.cloned.1.call-start = ((), (), s32[]{:S(2)}) async-start(), calls=%async_computation | async-start | bytes 6758400 | tf_op jit(solution)/shard_map/all_gather | solution.py:528
  8.5 13.0 %collective-permute-start = (bf16[1,6,80,256]{3,2,1,0:T(8,128)(2,1)S(1)}, bf16[1,6,80,256]{3,2,1,0:T(8,128)(2,1)S(1)}, u32[]{:S(2)}, u32[]{:S(2)}) collective-permute-start(bf16[1,6,80,256]{3,2,1,0:T(8,128)(2,1)S(1)} %slice.89), channel_id=1, source_target_pairs={{0,2},{1,3},{2,4},{3,5},{4,6},{5,7},{6,0},{7,1},{8,10},{9,11},{10,... | collective-permute-start | bytes 737288 | tf_op jit(solution)/shard_map/ppermute | solution.py:425
  8.5 13.0 %collective-permute-start.1 = (bf16[1,6,80,256]{3,2,1,0:T(8,128)(2,1)S(1)}, bf16[1,6,80,256]{3,2,1,0:T(8,128)(2,1)S(1)}, u32[]{:S(2)}, u32[]{:S(2)}) collective-permute-start(bf16[1,6,80,256]{3,2,1,0:T(8,128)(2,1)S(1)} %slice.89), channel_id=1, source_target_pairs={{0,6},{1,7},{2,0},{3,1},{4,2},{5,3},{6,4},{7,5},{8,14},{9,15},{10,... | collective-permute-start | bytes 737288 | tf_op jit(solution)/shard_map/ppermute | solution.py:425
  10.5 10.9 %collective-permute-start.2 = (bf16[1,6,80,256]{3,2,1,0:T(8,128)(2,1)S(1)}, bf16[1,6,80,256]{3,2,1,0:T(8,128)(2,1)S(1)}, u32[]{:S(2)}, u32[]{:S(2)}) collective-permute-start(bf16[1,6,80,256]{3,2,1,0:T(8,128)(2,1)S(1)} %slice.89), channel_id=1, source_target_pairs={{0,16},{1,17},{2,18},{3,19},{4,20},{5,21},{6,22},{7,23},{8,9},{9,8... | collective-permute-start | bytes 737288 | tf_op jit(solution)/shard_map/ppermute | solution.py:425
  12.0 9.5 %collective-permute-start.3 = (bf16[1,6,80,256]{3,2,1,0:T(8,128)(2,1)S(1)}, bf16[1,6,80,256]{3,2,1,0:T(8,128)(2,1)S(1)}, u32[]{:S(2)}, u32[]{:S(2)}) collective-permute-start(bf16[1,6,80,256]{3,2,1,0:T(8,128)(2,1)S(1)} %slice.89), channel_id=1, source_target_pairs={{0,1},{1,0},{2,3},{3,2},{4,5},{5,4},{6,7},{7,6},{8,24},{9,25},{10,... | collective-permute-start | bytes 737288 | tf_op jit(solution)/shard_map/ppermute | solution.py:425
  14.4 13.3 %collective-permute-start.8 = (bf16[16,2560]{1,0:T(8,128)(2,1)S(1)}, bf16[16,2560]{1,0:T(8,128)(2,1)S(1)}, u32[]{:S(2)}, u32[]{:S(2)}) collective-permute-start(bf16[16,2560]{1,0:T(8,128)(2,1)S(1)} %slice_bitcast_fusion), channel_id=1, source_target_pairs={{0,1},{1,2},{2,3},{3,4},{4,5},{5,6},{6,7},{8,9},{9,10},{10,11},{11... | collective-permute-start | bytes 245768 | tf_op jit(solution)/shard_map/ppermute | solution.py:491
  23.0 16.7 %collective-permute-start.5 = (bf16[2,6,80,256]{3,2,1,0:T(8,128)(2,1)S(1)}, bf16[2,6,80,256]{3,2,1,0:T(8,128)(2,1)S(1)}, u32[]{:S(2)}, u32[]{:S(2)}) collective-permute-start(bf16[2,6,80,256]{3,2,1,0:T(8,128)(2,1)S(1)} %get-tuple-element.127), channel_id=1, source_target_pairs={{0,16},{1,17},{2,18},{3,19},{4,20},{5,21},{6,22},{7,23},{8,9},{9,8... | collective-permute-start | bytes 1474568 | tf_op jit(solution)/shard_map/ppermute | solution.py:425
  24.4 15.2 %collective-permute-start.6 = (bf16[2,6,80,256]{3,2,1,0:T(8,128)(2,1)S(1)}, bf16[2,6,80,256]{3,2,1,0:T(8,128)(2,1)S(1)}, u32[]{:S(2)}, u32[]{:S(2)}) collective-permute-start(bf16[2,6,80,256]{3,2,1,0:T(8,128)(2,1)S(1)} %get-tuple-element.127), channel_id=1, source_target_pairs={{0,1},{1,0},{2,3},{3,2},{4,5},{5,4},{6,7},{7,6},{8,24},{9,25},{10,... | collective-permute-start | bytes 1474568 | tf_op jit(solution)/shard_map/ppermute | solution.py:425
  27.3 12.3 %collective-permute-start.4 = (bf16[1,6,80,256]{3,2,1,0:T(8,128)(2,1)S(1)}, bf16[1,6,80,256]{3,2,1,0:T(8,128)(2,1)S(1)}, u32[]{:S(2)}, u32[]{:S(2)}) collective-permute-start(bf16[1,6,80,256]{3,2,1,0:T(8,128)(2,1)S(1)} %slice.89), channel_id=1, source_target_pairs={{0,4},{1,5},{2,6},{3,7},{4,0},{5,1},{6,2},{7,3},{8,12},{9,13},{10,... | collective-permute-start | bytes 737288 | tf_op jit(solution)/shard_map/ppermute | solution.py:425
  27.3 12.3 %collective-permute-start.7 = (bf16[1,6,80,256]{3,2,1,0:T(8,128)(2,1)S(1)}, bf16[1,6,80,256]{3,2,1,0:T(8,128)(2,1)S(1)}, u32[]{:S(2)}, u32[]{:S(2)}) collective-permute-start(bf16[1,6,80,256]{3,2,1,0:T(8,128)(2,1)S(1)} %collective-permute-done.2), channel_id=1, source_target_pairs={{0,1},{1,0},{2,3},{3,2},{4,5},{5,4},{6,7},{7,6},{8,24},{9,25},{10,... | collective-permute-start | bytes 737288 | tf_op jit(solution)/shard_map/ppermute | solution.py:425
  27.7 12.0 %copy-start.3 = (bf16[4,6,80,256]{3,2,1,0:T(8,128)(2,1)}, bf16[4,6,80,256]{3,2,1,0:T(8,128)(2,1)S(1)}, u32[]{:S(2)}) copy-start(bf16[4,6,80,256]{3,2,1,0:T(8,128)(2,1)S(1)} %constant_dynamic-update-slice_fusion.3) | copy-start | bytes 2949124
  39.7 16.4 %collective-permute-start.10 = (bf16[1,6,80,256]{3,2,1,0:T(8,128)(2,1)S(1)}, bf16[1,6,80,256]{3,2,1,0:T(8,128)(2,1)S(1)}, u32[]{:S(2)}, u32[]{:S(2)}) collective-permute-start(bf16[1,6,80,256]{3,2,1,0:T(8,128)(2,1)S(1)} %collective-permute-done.4), channel_id=1, source_target_pairs={{0,1},{1,0},{2,3},{3,2},{4,5},{5,4},{6,7},{7,6},{8,24},{9,25},{10,... | collective-permute-start | bytes 737288 | tf_op jit(solution)/shard_map/ppermute | solution.py:425
  40.9 15.2 %collective-permute-start.9 = (bf16[1,6,80,256]{3,2,1,0:T(8,128)(2,1)S(1)}, bf16[1,6,80,256]{3,2,1,0:T(8,128)(2,1)S(1)}, u32[]{:S(2)}, u32[]{:S(2)}) collective-permute-start(bf16[1,6,80,256]{3,2,1,0:T(8,128)(2,1)S(1)} %collective-permute-done.4), channel_id=1, source_target_pairs={{0,16},{1,17},{2,18},{3,19},{4,20},{5,21},{6,22},{7,23},{8,9},{9,8... | collective-permute-start | bytes 737288 | tf_op jit(solution)/shard_map/ppermute | solution.py:425
  42.7 13.9 %collective-permute-start.12 = (bf16[4,6,80,256]{3,2,1,0:T(8,128)(2,1)}, bf16[4,6,80,256]{3,2,1,0:T(8,128)(2,1)S(1)}, u32[]{:S(2)}, u32[]{:S(2)}) collective-permute-start(bf16[4,6,80,256]{3,2,1,0:T(8,128)(2,1)} %constant_dynamic-update-slice_fusion.2.refs_2_), channel_id=1, source_target_pairs={{0,8},{1,9},{2,10},{3,11},{4,12},{5,13},{6,14},{7,15},{8,0},{9,1},... | collective-permute-start | bytes 2949128 | tf_op jit(solution)/shard_map/ppermute | solution.py:425
  42.7 13.9 %collective-permute-start.11 = (bf16[2,6,80,256]{3,2,1,0:T(8,128)(2,1)S(1)}, bf16[2,6,80,256]{3,2,1,0:T(8,128)(2,1)S(1)}, u32[]{:S(2)}, u32[]{:S(2)}) collective-permute-start(bf16[2,6,80,256]{3,2,1,0:T(8,128)(2,1)S(1)} %collective-permute-done.5), channel_id=1, source_target_pairs={{0,1},{1,0},{2,3},{3,2},{4,5},{5,4},{6,7},{7,6},{8,24},{9,25},{10,... | collective-permute-start | bytes 1474568 | tf_op jit(solution)/shard_map/ppermute | solution.py:425
  43.9 12.2 %copy-start.5 = (bf16[8,6,80,256]{3,2,1,0:T(8,128)(2,1)S(1)}, bf16[8,6,80,256]{3,2,1,0:T(8,128)(2,1)}, u32[]{:S(2)}) copy-start(bf16[8,6,80,256]{3,2,1,0:T(8,128)(2,1)} %get-tuple-element.126) | copy-start | bytes 5898244
  56.6 10.3 %copy-start.11 = (bf16[4,6,80,256]{3,2,1,0:T(8,128)(2,1)}, bf16[4,6,80,256]{3,2,1,0:T(8,128)(2,1)S(1)}, u32[]{:S(2)}) copy-start(bf16[4,6,80,256]{3,2,1,0:T(8,128)(2,1)S(1)} %collective-permute-done.12.refs_6_) | copy-start | bytes 2949124
  56.6 10.3 %copy-start.6 = (bf16[8,6,80,256]{3,2,1,0:T(8,128)(2,1)}, bf16[8,6,80,256]{3,2,1,0:T(8,128)(2,1)S(1)}, u32[]{:S(2)}) copy-start(bf16[8,6,80,256]{3,2,1,0:T(8,128)(2,1)S(1)} %constant_dynamic-update-slice_fusion.6.refs_3_) | copy-start | bytes 5898244
  56.6 8.7 %collective-permute-start.14 = (bf16[8,6,80,256]{3,2,1,0:T(8,128)(2,1)S(1)}, bf16[8,6,80,256]{3,2,1,0:T(8,128)(2,1)S(1)}, u32[]{:S(2)}, u32[]{:S(2)}) collective-permute-start(bf16[8,6,80,256]{3,2,1,0:T(8,128)(2,1)S(1)} %constant_dynamic-update-slice_fusion.6.refs_3_), channel_id=1, source_target_pairs={{0,8},{1,9},{2,10},{3,11},{4,12},{5,13},{6,14},{7,15},{8,0},{9,1},... | collective-permute-start | bytes 5898248 | tf_op jit(solution)/shard_map/ppermute | solution.py:425
  59.0 6.3 %collective-permute-start.15 = (bf16[3,6,80,256]{3,2,1,0:T(8,128)(2,1)S(1)}, bf16[3,6,80,256]{3,2,1,0:T(8,128)(2,1)S(1)}, u32[]{:S(2)}, u32[]{:S(2)}) collective-permute-start(bf16[3,6,80,256]{3,2,1,0:T(8,128)(2,1)S(1)} %constant_dynamic-update-slice_fusion.11.refs_4_), channel_id=1, source_target_pairs={{0,8},{1,9},{2,10},{3,11},{4,12},{5,13},{6,14},{7,15},{8,0},{9,1},... | collective-permute-start | bytes 2211848 | tf_op jit(solution)/shard_map/ppermute | solution.py:425
  59.0 6.3 %collective-permute-start.13 = (bf16[1,6,80,256]{3,2,1,0:T(8,128)(2,1)S(1)}, bf16[1,6,80,256]{3,2,1,0:T(8,128)(2,1)S(1)}, u32[]{:S(2)}, u32[]{:S(2)}) collective-permute-start(bf16[1,6,80,256]{3,2,1,0:T(8,128)(2,1)S(1)} %collective-permute-done.9), channel_id=1, source_target_pairs={{0,1},{1,0},{2,3},{3,2},{4,5},{5,4},{6,7},{7,6},{8,24},{9,25},{10,... | collective-permute-start | bytes 737288 | tf_op jit(solution)/shard_map/ppermute | solution.py:425
  65.3 1.6 %copy-start.10 = (bf16[8,6,80,256]{3,2,1,0:T(8,128)(2,1)}, bf16[8,6,80,256]{3,2,1,0:T(8,128)(2,1)S(1)}, u32[]{:S(2)}) copy-start(bf16[8,6,80,256]{3,2,1,0:T(8,128)(2,1)S(1)} %collective-permute-done.14.refs_7_) | copy-start | bytes 5898244
  65.3 1.6 %collective-permute-start.16 = (bf16[1,6,80,256]{3,2,1,0:T(8,128)(2,1)S(1)}, bf16[1,6,80,256]{3,2,1,0:T(8,128)(2,1)S(1)}, u32[]{:S(2)}, u32[]{:S(2)}) collective-permute-start(bf16[1,6,80,256]{3,2,1,0:T(8,128)(2,1)S(1)} %collective-permute-done.13.refs_5_), channel_id=1, source_target_pairs={{0,8},{1,9},{2,10},{3,11},{4,12},{5,13},{6,14},{7,15},{8,0},{9,1},... | collective-permute-start | bytes 737288 | tf_op jit(solution)/shard_map/ppermute | solution.py:425
  66.9 21.6 %copy-start.8 = (f32[2560]{0:T(1024)S(1)}, f32[2560]{0:T(1024)}, u32[]{:S(2)}) copy-start(f32[2560]{0:T(1024)} %param.15) | copy-start | bytes 30724
  87.3 7.2 %collective-permute-start.17 = (bf16[80,1280]{1,0:T(8,128)(2,1)S(1)}, bf16[80,1280]{1,0:T(8,128)(2,1)S(1)}, u32[]{:S(2)}, u32[]{:S(2)}) collective-permute-start(bf16[80,1280]{1,0:T(8,128)(2,1)S(1)} %get-tuple-element.89), channel_id=1, source_target_pairs={{0,1},{1,0},{2,3},{3,2},{4,5},{5,4},{6,7},{7,6},{8,9},{9,8},{10,11... | collective-permute-start | bytes 614408 | tf_op jit(solution)/shard_map/ppermute | solution.py:400
  94.8 19.3 %collective-permute-start.18 = (bf16[80,1280]{1,0:T(8,128)(2,1)S(1)}, bf16[80,1280]{1,0:T(8,128)(2,1)S(1)}, u32[]{:S(2)}, u32[]{:S(2)}) collective-permute-start(bf16[80,1280]{1,0:T(8,128)(2,1)S(1)} %fusion.9), channel_id=1, source_target_pairs={{0,2},{1,3},{2,4},{3,5},{4,6},{5,7},{8,10},{9,11},{10,12},{11,13},... | collective-permute-start | bytes 614408 | tf_op jit(solution)/shard_map/ppermute | solution.py:400
  96.1 19.0 %collective-permute-start.19 = (bf16[80,1280]{1,0:T(8,128)(2,1)S(1)}, bf16[80,1280]{1,0:T(8,128)(2,1)S(1)}, u32[]{:S(2)}, u32[]{:S(2)}) collective-permute-start(bf16[80,1280]{1,0:T(8,128)(2,1)S(1)} %fusion.9), channel_id=1, source_target_pairs={{0,4},{1,5},{2,6},{3,7},{8,12},{9,13},{10,14},{11,15},{16,20},{17,... | collective-permute-start | bytes 614408 | tf_op jit(solution)/shard_map/ppermute | solution.py:400
  97.4 17.7 %collective-permute-start.20 = (bf16[80,1280]{1,0:T(8,128)(2,1)S(1)}, bf16[80,1280]{1,0:T(8,128)(2,1)S(1)}, u32[]{:S(2)}, u32[]{:S(2)}) collective-permute-start(bf16[80,1280]{1,0:T(8,128)(2,1)S(1)} %fusion.9), channel_id=1, source_target_pairs={{0,6},{1,7},{8,14},{9,15},{16,22},{17,23},{24,30},{25,31}} | collective-permute-start | bytes 614408 | tf_op jit(solution)/shard_map/ppermute | solution.py:400
  98.7 27.3 %copy-start = (bf16[10,768,256]{2,1,0:T(8,128)(2,1)S(1)}, bf16[10,768,256]{2,1,0:T(8,128)(2,1)}, u32[]{:S(2)}) copy-start(bf16[10,768,256]{2,1,0:T(8,128)(2,1)} %get-tuple-element.95.refs_3_) | copy-start | bytes 11796484
  114.1 11.9 %copy-start.1 = (bf16[5,768,256]{2,1,0:T(8,128)(2,1)S(1)}, bf16[5,768,256]{2,1,0:T(8,128)(2,1)}, u32[]{:S(2)}) copy-start(bf16[5,768,256]{2,1,0:T(8,128)(2,1)} %get-tuple-element.98.refs_1_) | copy-start | bytes 5898244
  115.0 7.0 %collective-permute-start.22 = (bf16[64,1280]{1,0:T(8,128)(2,1)S(1)}, bf16[64,1280]{1,0:T(8,128)(2,1)S(1)}, u32[]{:S(2)}, u32[]{:S(2)}) collective-permute-start(bf16[64,1280]{1,0:T(8,128)(2,1)S(1)} %get-tuple-element.106), channel_id=1, source_target_pairs={{0,1},{1,0},{2,3},{3,2},{4,5},{5,4},{6,7},{7,6},{8,9},{9,8},{10,11... | collective-permute-start | bytes 491528 | tf_op jit(solution)/shard_map/ppermute | solution.py:400
  116.5 9.5 %collective-permute-start.21 = (bf16[64,1280]{1,0:T(8,128)(2,1)S(1)}, bf16[64,1280]{1,0:T(8,128)(2,1)S(1)}, u32[]{:S(2)}, u32[]{:S(2)}) collective-permute-start(bf16[64,1280]{1,0:T(8,128)(2,1)S(1)} %get-tuple-element.122), channel_id=1, source_target_pairs={{0,1},{1,0},{2,3},{3,2},{4,5},{5,4},{6,7},{7,6},{8,9},{9,8},{10,11... | collective-permute-start | bytes 491528 | tf_op jit(solution)/shard_map/ppermute | solution.py:400
  122.1 8.6 %collective-permute-start.23 = (bf16[64,1280]{1,0:T(8,128)(2,1)S(1)}, bf16[64,1280]{1,0:T(8,128)(2,1)S(1)}, u32[]{:S(2)}, u32[]{:S(2)}) collective-permute-start(bf16[64,1280]{1,0:T(8,128)(2,1)S(1)} %fusion.7), channel_id=1, source_target_pairs={{0,2},{1,3},{2,4},{3,5},{4,6},{5,7},{8,10},{9,11},{10,12},{11,13},... | collective-permute-start | bytes 491528 | tf_op jit(solution)/shard_map/ppermute | solution.py:400
  123.4 14.1 %collective-permute-start.24 = (bf16[64,1280]{1,0:T(8,128)(2,1)S(1)}, bf16[64,1280]{1,0:T(8,128)(2,1)S(1)}, u32[]{:S(2)}, u32[]{:S(2)}) collective-permute-start(bf16[64,1280]{1,0:T(8,128)(2,1)S(1)} %fusion.7), channel_id=1, source_target_pairs={{0,4},{1,5},{2,6},{3,7},{8,12},{9,13},{10,14},{11,15},{16,20},{17,... | collective-permute-start | bytes 491528 | tf_op jit(solution)/shard_map/ppermute | solution.py:400
  124.7 12.8 %collective-permute-start.25 = (bf16[64,1280]{1,0:T(8,128)(2,1)S(1)}, bf16[64,1280]{1,0:T(8,128)(2,1)S(1)}, u32[]{:S(2)}, u32[]{:S(2)}) collective-permute-start(bf16[64,1280]{1,0:T(8,128)(2,1)S(1)} %fusion.7), channel_id=1, source_target_pairs={{0,6},{1,7},{8,14},{9,15},{16,22},{17,23},{24,30},{25,31}} | collective-permute-start | bytes 491528 | tf_op jit(solution)/shard_map/ppermute | solution.py:400
  137.7 5.4 %collective-permute-start.26 = (bf16[64,1280]{1,0:T(8,128)(2,1)S(1)}, bf16[64,1280]{1,0:T(8,128)(2,1)S(1)}, u32[]{:S(2)}, u32[]{:S(2)}) collective-permute-start(bf16[64,1280]{1,0:T(8,128)(2,1)S(1)} %get-tuple-element.124), channel_id=1, source_target_pairs={{0,1},{1,0},{2,3},{3,2},{4,5},{5,4},{6,7},{7,6},{8,9},{9,8},{10,11... | collective-permute-start | bytes 491528 | tf_op jit(solution)/shard_map/ppermute | solution.py:400
Sparse Core Ops, SparseCore 0:
  10.3 80.0 all-gather.1

commit v6 on v5

--- a/solution.py
+++ b/solution.py
@@ -10,7 +10,7 @@
 SPAN = 128
 TILE = 256
 RIM = 16
-VMEM = 50 * 1024 * 1024
+VMEM = 48 * 1024 * 1024
 SMALL = 16 * 1024 * 1024
 LOG2E = math.log2(math.e)
 BF16 = jnp.bfloat16

time: 154 us -> 156 us (1.013)
  Pallas kernels: 56.1 us -> 57.8 us
  local copies, waits for them, and re-layouts: 6.54 us -> 8.16 us
    pallas_call x2, Pallas kernels: 35.8 us -> 38.1 us  [run_scan(): pl.pallas_call(lambda *refs: scan_kernel(leads, extras, tiles, len(pieces...]
  transfers between devices with their start and end apart: 28 -> 28, of which waited for: 11 -> 10; matrix products, arithmetic and copies ran while one was open for 4% -> 5% of each run, Pallas kernels for 34% -> 35%
where the time goes in v6:
time: 156 us
  Pallas kernels  57.8 us (37%)
  waiting for transfers between devices  43.8 us (28%)
  starting transfers between devices  30.6 us (20%)
  between operations  14.3 us (9%)
  local copies, waits for them, and re-layouts  8.16 us (5%)
    pallas_call x2, Pallas kernels, run_scan(): pl.pallas_call(lambda *refs: scan_kernel(leads, extras, tiles, len(pieces...  38.1 us
    ppermute x10, waiting for transfers between devices, shifted(): return lax.ppermute(value, 'seq', pairs)  22.9 us
    ppermute x16, waiting for transfers between devices, send(): return lax.ppermute(value, ('dp', 'seq'), pairs)  20.9 us
    ppermute x16, starting transfers between devices, send(): return lax.ppermute(value, ('dp', 'seq'), pairs)  15.9 us
    ppermute x10, starting transfers between devices, shifted(): return lax.ppermute(value, 'seq', pairs)  12.2 us
    pallas_call x1, Pallas kernels, run_decay(): pl.pallas_call(decay_kernel, grid=(tiles,), in_specs=[whole((tiles * coun...  11.6 us
    pallas_call x3, Pallas kernels, run_norm(): pl.pallas_call(lambda *refs: norm_kernel(len(state), *refs), grid=(tiles,...  8.11 us
  transfers between devices with their start and end apart: 28, of which 10 were waited for; matrix products, arithmetic and copies ran while one was open for 5% of the time, Pallas kernels for 35%

profile of v6, /device:TPU:24, one launch (start us, length us, event | category | flops | bytes accessed | tf_op | source)
XLA Modules:
  0.0 155.9 jit_solution(1830843279608716759)
XLA Ops:
  6.6 1.1 copy.40
  7.7 0.7 slice.90
  8.5 2.0 %collective-permute-start.1 = (bf16[1,6,80,256]{3,2,1,0:T(8,128)(2,1)S(1)}, bf16[1,6,80,256]{3,2,1,0:T(8,128)(2,1)S(1)}, u32[]{:S(2)}, u32[]{:S(2)}) collective-permute-start(bf16[1,6,80,256]{3,2,1,0:T(8,128)(2,1)S(1)} %slice.89), channel_id=1, source_target_pairs={{0,6},{1,7},{2,0},{3,1},{4,2},{5,3},{6,4},{7,5},{8,14},{9,15},{10,... | collective-permute-start | bytes 737288 | tf_op jit(solution)/shard_map/ppermute | solution.py:425
  10.5 1.5 collective-permute-start.2
  12.0 1.5 collective-permute-start.3
  13.5 0.9 slice_bitcast_fusion
  14.4 2.4 %collective-permute-start.8 = (bf16[16,2560]{1,0:T(8,128)(2,1)S(1)}, bf16[16,2560]{1,0:T(8,128)(2,1)S(1)}, u32[]{:S(2)}, u32[]{:S(2)}) collective-permute-start(bf16[16,2560]{1,0:T(8,128)(2,1)S(1)} %slice_bitcast_fusion), channel_id=1, source_target_pairs={{0,1},{1,2},{2,3},{3,4},{4,5},{5,6},{6,7},{8,9},{9,10},{10,11},{11... | collective-permute-start | bytes 245768 | tf_op jit(solution)/shard_map/ppermute | solution.py:491
  16.9 0.2 fusion.10
  17.1 0.2 multiply_reduce_fusion
  19.1 2.4 %collective-permute-done = bf16[1,6,80,256]{3,2,1,0:T(8,128)(2,1)S(1)} collective-permute-done((bf16[1,6,80,256]{3,2,1,0:T(8,128)(2,1)S(1)}, bf16[1,6,80,256]{3,2,1,0:T(8,128)(2,1)S(1)}, u32[]{:S(2)}, u32[]{:S(2)}) %collective-permute-start) | collective-permute-done | bytes 245792 | tf_op jit(solution)/shard_map/ppermute | solution.py:425
  21.5 0.7 constant_dynamic-update-slice_fusion.10
  22.2 0.7 constant_dynamic-update-slice_fusion.9
  22.9 1.5 collective-permute-start.5
  24.4 2.9 %collective-permute-start.6 = (bf16[2,6,80,256]{3,2,1,0:T(8,128)(2,1)S(1)}, bf16[2,6,80,256]{3,2,1,0:T(8,128)(2,1)}, u32[]{:S(2)}, u32[]{:S(2)}) collective-permute-start(bf16[2,6,80,256]{3,2,1,0:T(8,128)(2,1)S(1)} %get-tuple-element.127), channel_id=1, source_target_pairs={{0,1},{1,0},{2,3},{3,2},{4,5},{5,4},{6,7},{7,6},{8,24},{9,25},{10,... | collective-permute-start | bytes 1474568 | tf_op jit(solution)/shard_map/ppermute | solution.py:425
  27.3 0.3 collective-permute-start.7
  27.7 11.9 %collective-permute-done.4 = bf16[1,6,80,256]{3,2,1,0:T(8,128)(2,1)S(1)} collective-permute-done((bf16[1,6,80,256]{3,2,1,0:T(8,128)(2,1)S(1)}, bf16[1,6,80,256]{3,2,1,0:T(8,128)(2,1)S(1)}, u32[]{:S(2)}, u32[]{:S(2)}) %collective-permute-start.4) | collective-permute-done | bytes 245792 | tf_op jit(solution)/shard_map/ppermute | solution.py:425
  39.7 1.2 collective-permute-start.10
  40.9 0.9 collective-permute-start.9
  42.0 1.0 constant_dynamic-update-slice_fusion.2.refs_2_
  43.0 1.2 collective-permute-start.11
  44.2 11.6 %decays.1 = (bf16[10,2,768,256]{3,2,1,0:T(8,128)(2,1)}, bf16[10,768,256]{2,1,0:T(8,128)(2,1)S(1)}, bf16[10,768,256]{2,1,0:T(8,128)(2,1)}, f32[10,16,256]{2,1,0:T(8,128)S(1)}) custom-call(f32[240,128]{1,0:T(8,128)S(1)} %bitcast.58, f32[240,1]{1,0:T(8,128)S(1)} %reshape.75.rate_ref), custom_call_target="tpu_custom_call" | custom-call | flops 10000000000 | bytes 16000000 | tf_op jit(solution)/shard_map/decays/pallas_call | solution.py:276
  55.9 1.4 constant_dynamic-update-slice_fusion.7
  57.4 1.4 collective-permute-start.14
  59.0 1.2 collective-permute-start.13
  60.2 5.1 %collective-permute-done.13.refs_5_ = bf16[1,6,80,256]{3,2,1,0:T(8,128)(2,1)S(1)} collective-permute-done((bf16[1,6,80,256]{3,2,1,0:T(8,128)(2,1)S(1)}, bf16[1,6,80,256]{3,2,1,0:T(8,128)(2,1)S(1)}, u32[]{:S(2)}, u32[]{:S(2)}) %collective-permute-start.13) | collective-permute-done | bytes 245792 | tf_op jit(solution)/shard_map/ppermute | solution.py:425
  65.4 1.5 collective-permute-done.16.refs_9_
  66.9 22.7 %project_scan.2 = (bf16[5,768,256]{2,1,0:T(8,128)(2,1)}, f32[64,1280]{1,0:T(8,128)S(1)}, bf16[80,1280]{1,0:T(8,128)(2,1)S(1)}, bf16[768,128]{1,0:T(8,128)(2,1)S(...) custom-call(s32[32]{0:T(128)S(1)} %get-tuple-element.63.refs_0_, s32[1]{0:T(128)} %bitcast.refs_1_.refs_0_, ...), custom_call_target="tpu_custom_call" | custom-call | flops 15000000512 | bytes 15000000 | tf_op jit(solution)/shard_map/project_scan/pallas_call | solution.py:348
  89.6 1.2 collective-permute-start.17
  90.8 6.0 %collective-permute-done.17 = bf16[80,1280]{1,0:T(8,128)(2,1)S(1)} collective-permute-done((bf16[80,1280]{1,0:T(8,128)(2,1)S(1)}, bf16[80,1280]{1,0:T(8,128)(2,1)S(1)}, u32[]{:S(2)}, u32[]{:S(2)}) %collective-permute-start.17) | collective-permute-done | bytes 204832 | tf_op jit(solution)/shard_map/ppermute | solution.py:400
  97.0 1.3 collective-permute-start.18
  98.3 1.3 collective-permute-start.19
  99.6 1.3 collective-permute-start.20
  100.9 15.4 %project_scan.3 = (bf16[5,768,256]{2,1,0:T(8,128)(2,1)S(1)}, f32[64,1280]{1,0:T(8,128)S(1)}, bf16[64,1280]{1,0:T(8,128)(2,1)S(1)}) custom-call(s32[32]{0:T(128)S(1)} %get-tuple-element.62.refs_0_, s32[1]{0:T(128)} %bitcast.refs_1_.refs_0_, bf16[32,5,80,256]{3,2,1,0:T(8,128)(2,1)} %all-gather.2.cloned.1.call-done.refs_2_, ...), custom_call_target="tpu_custom_call" | custom-call | flops 15000000512 | bytes 15000000 | tf_op jit(solution)/shard_map/project_scan/pallas_call | solution.py:348
  116.3 1.0 collective-permute-done.19
  117.4 1.0 collective-permute-start.22
  118.4 0.2 select_convert_fusion.2
  118.6 1.1 collective-permute-start.21
  119.7 4.6 %collective-permute-done.22 = bf16[64,1280]{1,0:T(8,128)(2,1)S(1)} collective-permute-done((bf16[64,1280]{1,0:T(8,128)(2,1)S(1)}, bf16[64,1280]{1,0:T(8,128)(2,1)S(1)}, u32[]{:S(2)}, u32[]{:S(2)}) %collective-permute-start.22) | collective-permute-done | bytes 163872 | tf_op jit(solution)/shard_map/ppermute | solution.py:400
  124.3 1.3 collective-permute-start.23
  125.6 1.3 collective-permute-start.24
  126.9 1.3 collective-permute-start.25
  128.3 1.8 %head_norm.3.refs_8_ = bf16[768,2560]{1,0:T(8,128)(2,1)} custom-call(s32[1]{0:T(128)} %bitcast.refs_1_.refs_0_, bf16[5,768,256]{2,1,0:T(8,128)(2,1)S(1)} %copy-done.1, bf16[768,128]{1,0:T(8,128)(2,1)S(1)} %get-tuple-element.91.refs_11_.refs_2_, bf16[10,768,256]{2,1,0:T(8,128)(2,1)S(1)} %copy-done, f32[1,2560]{1,0:T(1,128)S(1)} %broadcast_in_dim.65.refs_4_, ...), custom_call_target="tpu_custom_call" | custom-call | flops 800000000 | bytes 1966080 | tf_op jit(solution)/shard_map/head_norm/pallas_call | solution.py:382
  130.1 2.5 %head_norm.4.refs_8_ = bf16[768,2560]{1,0:T(8,128)(2,1)} custom-call(s32[1]{0:T(128)} %bitcast.refs_1_.refs_0_, bf16[5,768,256]{2,1,0:T(8,128)(2,1)S(1)} %copy-done.1, bf16[768,128]{1,0:T(8,128)(2,1)S(1)} %get-tuple-element.91.refs_11_.refs_2_, bf16[10,768,256]{2,1,0:T(8,128)(2,1)S(1)} %copy-done, ...), custom_call_target="tpu_custom_call", output_to_operand_aliasing={{}: (8, {})} | custom-call | flops 1200000000 | bytes 2949120 | tf_op jit(solution)/shard_map/head_norm/pallas_call | solution.py:382
  132.6 0.3 collective-permute-done.23
  132.9 6.8 %collective-permute-done.24 = bf16[64,1280]{1,0:T(8,128)(2,1)S(1)} collective-permute-done((bf16[64,1280]{1,0:T(8,128)(2,1)S(1)}, bf16[64,1280]{1,0:T(8,128)(2,1)S(1)}, u32[]{:S(2)}, u32[]{:S(2)}) %collective-permute-start.24) | collective-permute-done | bytes 163872 | tf_op jit(solution)/shard_map/ppermute | solution.py:400
  139.9 1.2 collective-permute-start.26
  141.0 4.2 %collective-permute-done.26.refs_7_ = bf16[64,1280]{1,0:T(8,128)(2,1)S(1)} collective-permute-done((bf16[64,1280]{1,0:T(8,128)(2,1)S(1)}, bf16[64,1280]{1,0:T(8,128)(2,1)S(1)}, u32[]{:S(2)}, u32[]{:S(2)}) %collective-permute-start.26) | collective-permute-done | bytes 163872 | tf_op jit(solution)/shard_map/ppermute | solution.py:400
  145.3 3.8 %head_norm.5 = bf16[768,2560]{1,0:T(8,128)(2,1)} custom-call(s32[1]{0:T(128)} %bitcast.refs_1_.refs_0_, bf16[5,768,256]{2,1,0:T(8,128)(2,1)S(1)} %get-tuple-element.94.refs_1_, bf16[768,128]{1,0:T(8,128)(2,1)S(1)} %get-tuple-element.91.refs_11_.refs_2_, bf16[10,768,256]{2,1,0:T(8,128)(2,1)S(1)} %copy-done, ...), custom_call_target="tpu_custom_call", output_to_operand_aliasing={{}: (8, {})} | custom-call | flops 2000000000 | bytes 4915200 | tf_op jit(solution)/shard_map/head_norm/pallas_call | solution.py:382
  (100 shorter events, 2.7 us)
Async XLA Ops:
  6.5 10.3 %copy-start.3 = (f32[1,40,768]{2,1,0:T(8,128)S(1)}, f32[1,40,768]{2,1,0:T(8,128)}, u32[]{:S(2)}) copy-start(f32[1,40,768]{2,1,0:T(8,128)} %param.13) | copy-start | bytes 368644
  6.5 10.5 %copy-start.11 = (f32[40]{0:T(128)S(1)}, f32[40]{0:T(128)}, u32[]{:S(2)}) copy-start(f32[40]{0:T(128)} %param.12) | copy-start | bytes 484
  6.5 11.2 %copy-start.7 = (f32[2816]{0:T(1024)S(1)}, f32[2816]{0:T(1024)}, u32[]{:S(2)}) copy-start(f32[2816]{0:T(1024)} %param.11) | copy-start | bytes 33796
  6.5 11.3 %copy-start.9 = (f32[40]{0:T(128)S(1)}, f32[40]{0:T(128)}, u32[]{:S(2)}) copy-start(f32[40]{0:T(128)} %param.14) | copy-start | bytes 484
  6.5 11.4 %copy-start.4 = (f32[4,2816]{1,0:T(4,128)S(1)}, f32[4,2816]{1,0:T(4,128)}, u32[]{:S(2)}) copy-start(f32[4,2816]{1,0:T(4,128)} %param.10) | copy-start | bytes 135172
  6.5 90.4 %all-gather.2.cloned.1.call-start = ((), (), s32[]{:S(2)}) async-start(), calls=%async_computation | async-start | bytes 6758400 | tf_op jit(solution)/shard_map/all_gather | solution.py:528
  8.5 13.0 %collective-permute-start = (bf16[1,6,80,256]{3,2,1,0:T(8,128)(2,1)S(1)}, bf16[1,6,80,256]{3,2,1,0:T(8,128)(2,1)S(1)}, u32[]{:S(2)}, u32[]{:S(2)}) collective-permute-start(bf16[1,6,80,256]{3,2,1,0:T(8,128)(2,1)S(1)} %slice.89), channel_id=1, source_target_pairs={{0,2},{1,3},{2,4},{3,5},{4,6},{5,7},{6,0},{7,1},{8,10},{9,11},{10,... | collective-permute-start | bytes 737288 | tf_op jit(solution)/shard_map/ppermute | solution.py:425
  8.5 13.0 %collective-permute-start.1 = (bf16[1,6,80,256]{3,2,1,0:T(8,128)(2,1)S(1)}, bf16[1,6,80,256]{3,2,1,0:T(8,128)(2,1)S(1)}, u32[]{:S(2)}, u32[]{:S(2)}) collective-permute-start(bf16[1,6,80,256]{3,2,1,0:T(8,128)(2,1)S(1)} %slice.89), channel_id=1, source_target_pairs={{0,6},{1,7},{2,0},{3,1},{4,2},{5,3},{6,4},{7,5},{8,14},{9,15},{10,... | collective-permute-start | bytes 737288 | tf_op jit(solution)/shard_map/ppermute | solution.py:425
  10.5 10.9 %collective-permute-start.2 = (bf16[1,6,80,256]{3,2,1,0:T(8,128)(2,1)S(1)}, bf16[1,6,80,256]{3,2,1,0:T(8,128)(2,1)S(1)}, u32[]{:S(2)}, u32[]{:S(2)}) collective-permute-start(bf16[1,6,80,256]{3,2,1,0:T(8,128)(2,1)S(1)} %slice.89), channel_id=1, source_target_pairs={{0,16},{1,17},{2,18},{3,19},{4,20},{5,21},{6,22},{7,23},{8,9},{9,8... | collective-permute-start | bytes 737288 | tf_op jit(solution)/shard_map/ppermute | solution.py:425
  12.0 9.5 %collective-permute-start.3 = (bf16[1,6,80,256]{3,2,1,0:T(8,128)(2,1)S(1)}, bf16[1,6,80,256]{3,2,1,0:T(8,128)(2,1)S(1)}, u32[]{:S(2)}, u32[]{:S(2)}) collective-permute-start(bf16[1,6,80,256]{3,2,1,0:T(8,128)(2,1)S(1)} %slice.89), channel_id=1, source_target_pairs={{0,1},{1,0},{2,3},{3,2},{4,5},{5,4},{6,7},{7,6},{8,24},{9,25},{10,... | collective-permute-start | bytes 737288 | tf_op jit(solution)/shard_map/ppermute | solution.py:425
  14.4 13.3 %collective-permute-start.8 = (bf16[16,2560]{1,0:T(8,128)(2,1)S(1)}, bf16[16,2560]{1,0:T(8,128)(2,1)S(1)}, u32[]{:S(2)}, u32[]{:S(2)}) collective-permute-start(bf16[16,2560]{1,0:T(8,128)(2,1)S(1)} %slice_bitcast_fusion), channel_id=1, source_target_pairs={{0,1},{1,2},{2,3},{3,4},{4,5},{5,6},{6,7},{8,9},{9,10},{10,11},{11... | collective-permute-start | bytes 245768 | tf_op jit(solution)/shard_map/ppermute | solution.py:491
  22.9 16.7 %collective-permute-start.5 = (bf16[2,6,80,256]{3,2,1,0:T(8,128)(2,1)S(1)}, bf16[2,6,80,256]{3,2,1,0:T(8,128)(2,1)S(1)}, u32[]{:S(2)}, u32[]{:S(2)}) collective-permute-start(bf16[2,6,80,256]{3,2,1,0:T(8,128)(2,1)S(1)} %get-tuple-element.127), channel_id=1, source_target_pairs={{0,16},{1,17},{2,18},{3,19},{4,20},{5,21},{6,22},{7,23},{8,9},{9,8... | collective-permute-start | bytes 1474568 | tf_op jit(solution)/shard_map/ppermute | solution.py:425
  24.4 15.2 %collective-permute-start.6 = (bf16[2,6,80,256]{3,2,1,0:T(8,128)(2,1)S(1)}, bf16[2,6,80,256]{3,2,1,0:T(8,128)(2,1)}, u32[]{:S(2)}, u32[]{:S(2)}) collective-permute-start(bf16[2,6,80,256]{3,2,1,0:T(8,128)(2,1)S(1)} %get-tuple-element.127), channel_id=1, source_target_pairs={{0,1},{1,0},{2,3},{3,2},{4,5},{5,4},{6,7},{7,6},{8,24},{9,25},{10,... | collective-permute-start | bytes 1474568 | tf_op jit(solution)/shard_map/ppermute | solution.py:425
  27.3 12.3 %collective-permute-start.4 = (bf16[1,6,80,256]{3,2,1,0:T(8,128)(2,1)S(1)}, bf16[1,6,80,256]{3,2,1,0:T(8,128)(2,1)S(1)}, u32[]{:S(2)}, u32[]{:S(2)}) collective-permute-start(bf16[1,6,80,256]{3,2,1,0:T(8,128)(2,1)S(1)} %slice.89), channel_id=1, source_target_pairs={{0,4},{1,5},{2,6},{3,7},{4,0},{5,1},{6,2},{7,3},{8,12},{9,13},{10,... | collective-permute-start | bytes 737288 | tf_op jit(solution)/shard_map/ppermute | solution.py:425
  27.3 12.3 %collective-permute-start.7 = (bf16[1,6,80,256]{3,2,1,0:T(8,128)(2,1)S(1)}, bf16[1,6,80,256]{3,2,1,0:T(8,128)(2,1)}, u32[]{:S(2)}, u32[]{:S(2)}) collective-permute-start(bf16[1,6,80,256]{3,2,1,0:T(8,128)(2,1)S(1)} %collective-permute-done.2), channel_id=1, source_target_pairs={{0,1},{1,0},{2,3},{3,2},{4,5},{5,4},{6,7},{7,6},{8,24},{9,25},{10,... | collective-permute-start | bytes 737288 | tf_op jit(solution)/shard_map/ppermute | solution.py:425
  39.7 17.7 %collective-permute-start.10 = (bf16[1,6,80,256]{3,2,1,0:T(8,128)(2,1)S(1)}, bf16[1,6,80,256]{3,2,1,0:T(8,128)(2,1)S(1)}, u32[]{:S(2)}, u32[]{:S(2)}) collective-permute-start(bf16[1,6,80,256]{3,2,1,0:T(8,128)(2,1)S(1)} %collective-permute-done.4), channel_id=1, source_target_pairs={{0,1},{1,0},{2,3},{3,2},{4,5},{5,4},{6,7},{7,6},{8,24},{9,25},{10,... | collective-permute-start | bytes 737288 | tf_op jit(solution)/shard_map/ppermute | solution.py:425
  40.9 16.5 %collective-permute-start.9 = (bf16[1,6,80,256]{3,2,1,0:T(8,128)(2,1)S(1)}, bf16[1,6,80,256]{3,2,1,0:T(8,128)(2,1)S(1)}, u32[]{:S(2)}, u32[]{:S(2)}) collective-permute-start(bf16[1,6,80,256]{3,2,1,0:T(8,128)(2,1)S(1)} %collective-permute-done.4), channel_id=1, source_target_pairs={{0,16},{1,17},{2,18},{3,19},{4,20},{5,21},{6,22},{7,23},{8,9},{9,8... | collective-permute-start | bytes 737288 | tf_op jit(solution)/shard_map/ppermute | solution.py:425
  42.9 14.4 %collective-permute-start.12 = (bf16[4,6,80,256]{3,2,1,0:T(8,128)(2,1)S(1)}, bf16[4,6,80,256]{3,2,1,0:T(8,128)(2,1)S(1)}, u32[]{:S(2)}, u32[]{:S(2)}) collective-permute-start(bf16[4,6,80,256]{3,2,1,0:T(8,128)(2,1)S(1)} %constant_dynamic-update-slice_fusion.2.refs_2_), channel_id=1, source_target_pairs={{0,8},{1,9},{2,10},{3,11},{4,12},{5,13},{6,14},{7,15},{8,0},{9,1},... | collective-permute-start | bytes 2949128 | tf_op jit(solution)/shard_map/ppermute | solution.py:425
  43.0 14.3 %collective-permute-start.11 = (bf16[2,6,80,256]{3,2,1,0:T(8,128)(2,1)S(1)}, bf16[2,6,80,256]{3,2,1,0:T(8,128)(2,1)S(1)}, u32[]{:S(2)}, u32[]{:S(2)}) collective-permute-start(bf16[2,6,80,256]{3,2,1,0:T(8,128)(2,1)S(1)} %collective-permute-done.5), channel_id=1, source_target_pairs={{0,1},{1,0},{2,3},{3,2},{4,5},{5,4},{6,7},{7,6},{8,24},{9,25},{10,... | collective-permute-start | bytes 1474568 | tf_op jit(solution)/shard_map/ppermute | solution.py:425
  44.2 11.6 %copy-start.5 = (bf16[8,6,80,256]{3,2,1,0:T(8,128)(2,1)S(1)}, bf16[8,6,80,256]{3,2,1,0:T(8,128)(2,1)}, u32[]{:S(2)}) copy-start(bf16[8,6,80,256]{3,2,1,0:T(8,128)(2,1)} %get-tuple-element.126) | copy-start | bytes 5898244
  55.9 3.0 %copy-start.2 = (bf16[10,768,256]{2,1,0:T(8,128)(2,1)}, bf16[10,768,256]{2,1,0:T(8,128)(2,1)S(1)}, u32[]{:S(2)}) copy-start(bf16[10,768,256]{2,1,0:T(8,128)(2,1)S(1)} %get-tuple-element.85.refs_14_.refs_7_) | copy-start | bytes 11796484
  57.4 9.5 %copy-start.6 = (bf16[8,6,80,256]{3,2,1,0:T(8,128)(2,1)}, bf16[8,6,80,256]{3,2,1,0:T(8,128)(2,1)S(1)}, u32[]{:S(2)}) copy-start(bf16[8,6,80,256]{3,2,1,0:T(8,128)(2,1)S(1)} %constant_dynamic-update-slice_fusion.6.refs_3_) | copy-start | bytes 5898244
  57.4 7.9 %collective-permute-start.14 = (bf16[8,6,80,256]{3,2,1,0:T(8,128)(2,1)S(1)}, bf16[8,6,80,256]{3,2,1,0:T(8,128)(2,1)S(1)}, u32[]{:S(2)}, u32[]{:S(2)}) collective-permute-start(bf16[8,6,80,256]{3,2,1,0:T(8,128)(2,1)S(1)} %constant_dynamic-update-slice_fusion.6.refs_3_), channel_id=1, source_target_pairs={{0,8},{1,9},{2,10},{3,11},{4,12},{5,13},{6,14},{7,15},{8,0},{9,1},... | collective-permute-start | bytes 5898248 | tf_op jit(solution)/shard_map/ppermute | solution.py:425
  58.9 6.3 %collective-permute-start.15 = (bf16[3,6,80,256]{3,2,1,0:T(8,128)(2,1)S(1)}, bf16[3,6,80,256]{3,2,1,0:T(8,128)(2,1)S(1)}, u32[]{:S(2)}, u32[]{:S(2)}) collective-permute-start(bf16[3,6,80,256]{3,2,1,0:T(8,128)(2,1)S(1)} %constant_dynamic-update-slice_fusion.11.refs_4_), channel_id=1, source_target_pairs={{0,8},{1,9},{2,10},{3,11},{4,12},{5,13},{6,14},{7,15},{8,0},{9,1},... | collective-permute-start | bytes 2211848 | tf_op jit(solution)/shard_map/ppermute | solution.py:425
  59.0 6.3 %collective-permute-start.13 = (bf16[1,6,80,256]{3,2,1,0:T(8,128)(2,1)S(1)}, bf16[1,6,80,256]{3,2,1,0:T(8,128)(2,1)S(1)}, u32[]{:S(2)}, u32[]{:S(2)}) collective-permute-start(bf16[1,6,80,256]{3,2,1,0:T(8,128)(2,1)S(1)} %collective-permute-done.9), channel_id=1, source_target_pairs={{0,1},{1,0},{2,3},{3,2},{4,5},{5,4},{6,7},{7,6},{8,24},{9,25},{10,... | collective-permute-start | bytes 737288 | tf_op jit(solution)/shard_map/ppermute | solution.py:425
  65.3 1.6 %copy-start.10 = (bf16[8,6,80,256]{3,2,1,0:T(8,128)(2,1)}, bf16[8,6,80,256]{3,2,1,0:T(8,128)(2,1)S(1)}, u32[]{:S(2)}) copy-start(bf16[8,6,80,256]{3,2,1,0:T(8,128)(2,1)S(1)} %collective-permute-done.14.refs_7_) | copy-start | bytes 5898244
  65.3 1.6 %collective-permute-start.16 = (bf16[1,6,80,256]{3,2,1,0:T(8,128)(2,1)S(1)}, bf16[1,6,80,256]{3,2,1,0:T(8,128)(2,1)S(1)}, u32[]{:S(2)}, u32[]{:S(2)}) collective-permute-start(bf16[1,6,80,256]{3,2,1,0:T(8,128)(2,1)S(1)} %collective-permute-done.13.refs_5_), channel_id=1, source_target_pairs={{0,8},{1,9},{2,10},{3,11},{4,12},{5,13},{6,14},{7,15},{8,0},{9,1},... | collective-permute-start | bytes 737288 | tf_op jit(solution)/shard_map/ppermute | solution.py:425
  66.9 23.9 %copy-start.8 = (f32[2560]{0:T(1024)S(1)}, f32[2560]{0:T(1024)}, u32[]{:S(2)}) copy-start(f32[2560]{0:T(1024)} %param.15) | copy-start | bytes 30724
  89.6 7.2 %collective-permute-start.17 = (bf16[80,1280]{1,0:T(8,128)(2,1)S(1)}, bf16[80,1280]{1,0:T(8,128)(2,1)S(1)}, u32[]{:S(2)}, u32[]{:S(2)}) collective-permute-start(bf16[80,1280]{1,0:T(8,128)(2,1)S(1)} %get-tuple-element.89), channel_id=1, source_target_pairs={{0,1},{1,0},{2,3},{3,2},{4,5},{5,4},{6,7},{7,6},{8,9},{9,8},{10,11... | collective-permute-start | bytes 614408 | tf_op jit(solution)/shard_map/ppermute | solution.py:400
  97.0 19.3 %collective-permute-start.18 = (bf16[80,1280]{1,0:T(8,128)(2,1)S(1)}, bf16[80,1280]{1,0:T(8,128)(2,1)S(1)}, u32[]{:S(2)}, u32[]{:S(2)}) collective-permute-start(bf16[80,1280]{1,0:T(8,128)(2,1)S(1)} %fusion.9), channel_id=1, source_target_pairs={{0,2},{1,3},{2,4},{3,5},{4,6},{5,7},{8,10},{9,11},{10,12},{11,13},... | collective-permute-start | bytes 614408 | tf_op jit(solution)/shard_map/ppermute | solution.py:400
  98.3 19.0 %collective-permute-start.19 = (bf16[80,1280]{1,0:T(8,128)(2,1)S(1)}, bf16[80,1280]{1,0:T(8,128)(2,1)S(1)}, u32[]{:S(2)}, u32[]{:S(2)}) collective-permute-start(bf16[80,1280]{1,0:T(8,128)(2,1)S(1)} %fusion.9), channel_id=1, source_target_pairs={{0,4},{1,5},{2,6},{3,7},{8,12},{9,13},{10,14},{11,15},{16,20},{17,... | collective-permute-start | bytes 614408 | tf_op jit(solution)/shard_map/ppermute | solution.py:400
  99.6 17.7 %collective-permute-start.20 = (bf16[80,1280]{1,0:T(8,128)(2,1)S(1)}, bf16[80,1280]{1,0:T(8,128)(2,1)S(1)}, u32[]{:S(2)}, u32[]{:S(2)}) collective-permute-start(bf16[80,1280]{1,0:T(8,128)(2,1)S(1)} %fusion.9), channel_id=1, source_target_pairs={{0,6},{1,7},{8,14},{9,15},{16,22},{17,23},{24,30},{25,31}} | collective-permute-start | bytes 614408 | tf_op jit(solution)/shard_map/ppermute | solution.py:400
  100.9 27.3 %copy-start = (bf16[10,768,256]{2,1,0:T(8,128)(2,1)S(1)}, bf16[10,768,256]{2,1,0:T(8,128)(2,1)}, u32[]{:S(2)}) copy-start(bf16[10,768,256]{2,1,0:T(8,128)(2,1)} %get-tuple-element.95.refs_3_) | copy-start | bytes 11796484
  116.3 11.9 %copy-start.1 = (bf16[5,768,256]{2,1,0:T(8,128)(2,1)S(1)}, bf16[5,768,256]{2,1,0:T(8,128)(2,1)}, u32[]{:S(2)}) copy-start(bf16[5,768,256]{2,1,0:T(8,128)(2,1)} %get-tuple-element.98.refs_1_) | copy-start | bytes 5898244
  117.4 6.9 %collective-permute-start.22 = (bf16[64,1280]{1,0:T(8,128)(2,1)S(1)}, bf16[64,1280]{1,0:T(8,128)(2,1)S(1)}, u32[]{:S(2)}, u32[]{:S(2)}) collective-permute-start(bf16[64,1280]{1,0:T(8,128)(2,1)S(1)} %get-tuple-element.106), channel_id=1, source_target_pairs={{0,1},{1,0},{2,3},{3,2},{4,5},{5,4},{6,7},{7,6},{8,9},{9,8},{10,11... | collective-permute-start | bytes 491528 | tf_op jit(solution)/shard_map/ppermute | solution.py:400
  118.6 9.6 %collective-permute-start.21 = (bf16[64,1280]{1,0:T(8,128)(2,1)S(1)}, bf16[64,1280]{1,0:T(8,128)(2,1)S(1)}, u32[]{:S(2)}, u32[]{:S(2)}) collective-permute-start(bf16[64,1280]{1,0:T(8,128)(2,1)S(1)} %get-tuple-element.122), channel_id=1, source_target_pairs={{0,1},{1,0},{2,3},{3,2},{4,5},{5,4},{6,7},{7,6},{8,9},{9,8},{10,11... | collective-permute-start | bytes 491528 | tf_op jit(solution)/shard_map/ppermute | solution.py:400
  124.3 8.6 %collective-permute-start.23 = (bf16[64,1280]{1,0:T(8,128)(2,1)S(1)}, bf16[64,1280]{1,0:T(8,128)(2,1)S(1)}, u32[]{:S(2)}, u32[]{:S(2)}) collective-permute-start(bf16[64,1280]{1,0:T(8,128)(2,1)S(1)} %fusion.7), channel_id=1, source_target_pairs={{0,2},{1,3},{2,4},{3,5},{4,6},{5,7},{8,10},{9,11},{10,12},{11,13},... | collective-permute-start | bytes 491528 | tf_op jit(solution)/shard_map/ppermute | solution.py:400
  125.6 14.1 %collective-permute-start.24 = (bf16[64,1280]{1,0:T(8,128)(2,1)S(1)}, bf16[64,1280]{1,0:T(8,128)(2,1)S(1)}, u32[]{:S(2)}, u32[]{:S(2)}) collective-permute-start(bf16[64,1280]{1,0:T(8,128)(2,1)S(1)} %fusion.7), channel_id=1, source_target_pairs={{0,4},{1,5},{2,6},{3,7},{8,12},{9,13},{10,14},{11,15},{16,20},{17,... | collective-permute-start | bytes 491528 | tf_op jit(solution)/shard_map/ppermute | solution.py:400
  126.9 12.8 %collective-permute-start.25 = (bf16[64,1280]{1,0:T(8,128)(2,1)S(1)}, bf16[64,1280]{1,0:T(8,128)(2,1)S(1)}, u32[]{:S(2)}, u32[]{:S(2)}) collective-permute-start(bf16[64,1280]{1,0:T(8,128)(2,1)S(1)} %fusion.7), channel_id=1, source_target_pairs={{0,6},{1,7},{8,14},{9,15},{16,22},{17,23},{24,30},{25,31}} | collective-permute-start | bytes 491528 | tf_op jit(solution)/shard_map/ppermute | solution.py:400
  139.9 5.4 %collective-permute-start.26 = (bf16[64,1280]{1,0:T(8,128)(2,1)S(1)}, bf16[64,1280]{1,0:T(8,128)(2,1)S(1)}, u32[]{:S(2)}, u32[]{:S(2)}) collective-permute-start(bf16[64,1280]{1,0:T(8,128)(2,1)S(1)} %get-tuple-element.124), channel_id=1, source_target_pairs={{0,1},{1,0},{2,3},{3,2},{4,5},{5,4},{6,7},{7,6},{8,9},{9,8},{10,11... | collective-permute-start | bytes 491528 | tf_op jit(solution)/shard_map/ppermute | solution.py:400
Sparse Core Ops, SparseCore 0:
  10.3 80.0 all-gather.1
